TPU v7x, 512 devices: a whole 4x8x8 slice. The times are simulated.
512 devices in a mesh: grp: 16 (over y, core), row: 32 (over x, z).
Axes of the slice: x: 4, y: 8, z: 8, core: 2. Of those that a mesh axis runs over, the one named last changes fastest.
Arguments:
- amplitudes: float32 [8192, 4096], P('grp', 'row'), may hold values from -6 to 6
- dressing: float32 [4096, 4096], P(None, 'row'), may hold values from -0.09375 to 0.09375
- pair_factor: float32 [128, 512, 64], P('grp'), may hold values from -0.25 to 0.25
- blocks: float32 [32, 512, 4096], P('grp', None, 'row'), may hold values from -6 to 6
- pair_block: int32 [128], replicated, may hold values from 0 to 31, as said below
- block_home: int32 [32], replicated, may hold values from 0 to 31, as said below
- tile_mask: int32 [128, 64], P('grp', 'row'), may hold values 0 or 1
- row_energy: float32 [8192], P('grp'), may hold values from 0.5 to 2
- column_energy: float32 [4096], P('row'), may hold values from 0.5 to 2
Outputs:
- residual: float32 [8192, 4096], P('grp', 'row')
- new_amplitudes: float32 [8192, 4096], P('grp', 'row')
Inputs may be any that keep to these rules, and one draw needn't show every extreme that they name: Block b is stored at position block_home[b] of blocks; block_home is a permutation, and the owner of block b is block_home[b] // 2. Pair domain p uses block pair_block[p]; the 8 pair domains g * 8 to g * 8 + 7 use blocks of 8 different owners, and pair domains of one group whose blocks have the same owner use the same block.
All inputs are finite; a program needn't handle non-finite values. No bound on the sum of `tile_mask` on one device may be relied on, other than what follows from the above.
Results may differ from a plain program's by a relative error of at most 0.000057.
Values sent between devices are 32-bit elements; how exact they have to be, the bound alone decides.
No kernel may reach another device: no remote copies, remote signals or barrier semaphores. Data moves between devices by JAX's collectives and lax.ppermute only.
A program may use at most 64 MiB of HBM per device.

v0:
```python
import jax
import jax.numpy as jnp
from jax import lax
from jax.sharding import PartitionSpec as P


def shards(
    amplitudes,
    dressing,
    pair_factor,
    blocks,
    pair_block,
    block_home,
    tile_mask,
    row_energy,
    column_energy,
):
    highest = lax.Precision.HIGHEST
    pair_count = pair_factor.shape[0]
    tile_width = pair_factor.shape[2]
    local_columns = amplitudes.shape[1]
    dressed = jnp.dot(
        lax.all_gather(amplitudes, "row", axis=1, tiled=True),
        dressing,
        precision=highest,
        preferred_element_type=jnp.float32,
    )
    group_index = lax.axis_index("grp")
    my_blocks = lax.dynamic_slice_in_dim(pair_block, group_index * pair_count, pair_count)
    pair_homes = jnp.take(block_home, my_blocks)
    portion = lax.all_gather(blocks, "grp", axis=0, tiled=True)
    length = portion.shape[0]
    picked = (pair_homes[:, None] == jnp.arange(length, dtype=jnp.int32)[None, :]).astype(
        jnp.float32
    )
    chosen = jnp.einsum("ki,iqc->kqc", picked, portion, precision=highest)
    integral = jnp.einsum("kqa,kqc->kac", pair_factor, chosen, precision=highest)
    column_mask = jnp.repeat(tile_mask.astype(jnp.float32), tile_width, axis=1)
    integral = integral * column_mask[:, None, :]
    residual = integral.reshape(pair_count * tile_width, local_columns) + dressed
    denominator = row_energy[:, None] + column_energy[None, :]
    return (residual, amplitudes - residual / denominator)


def solution(mesh):
    placed = (
        P("grp", "row"),
        P(None, "row"),
        P("grp", None, None),
        P("grp", None, "row"),
        P(),
        P(),
        P("grp", "row"),
        P("grp"),
        P("row"),
    )
    return jax.shard_map(
        shards,
        mesh=mesh,
        in_specs=placed,
        out_specs=(P("grp", "row"), P("grp", "row")),
        check_vma=False,
    )
```

profile of v0, /device:TPU:1, one launch (start us, length us, event | category | flops | bytes accessed | tf_op | source)
XLA Modules:
  0.0 200.1 jit_solution(2864042528258960556)
XLA Ops:
  7.2 0.0 copy-start
  7.2 0.0 all-gather.3.cloned.1.call-start
  7.2 0.7 all-gather.3.cloned.1.call-update
  7.9 0.0 all-gather.5.cloned.1.call-start
  8.0 0.7 all-gather.5.cloned.1.call-update
  8.7 0.7 convert_element_type.4
  9.4 0.1 copy.15
  9.4 0.1 broadcast_in_dim.12
  9.5 0.1 mul.17
  9.6 0.7 compare_select_fusion
  10.3 1.3 gather_fusion
  11.6 0.7 and_select_fusion
  12.4 0.0 copy-start.2
  12.4 61.9 %all-gather.3.cloned.1.call-done = f32[32,512,128]{2,1,0:T(8,128)} async-done(((f32[2,512,128]{2,1,0:T(8,128)}), f32[32,512,128]{2,1,0:T(8,128)}) %all-gather.3.cloned.1.call-update) | async-done | bytes 8388624 | tf_op jit(solution)/shard_map/all_gather | solution.py:31
  74.3 10.6 %fusion = f32[8,512,128]{2,0,1:T(8,128)S(1)} fusion(f32[32,512,128]{2,1,0:T(8,128)} %all-gather.3.cloned.1.call-done, s32[8]{0:T(128)S(1)} %and_select_fusion), kind=kOutput, calls=%fused_computation.1 | convolution fusion | flops 201326848 | bytes 10485792 | tf_op jit(solution)/shard_map/ki,iqc->kqc/dot_general | solution.py:36
  84.9 0.0 copy-done.2
  84.9 0.0 copy-start.1
  84.9 0.0 copy-start.3
  84.9 0.0 copy-start.4
  84.9 2.4 %fusion.4 = f32[8,128,64]{1,2,0:T(8,128)} fusion(f32[8,512,64]{1,2,0:T(8,128)S(1)} %copy-done.2, f32[8,512,128]{2,0,1:T(8,128)S(1)} %fusion, f32[8,128]{1,0:T(8,128)S(1)} %mul.17), kind=kOutput, calls=%fused_computation.6 | convolution fusion | flops 402718720 | bytes 3411968 | tf_op jit(solution)/shard_map/kqa,kqc->kac/dot_general | solution.py:37
  87.3 96.0 %all-gather.5.cloned.1.call-done = f32[512,4096]{1,0:T(8,128)} async-done(((f32[512,128]{1,0:T(8,128)}), f32[512,4096]{1,0:T(8,128)}) %all-gather.5.cloned.1.call-update) | async-done | bytes 8388624 | tf_op jit(solution)/shard_map/all_gather | solution.py:23
  183.2 0.0 copy-done
  183.2 0.0 copy-done.1
  183.3 0.0 copy-done.3
  183.3 0.0 copy-done.4
  183.3 10.0 %divide_subtract_fusion = (f32[512,128]{1,0:T(8,128)}, f32[512,128]{1,0:T(8,128)}) fusion(f32[512,128]{1,0:T(8,128)S(1)} %copy-done.1, f32[128]{0:T(128)S(1)} %copy-done.4, f32[512]{0:T(512)S(1)} %copy-done.3, f32[512,128]{1,0:T(8,128)} %bitcast.9, f32[512,4096]{1,0:T(8,128)} %all-gather.5.cloned.1.call-done, f32[4096,128]{1,0:T(8,128)S(1)} %copy-done), kind=kOutput, calls=%fused_computation.7 | convolution fusion | flops 3221487616 | bytes 11536896 | tf_op jit(solution)/shard_map/dot_general | solution.py:22
  (1 shorter events, 0.0 us)
Async XLA Ops:
  7.2 176.1 %copy-start = (f32[4096,128]{1,0:T(8,128)S(1)}, f32[4096,128]{1,0:T(8,128)}, u32[]{:S(2)}) copy-start(f32[4096,128]{1,0:T(8,128)} %param.10) | copy-start | bytes 6291460
  7.2 67.1 %all-gather.3.cloned.1.call-start = ((), (), s32[]{:S(2)}) async-start(), calls=%async_computation | async-start | bytes 8912896 | tf_op jit(solution)/shard_map/all_gather | solution.py:31
  7.9 175.3 %all-gather.5.cloned.1.call-start = ((), (), s32[]{:S(2)}) async-start(), calls=%async_computation.1 | async-start | bytes 8650752 | tf_op jit(solution)/shard_map/all_gather | solution.py:23
  12.4 72.5 %copy-start.2 = (f32[8,512,64]{1,2,0:T(8,128)S(1)}, f32[8,512,64]{1,2,0:T(8,128)}, u32[]{:S(2)}) copy-start(f32[8,512,64]{1,2,0:T(8,128)} %param.11) | copy-start | bytes 3145732
  84.9 98.4 %copy-start.1 = (f32[512,128]{1,0:T(8,128)S(1)}, f32[512,128]{1,0:T(8,128)}, u32[]{:S(2)}) copy-start(f32[512,128]{1,0:T(8,128)} %param.9) | copy-start | bytes 786436
  84.9 98.4 %copy-start.3 = (f32[512]{0:T(512)S(1)}, f32[512]{0:T(512)}, u32[]{:S(2)}) copy-start(f32[512]{0:T(512)} %param.16) | copy-start | bytes 6148
  84.9 98.4 %copy-start.4 = (f32[128]{0:T(128)S(1)}, f32[128]{0:T(128)}, u32[]{:S(2)}) copy-start(f32[128]{0:T(128)} %param.17) | copy-start | bytes 1540
Sparse Core Ops, SparseCore 0:
  10.1 64.1 all-gather.2
  77.3 105.8 all-gather.4
where the time goes:
time: 202 us; the launch traced here: 200 us
  waiting for transfers between devices  159 us (79%)
  matrix products  22.9 us (11%)
  between operations  14.1 us (7%)
  other arithmetic  2.16 us (1%)
    all_gather x1, waiting for transfers between devices, shards(): lax.all_gather(amplitudes, 'row', axis=1, tiled=True)  96 us
    all_gather x1, waiting for transfers between devices, shards(): portion = lax.all_gather(blocks, 'grp', axis=0, tiled=True)  61.9 us
    dot_general x1, matrix products, shards(): chosen = jnp.einsum('ki,iqc->kqc', picked, portion, precision=highest)  10.6 us
    dot_general x1, matrix products, shards(): jnp.dot(lax.all_gather(amplitudes, 'row', axis=1, tiled=True), dressing,...  9.96 us
  transfers between devices with their start and end apart: 2, of which 2 were waited for; matrix products, arithmetic and copies ran while one was open for 8% of the time, Pallas kernels for 0%

commit v1 on v0

v1 whole, which is shorter than its diff:
```python
import jax
import jax.numpy as jnp
from jax import lax
from jax.experimental import pallas as pl
from jax.experimental.pallas import tpu as pltpu
from jax.sharding import Mesh
from jax.sharding import PartitionSpec as P

MIB = 1024 * 1024


def split(value):
    high = value.astype(jnp.bfloat16)
    low = (value - high.astype(jnp.float32)).astype(jnp.bfloat16)
    return high, low


def dot3(left, right):
    one = lambda a, b: jnp.dot(a, b, preferred_element_type=jnp.float32)
    return one(left[0], right[0]) + (one(left[0], right[1]) + one(left[1], right[0]))


def partial_kernel(pieces, z_ref, *refs):
    amps = refs[:pieces]
    panels = refs[pieces : pieces + 4]
    outs = refs[pieces + 4 : pieces + 8]
    high, low = refs[pieces + 8 :]
    z = z_ref[0]
    depth = amps[0].shape[1]
    for k in range(pieces):
        shift = -k if k <= pieces // 2 else k - pieces // 2
        at = lax.rem(z + shift + pieces, pieces) * depth
        at = pl.multiple_of(at, depth)
        h, l = split(amps[k][...])
        high[:, pl.ds(at, depth)] = h
        low[:, pl.ds(at, depth)] = l
    left = (high[...], low[...])
    for k in range(0, 4, 2):
        right = split(jnp.concatenate([panels[k][...], panels[k + 1][...]], axis=1))
        both = dot3(left, right)
        width = both.shape[1] // 2
        outs[k][...] = both[:, :width]
        outs[k + 1][...] = both[:, width:]


def final_kernel(
    home_ref, mask_ref, factor_ref, block_ref, amp_ref, p0, p1, p2, p3, row_ref, col_ref, res_ref, new_ref
):
    k = pl.program_id(0)
    integral = dot3(split(factor_ref[0]), split(block_ref[0]))
    tile = integral.shape[0]
    lane = lax.broadcasted_iota(jnp.int32, integral.shape, 1)
    first = mask_ref[2 * k].astype(jnp.float32)
    second = mask_ref[2 * k + 1].astype(jnp.float32)
    integral = integral * jnp.where(lane < tile, first, second)
    residual = integral + ((p0[...] + p1[...]) + (p2[...] + p3[...]))
    res_ref[...] = residual
    new_ref[...] = amp_ref[...] - residual / (row_ref[...] + col_ref[...])


def shards(
    amplitudes,
    dressing,
    pair_factor,
    blocks,
    pair_block,
    block_home,
    tile_mask,
    row_energy,
    column_energy,
):
    f32 = jnp.float32
    ny, nc = lax.axis_size("y"), lax.axis_size("core")
    nx, nz = lax.axis_size("x"), lax.axis_size("z")
    x, z = lax.axis_index("x"), lax.axis_index("z")
    pair_count, naux, tile = pair_factor.shape
    rows, width = amplitudes.shape

    def shift(value, axis, step):
        n = lax.axis_size(axis)
        return lax.ppermute(value, axis, [(i, (i + step) % n) for i in range(n)])

    portion = lax.all_gather(blocks, ("y", "core"), axis=0, tiled=True)

    depth = nz * width
    panels = []
    for s in range(nx):
        part = lax.dynamic_slice_in_dim(dressing, lax.rem(x + s, nx) * depth, depth)
        panels.append(part if s == 0 else shift(part, "x", s))

    back, ahead = [amplitudes], [amplitudes]
    for s in range(nz // 2):
        back.append(shift(back[-1], "z", 1))
        if s < nz - 1 - nz // 2:
            ahead.append(shift(ahead[-1], "z", -1))
    pieces = back + ahead[1:]

    vmem = pl.BlockSpec(memory_space=pltpu.VMEM)
    smem = pl.BlockSpec(memory_space=pltpu.SMEM)
    partials = pl.pallas_call(
        lambda *refs: partial_kernel(nz, *refs),
        out_shape=[jax.ShapeDtypeStruct((rows, width), f32)] * nx,
        in_specs=[smem] + [vmem] * (nz + nx),
        out_specs=[vmem] * nx,
        scratch_shapes=[pltpu.VMEM((rows, depth), jnp.bfloat16)] * 2,
        compiler_params=pltpu.CompilerParams(vmem_limit_bytes=40 * MIB),
        cost_estimate=pl.CostEstimate(
            flops=6 * rows * depth * width * nx,
            bytes_accessed=4 * (rows * depth + depth * width * nx + rows * width * nx),
            transcendentals=0,
        ),
        name="dressed_partials",
    )(z[None], *pieces, *panels)
    sums = [partials[0]] + [shift(partials[s], "x", -s) for s in range(1, nx)]

    group = lax.axis_index("y") * nc + lax.axis_index("core")
    mine = lax.dynamic_slice_in_dim(pair_block, group * pair_count, pair_count)
    homes = jnp.sum(
        jnp.where(mine[:, None] == jnp.arange(block_home.shape[0])[None, :], block_home[None, :], 0), axis=1
    )
    part = pl.BlockSpec((tile, width), lambda k, home, mask: (k, 0))
    residual, new = pl.pallas_call(
        final_kernel,
        out_shape=[jax.ShapeDtypeStruct((rows, width), f32)] * 2,
        grid_spec=pltpu.PrefetchScalarGridSpec(
            num_scalar_prefetch=2,
            grid=(pair_count,),
            in_specs=[
                pl.BlockSpec((1, tile, naux), lambda k, home, mask: (k, 0, 0)),
                pl.BlockSpec((1, naux, width), lambda k, home, mask: (home[k], 0, 0)),
                part,
                part,
                part,
                part,
                part,
                pl.BlockSpec((tile, 1), lambda k, home, mask: (k, 0)),
                pl.BlockSpec((1, width), lambda k, home, mask: (0, 0)),
            ],
            out_specs=[part, part],
        ),
        compiler_params=pltpu.CompilerParams(vmem_limit_bytes=40 * MIB),
        cost_estimate=pl.CostEstimate(
            flops=6 * rows * naux * width,
            bytes_accessed=4 * (rows * naux + pair_count * naux * width + 7 * rows * width),
            transcendentals=0,
        ),
        name="integral_update",
    )(
        homes,
        tile_mask.reshape(-1),
        jnp.swapaxes(pair_factor, 1, 2),
        portion,
        amplitudes,
        *sums,
        row_energy[:, None],
        column_energy[None, :],
    )
    return residual, new


def solution(mesh):
    sizes = dict(zip(("y", "core", "x", "z"), (8, 2, 4, 8)))
    fine = Mesh(mesh.devices.reshape(tuple(sizes.values())), tuple(sizes))
    grp, row = ("y", "core"), ("x", "z")
    placed = (
        P(grp, row),
        P(None, row),
        P(grp, None, None),
        P(grp, None, row),
        P(),
        P(),
        P(grp, row),
        P(grp),
        P(row),
    )
    return jax.shard_map(
        shards,
        mesh=fine,
        in_specs=placed,
        out_specs=(P(grp, row), P(grp, row)),
        check_vma=False,
    )
```

time: 202 us -> 110 us (0.54)
  waiting for transfers between devices: 159 us -> 20 us
  starting transfers between devices: 0.08 us -> 48.4 us
  matrix products: 22.9 us -> 0 us
  local copies, waits for them, and re-layouts: 1.57 us -> 16.7 us
  Pallas kernels: 0 us -> 8.81 us
    all_gather x2 -> x1, waiting for transfers between devices: 158 us -> 0.01 us  [shards(): portion = lax.all_gather(blocks, ('y', 'core'), axis=0, tiled=True)]
    ppermute x0 -> x13, starting transfers between devices: none -> 48.3 us  [shift(): return lax.ppermute(value, axis, [(i, (i + step) % n) for i in range(n)])]
    dot_general x3 -> x0, matrix products: 22.9 us -> none  [the longest x1 10.6 us: shards(): chosen = jnp.einsum('ki,iqc->kqc', picked, portion, precision=highest)]
    ppermute x0 -> x13, waiting for transfers between devices: none -> 19.3 us  [shift(): return lax.ppermute(value, axis, [(i, (i + step) % n) for i in range(n)])]
    unnamed x10 -> x41, local copies, waits for them, and re-layouts: 0.03 us -> 13.7 us
    pallas_call x0 -> x2, Pallas kernels: none -> 8.81 us  [the longest x1 4.64 us: shards(): pl.pallas_call(lambda *refs: partial_kernel(nz, *refs), out_shape=[jax.Sh...]
    dynamic_slice x0 -> x2, local copies, waits for them, and re-layouts: none -> 2.84 us  [the longest x1 2.76 us: shards(): part = lax.dynamic_slice_in_dim(dressing, lax.rem(x + s, nx) * depth, depth)]
  transfers between devices with their start and end apart: 2 -> 14, of which waited for: 2 -> 6; matrix products, arithmetic and copies ran while one was open for 8% -> 3% of each run, Pallas kernels for 0% -> 4%
where the time goes in v1:
time: 110 us; the launch traced here: 108 us
  starting transfers between devices  48.4 us (44%)
  waiting for transfers between devices  20 us (18%)
  local copies, waits for them, and re-layouts  16.7 us (15%)
  between operations  14.3 us (13%)
  Pallas kernels  8.81 us (8%)
    ppermute x13, starting transfers between devices, shift(): return lax.ppermute(value, axis, [(i, (i + step) % n) for i in range(n)])  48.3 us
    ppermute x13, waiting for transfers between devices, shift(): return lax.ppermute(value, axis, [(i, (i + step) % n) for i in range(n)])  19.3 us
    unnamed x41, local copies, waits for them, and re-layouts  13.7 us
    pallas_call x1, Pallas kernels, shards(): pl.pallas_call(lambda *refs: partial_kernel(nz, *refs), out_shape=[jax.Sh...  4.64 us
    pallas_call x1, Pallas kernels, shards(): pl.pallas_call(final_kernel, out_shape=[jax.ShapeDtypeStruct((rows, width...  4.18 us
    dynamic_slice x1, local copies, waits for them, and re-layouts, shards(): part = lax.dynamic_slice_in_dim(dressing, lax.rem(x + s, nx) * depth, depth)  2.76 us
  transfers between devices with their start and end apart: 14, of which 6 were waited for; matrix products, arithmetic and copies ran while one was open for 3% of the time, Pallas kernels for 4%

profile of v1, /device:TPU:1, one launch (start us, length us, event | category | flops | bytes accessed | tf_op | source)
XLA Modules:
  0.0 108.3 jit_solution(17975540964156172833)
XLA Ops:
  7.2 0.0 all-gather.2.cloned.1.call-start
  7.2 0.7 all-gather.2.cloned.1.call-update
  7.9 4.8 %collective-permute-start = (f32[512,128]{1,0:T(8,128)}, f32[512,128]{1,0:T(8,128)S(1)}, u32[]{:S(2)}, u32[]{:S(2)}) collective-permute-start(f32[512,128]{1,0:T(8,128)} %amp_ref.1), channel_id=1, source_target_pairs={{0,1},{1,2},{2,3},{3,4},{4,5},{5,6},{6,7},{7,0},{8,9},{9,10},{10,1... | collective-permute-start | bytes 786440 | tf_op jit(solution)/shard_map/ppermute | solution.py:81
  12.7 8.6 %collective-permute-start.4 = (f32[512,128]{1,0:T(8,128)}, f32[512,128]{1,0:T(8,128)S(1)}, u32[]{:S(2)}, u32[]{:S(2)}) collective-permute-start(f32[512,128]{1,0:T(8,128)} %amp_ref.1), channel_id=1, source_target_pairs={{0,7},{1,0},{2,1},{3,2},{4,3},{5,4},{6,5},{7,6},{8,15},{9,8},{10,9... | collective-permute-start | bytes 786440 | tf_op jit(solution)/shard_map/ppermute | solution.py:81
  21.3 4.3 %collective-permute-done.refs_2_ = f32[512,128]{1,0:T(8,128)S(1)} collective-permute-done((f32[512,128]{1,0:T(8,128)}, f32[512,128]{1,0:T(8,128)S(1)}, u32[]{:S(2)}, u32[]{:S(2)}) %collective-permute-start) | collective-permute-done | bytes 262176 | tf_op jit(solution)/shard_map/ppermute | solution.py:81
  25.6 1.9 %collective-permute-start.1 = (f32[512,128]{1,0:T(8,128)S(1)}, f32[512,128]{1,0:T(8,128)S(1)}, u32[]{:S(2)}, u32[]{:S(2)}) collective-permute-start(f32[512,128]{1,0:T(8,128)S(1)} %collective-permute-done.refs_2_), channel_id=1, source_target_pairs={{0,1},{1,2},{2,3},{3,4},{4,5},{5,6},{6,7},{7,0},{8,9},{9,10},{10,1... | collective-permute-start | bytes 786440 | tf_op jit(solution)/shard_map/ppermute | solution.py:81
  27.6 0.0 copy-start.2
  27.6 2.8 %constant_dynamic-slice_fusion.3 = (f32[1024,128]{1,0:T(8,128)}, f32[1024,128]{1,0:T(8,128)}, f32[1024,128]{1,0:T(8,128)S(1)}, f32[1024,128]{1,0:T(8,128)}) fusion(f32[4096,128]{1,0:T(8,128)} %param.10, s32[]{:T(128)S(6)} %select_n.24, s32[]{:T(128)S(6)} %select_n.22, s32[]{:T(128)S(6)} %select_n.21, s32[]{:T(128)S(6)} %select_n.23), kind=kLoop, calls=%fused_computation.5 | loop fusion | bytes 4194320 | tf_op jit(solution)/shard_map/dynamic_slice | solution.py:88
  30.3 3.1 %collective-permute-start.7 = (f32[1024,128]{1,0:T(8,128)}, f32[1024,128]{1,0:T(8,128)S(1)}, u32[]{:S(2)}, u32[]{:S(2)}) collective-permute-start(f32[1024,128]{1,0:T(8,128)} %get-tuple-element.11), channel_id=1, source_target_pairs={{0,8},{8,16},{16,24},{24,0},{1,9},{9,17},{17,25},{25,1},{2,10},{10... | collective-permute-start | bytes 1572872 | tf_op jit(solution)/shard_map/ppermute | solution.py:81
  33.5 4.4 %collective-permute-start.8 = (f32[1024,128]{1,0:T(8,128)}, f32[1024,128]{1,0:T(8,128)S(1)}, u32[]{:S(2)}, u32[]{:S(2)}) collective-permute-start(f32[1024,128]{1,0:T(8,128)} %get-tuple-element.13), channel_id=1, source_target_pairs={{0,16},{8,24},{16,0},{24,8},{1,17},{9,25},{17,1},{25,9},{2,18},{10... | collective-permute-start | bytes 1572872 | tf_op jit(solution)/shard_map/ppermute | solution.py:81
  37.8 3.1 %collective-permute-start.9 = (f32[1024,128]{1,0:T(8,128)}, f32[1024,128]{1,0:T(8,128)S(1)}, u32[]{:S(2)}, u32[]{:S(2)}) collective-permute-start(f32[1024,128]{1,0:T(8,128)} %get-tuple-element.10), channel_id=1, source_target_pairs={{0,24},{8,0},{16,8},{24,16},{1,25},{9,1},{17,9},{25,17},{2,26},{10... | collective-permute-start | bytes 1572872 | tf_op jit(solution)/shard_map/ppermute | solution.py:81
  40.9 0.0 collective-permute-done.4.refs_6_
  40.9 4.6 %collective-permute-start.5 = (f32[512,128]{1,0:T(8,128)S(1)}, f32[512,128]{1,0:T(8,128)S(1)}, u32[]{:S(2)}, u32[]{:S(2)}) collective-permute-start(f32[512,128]{1,0:T(8,128)S(1)} %collective-permute-done.4.refs_6_), channel_id=1, source_target_pairs={{0,7},{1,0},{2,1},{3,2},{4,3},{5,4},{6,5},{7,6},{8,15},{9,8},{10,9... | collective-permute-start | bytes 786440 | tf_op jit(solution)/shard_map/ppermute | solution.py:81
  45.5 0.0 copy-start.6
  45.5 0.7 copy-done.6
  46.2 0.0 collective-permute-done.1.refs_3_
  46.2 1.9 %collective-permute-start.2 = (f32[512,128]{1,0:T(8,128)S(1)}, f32[512,128]{1,0:T(8,128)}, u32[]{:S(2)}, u32[]{:S(2)}) collective-permute-start(f32[512,128]{1,0:T(8,128)S(1)} %collective-permute-done.1.refs_3_), channel_id=1, source_target_pairs={{0,1},{1,2},{2,3},{3,4},{4,5},{5,6},{6,7},{7,0},{8,9},{9,10},{10,1... | collective-permute-start | bytes 786440 | tf_op jit(solution)/shard_map/ppermute | solution.py:81
  48.1 0.0 copy-start.8
  48.1 0.7 copy-done.8
  48.8 0.0 collective-permute-done.5.refs_7_
  48.8 5.4 %collective-permute-start.6 = (f32[512,128]{1,0:T(8,128)S(1)}, f32[512,128]{1,0:T(8,128)S(1)}, u32[]{:S(2)}, u32[]{:S(2)}) collective-permute-start(f32[512,128]{1,0:T(8,128)S(1)} %collective-permute-done.5.refs_7_), channel_id=1, source_target_pairs={{0,7},{1,0},{2,1},{3,2},{4,3},{5,4},{6,5},{7,6},{8,15},{9,8},{10,9... | collective-permute-start | bytes 786440 | tf_op jit(solution)/shard_map/ppermute | solution.py:81
  54.2 0.0 copy-start.10
  54.2 0.7 copy-done.10
  54.9 0.0 collective-permute-done.2.refs_4_
  54.9 1.9 %collective-permute-start.3 = (f32[512,128]{1,0:T(8,128)}, f32[512,128]{1,0:T(8,128)S(1)}, u32[]{:S(2)}, u32[]{:S(2)}) collective-permute-start(f32[512,128]{1,0:T(8,128)} %collective-permute-done.2.refs_4_), channel_id=1, source_target_pairs={{0,1},{1,2},{2,3},{3,4},{4,5},{5,6},{6,7},{7,0},{8,9},{9,10},{10,1... | collective-permute-start | bytes 786440 | tf_op jit(solution)/shard_map/ppermute | solution.py:81
  56.8 0.0 collective-permute-done.7.refs_10_
  56.8 1.2 %collective-permute-done.8.refs_11_ = f32[1024,128]{1,0:T(8,128)S(1)} collective-permute-done((f32[1024,128]{1,0:T(8,128)}, f32[1024,128]{1,0:T(8,128)S(1)}, u32[]{:S(2)}, u32[]{:S(2)}) %collective-permute-start.8) | collective-permute-done | bytes 524320 | tf_op jit(solution)/shard_map/ppermute | solution.py:81
  58.1 2.3 %collective-permute-done.9.refs_12_ = f32[1024,128]{1,0:T(8,128)S(1)} collective-permute-done((f32[1024,128]{1,0:T(8,128)}, f32[1024,128]{1,0:T(8,128)S(1)}, u32[]{:S(2)}, u32[]{:S(2)}) %collective-permute-start.9) | collective-permute-done | bytes 524320 | tf_op jit(solution)/shard_map/ppermute | solution.py:81
  60.3 0.0 copy-start.4
  60.3 0.8 copy-done.4
  61.2 0.0 collective-permute-done.6.refs_8_
  61.2 0.0 copy-start.12
  61.2 0.7 copy-done.12
  61.9 2.0 %collective-permute-done.3.refs_5_ = f32[512,128]{1,0:T(8,128)S(1)} collective-permute-done((f32[512,128]{1,0:T(8,128)}, f32[512,128]{1,0:T(8,128)S(1)}, u32[]{:S(2)}, u32[]{:S(2)}) %collective-permute-start.3) | collective-permute-done | bytes 262176 | tf_op jit(solution)/shard_map/ppermute | solution.py:81
  63.8 0.7 copy-done.14
  64.5 0.0 copy-done.2
  64.5 1.1 copy-done.5
  65.6 1.0 copy-done.7
  66.6 0.9 copy-done.9
  67.5 1.0 copy-done.11
  68.5 0.9 copy-done.13
  69.5 0.9 copy-done.15
  70.4 0.0 copy-start.1
  70.4 0.0 copy-start.3
  70.4 4.6 %dressed_partials.1 = (f32[512,128]{1,0:T(8,128)S(1)}, f32[512,128]{1,0:T(8,128)}, f32[512,128]{1,0:T(8,128)}, f32[512,128]{1,0:T(8,128)}) custom-call(s32[1]{0:T(128)} %bitcast.1.refs_0_, f32[512,128]{1,0:T(8,128)S(1)} %copy-done.2, f32[512,128]{1,0:T(8,128)S(1)} %collective-permute-done.refs_2_, f32[512,128]{1,0:T(8,128)S(1)} %copy-done.9, ...), custom_call_target="tpu_custom_call" | custom-call | flops 1610612736 | bytes 5242880 | tf_op jit(solution)/shard_map/dressed_partials/pallas_call | solution.py:100
  75.1 3.3 %collective-permute-start.10 = (f32[512,128]{1,0:T(8,128)}, f32[512,128]{1,0:T(8,128)S(1)}, u32[]{:S(2)}, u32[]{:S(2)}) collective-permute-start(f32[512,128]{1,0:T(8,128)} %get-tuple-element.7), channel_id=1, source_target_pairs={{0,24},{8,0},{16,8},{24,16},{1,25},{9,1},{17,9},{25,17},{2,26},{10... | collective-permute-start | bytes 786440 | tf_op jit(solution)/shard_map/ppermute | solution.py:81
  78.4 3.5 %collective-permute-start.11 = (f32[512,128]{1,0:T(8,128)}, f32[512,128]{1,0:T(8,128)S(1)}, u32[]{:S(2)}, u32[]{:S(2)}) collective-permute-start(f32[512,128]{1,0:T(8,128)} %get-tuple-element.8), channel_id=1, source_target_pairs={{0,16},{8,24},{16,0},{24,8},{1,17},{9,25},{17,1},{25,9},{2,18},{10... | collective-permute-start | bytes 786440 | tf_op jit(solution)/shard_map/ppermute | solution.py:81
  81.9 1.9 %collective-permute-start.12 = (f32[512,128]{1,0:T(8,128)}, f32[512,128]{1,0:T(8,128)S(1)}, u32[]{:S(2)}, u32[]{:S(2)}) collective-permute-start(f32[512,128]{1,0:T(8,128)} %get-tuple-element.9), channel_id=1, source_target_pairs={{0,8},{8,16},{16,24},{24,0},{1,9},{9,17},{17,25},{25,1},{2,10},{10... | collective-permute-start | bytes 786440 | tf_op jit(solution)/shard_map/ppermute | solution.py:81
  83.8 0.0 copy-done.16
  83.8 0.1 copy.17.row_ref
  84.0 0.0 copy-done.17
  84.0 0.1 copy.16
  84.1 0.1 reshape.9.mask_ref
  84.1 0.0 copy-done.18
  84.2 0.1 dynamic_slice.15
  84.2 0.0 copy-done.19
  84.2 0.2 select_reduce_fusion.home_ref
  84.4 0.0 collective-permute-done.10.p1
  84.4 2.8 %collective-permute-done.11.p2 = f32[512,128]{1,0:T(8,128)S(1)} collective-permute-done((f32[512,128]{1,0:T(8,128)}, f32[512,128]{1,0:T(8,128)S(1)}, u32[]{:S(2)}, u32[]{:S(2)}) %collective-permute-start.11) | collective-permute-done | bytes 262176 | tf_op jit(solution)/shard_map/ppermute | solution.py:81
  87.2 6.7 %collective-permute-done.12.p3 = f32[512,128]{1,0:T(8,128)S(1)} collective-permute-done((f32[512,128]{1,0:T(8,128)}, f32[512,128]{1,0:T(8,128)S(1)}, u32[]{:S(2)}, u32[]{:S(2)}) %collective-permute-start.12) | collective-permute-done | bytes 262176 | tf_op jit(solution)/shard_map/ppermute | solution.py:81
  93.9 0.0 copy-done.1
  93.9 0.0 copy-done.3
  93.9 3.4 %copy-done = f32[32,512,128]{2,1,0:T(8,128)S(1)} copy-done((f32[32,512,128]{2,1,0:T(8,128)S(1)}, f32[32,512,128]{2,1,0:T(8,128)}, u32[]{:S(2)}) %copy-start) | copy-done | bytes 8388632
  97.3 4.2 %integral_update.1 = (f32[512,128]{1,0:T(8,128)}, f32[512,128]{1,0:T(8,128)}) custom-call(s32[8]{0:T(128)S(1)} %select_reduce_fusion.home_ref, s32[16]{0:T(128)S(1)} %reshape.9.mask_ref, f32[8,64,512]{2,1,0:T(8,128)S(1)} %bitcast.4, f32[32,512,128]{2,1,0:T(8,128)S(1)} %copy-done, f32[512,128]{1,0:T(8,128)S(1)} %copy-done.2, ...), custom_call_target="tpu_custom_call" | custom-call | flops 201326592 | bytes 4980736 | tf_op jit(solution)/shard_map/integral_update/pallas_call | solution.py:122
  (13 shorter events, 0.0 us)
Async XLA Ops:
  7.2 86.8 %all-gather.2.cloned.1.call-start = ((), (), s32[]{:S(2)}) async-start(), calls=%async_computation | async-start | bytes 8912896 | tf_op jit(solution)/shard_map/all_gather | solution.py:83
  7.9 17.7 %collective-permute-start = (f32[512,128]{1,0:T(8,128)}, f32[512,128]{1,0:T(8,128)S(1)}, u32[]{:S(2)}, u32[]{:S(2)}) collective-permute-start(f32[512,128]{1,0:T(8,128)} %amp_ref.1), channel_id=1, source_target_pairs={{0,1},{1,2},{2,3},{3,4},{4,5},{5,6},{6,7},{7,0},{8,9},{9,10},{10,1... | collective-permute-start | bytes 786440 | tf_op jit(solution)/shard_map/ppermute | solution.py:81
  12.7 28.2 %collective-permute-start.4 = (f32[512,128]{1,0:T(8,128)}, f32[512,128]{1,0:T(8,128)S(1)}, u32[]{:S(2)}, u32[]{:S(2)}) collective-permute-start(f32[512,128]{1,0:T(8,128)} %amp_ref.1), channel_id=1, source_target_pairs={{0,7},{1,0},{2,1},{3,2},{4,3},{5,4},{6,5},{7,6},{8,15},{9,8},{10,9... | collective-permute-start | bytes 786440 | tf_op jit(solution)/shard_map/ppermute | solution.py:81
  25.6 20.6 %collective-permute-start.1 = (f32[512,128]{1,0:T(8,128)S(1)}, f32[512,128]{1,0:T(8,128)S(1)}, u32[]{:S(2)}, u32[]{:S(2)}) collective-permute-start(f32[512,128]{1,0:T(8,128)S(1)} %collective-permute-done.refs_2_), channel_id=1, source_target_pairs={{0,1},{1,2},{2,3},{3,4},{4,5},{5,6},{6,7},{7,0},{8,9},{9,10},{10,1... | collective-permute-start | bytes 786440 | tf_op jit(solution)/shard_map/ppermute | solution.py:81
  27.6 37.0 %copy-start.2 = (f32[512,128]{1,0:T(8,128)S(1)}, f32[512,128]{1,0:T(8,128)}, u32[]{:S(2)}) copy-start(f32[512,128]{1,0:T(8,128)} %amp_ref.1) | copy-start | bytes 786436
  30.3 26.5 %collective-permute-start.7 = (f32[1024,128]{1,0:T(8,128)}, f32[1024,128]{1,0:T(8,128)S(1)}, u32[]{:S(2)}, u32[]{:S(2)}) collective-permute-start(f32[1024,128]{1,0:T(8,128)} %get-tuple-element.11), channel_id=1, source_target_pairs={{0,8},{8,16},{16,24},{24,0},{1,9},{9,17},{17,25},{25,1},{2,10},{10... | collective-permute-start | bytes 1572872 | tf_op jit(solution)/shard_map/ppermute | solution.py:81
  33.5 24.6 %collective-permute-start.8 = (f32[1024,128]{1,0:T(8,128)}, f32[1024,128]{1,0:T(8,128)S(1)}, u32[]{:S(2)}, u32[]{:S(2)}) collective-permute-start(f32[1024,128]{1,0:T(8,128)} %get-tuple-element.13), channel_id=1, source_target_pairs={{0,16},{8,24},{16,0},{24,8},{1,17},{9,25},{17,1},{25,9},{2,18},{10... | collective-permute-start | bytes 1572872 | tf_op jit(solution)/shard_map/ppermute | solution.py:81
  37.8 22.5 %collective-permute-start.9 = (f32[1024,128]{1,0:T(8,128)}, f32[1024,128]{1,0:T(8,128)S(1)}, u32[]{:S(2)}, u32[]{:S(2)}) collective-permute-start(f32[1024,128]{1,0:T(8,128)} %get-tuple-element.10), channel_id=1, source_target_pairs={{0,24},{8,0},{16,8},{24,16},{1,25},{9,1},{17,9},{25,17},{2,26},{10... | collective-permute-start | bytes 1572872 | tf_op jit(solution)/shard_map/ppermute | solution.py:81
  40.9 7.9 %collective-permute-start.5 = (f32[512,128]{1,0:T(8,128)S(1)}, f32[512,128]{1,0:T(8,128)S(1)}, u32[]{:S(2)}, u32[]{:S(2)}) collective-permute-start(f32[512,128]{1,0:T(8,128)S(1)} %collective-permute-done.4.refs_6_), channel_id=1, source_target_pairs={{0,7},{1,0},{2,1},{3,2},{4,3},{5,4},{6,5},{7,6},{8,15},{9,8},{10,9... | collective-permute-start | bytes 786440 | tf_op jit(solution)/shard_map/ppermute | solution.py:81
  45.5 0.7 copy-start.6
  46.2 8.7 %collective-permute-start.2 = (f32[512,128]{1,0:T(8,128)S(1)}, f32[512,128]{1,0:T(8,128)}, u32[]{:S(2)}, u32[]{:S(2)}) collective-permute-start(f32[512,128]{1,0:T(8,128)S(1)} %collective-permute-done.1.refs_3_), channel_id=1, source_target_pairs={{0,1},{1,2},{2,3},{3,4},{4,5},{5,6},{6,7},{7,0},{8,9},{9,10},{10,1... | collective-permute-start | bytes 786440 | tf_op jit(solution)/shard_map/ppermute | solution.py:81
  48.1 0.7 copy-start.8
  48.8 12.3 %collective-permute-start.6 = (f32[512,128]{1,0:T(8,128)S(1)}, f32[512,128]{1,0:T(8,128)S(1)}, u32[]{:S(2)}, u32[]{:S(2)}) collective-permute-start(f32[512,128]{1,0:T(8,128)S(1)} %collective-permute-done.5.refs_7_), channel_id=1, source_target_pairs={{0,7},{1,0},{2,1},{3,2},{4,3},{5,4},{6,5},{7,6},{8,15},{9,8},{10,9... | collective-permute-start | bytes 786440 | tf_op jit(solution)/shard_map/ppermute | solution.py:81
  54.2 0.7 copy-start.10
  54.9 8.9 %collective-permute-start.3 = (f32[512,128]{1,0:T(8,128)}, f32[512,128]{1,0:T(8,128)S(1)}, u32[]{:S(2)}, u32[]{:S(2)}) collective-permute-start(f32[512,128]{1,0:T(8,128)} %collective-permute-done.2.refs_4_), channel_id=1, source_target_pairs={{0,1},{1,2},{2,3},{3,4},{4,5},{5,6},{6,7},{7,0},{8,9},{9,10},{10,1... | collective-permute-start | bytes 786440 | tf_op jit(solution)/shard_map/ppermute | solution.py:81
  60.3 0.8 copy-start.4
  61.2 0.7 copy-start.12
  63.8 0.7 copy-start.14
  64.5 1.1 copy-start.5
  65.6 1.0 copy-start.7
  66.6 0.9 copy-start.9
  67.5 1.0 copy-start.11
  68.5 0.9 copy-start.13
  69.4 0.9 copy-start.15
  70.4 13.4 %copy-start.16 = (f32[512]{0:T(512)S(1)}, f32[512]{0:T(512)}, u32[]{:S(2)}) copy-start(f32[512]{0:T(512)} %param.16) | copy-start | bytes 6148
  70.4 13.6 %copy-start.17 = (s32[8,2]{0,1:T(2,128)S(1)}, s32[8,2]{0,1:T(2,128)}, u32[]{:S(2)}) copy-start(s32[8,2]{0,1:T(2,128)} %param.15) | copy-start | bytes 196
  70.4 13.7 %copy-start.18 = (s32[128]{0:T(128)S(1)}, s32[128]{0:T(128)}, u32[]{:S(2)}) copy-start(s32[128]{0:T(128)} %param.13) | copy-start | bytes 1540
  70.4 13.8 %copy-start.19 = (s32[32]{0:T(128)S(1)}, s32[32]{0:T(128)}, u32[]{:S(2)}) copy-start(s32[32]{0:T(128)} %param.14) | copy-start | bytes 388
  70.4 23.5 %copy-start.1 = (f32[8,512,64]{1,2,0:T(8,128)S(1)}, f32[8,512,64]{1,2,0:T(8,128)}, u32[]{:S(2)}) copy-start(f32[8,512,64]{1,2,0:T(8,128)} %param.11) | copy-start | bytes 3145732
  70.4 23.5 %copy-start.3 = (f32[128]{0:T(128)S(1)}, f32[128]{0:T(128)}, u32[]{:S(2)}) copy-start(f32[128]{0:T(128)} %param.17) | copy-start | bytes 1540
  75.1 9.3 %collective-permute-start.10 = (f32[512,128]{1,0:T(8,128)}, f32[512,128]{1,0:T(8,128)S(1)}, u32[]{:S(2)}, u32[]{:S(2)}) collective-permute-start(f32[512,128]{1,0:T(8,128)} %get-tuple-element.7), channel_id=1, source_target_pairs={{0,24},{8,0},{16,8},{24,16},{1,25},{9,1},{17,9},{25,17},{2,26},{10... | collective-permute-start | bytes 786440 | tf_op jit(solution)/shard_map/ppermute | solution.py:81
  78.4 8.8 %collective-permute-start.11 = (f32[512,128]{1,0:T(8,128)}, f32[512,128]{1,0:T(8,128)S(1)}, u32[]{:S(2)}, u32[]{:S(2)}) collective-permute-start(f32[512,128]{1,0:T(8,128)} %get-tuple-element.8), channel_id=1, source_target_pairs={{0,16},{8,24},{16,0},{24,8},{1,17},{9,25},{17,1},{25,9},{2,18},{10... | collective-permute-start | bytes 786440 | tf_op jit(solution)/shard_map/ppermute | solution.py:81
  81.9 12.0 %collective-permute-start.12 = (f32[512,128]{1,0:T(8,128)}, f32[512,128]{1,0:T(8,128)S(1)}, u32[]{:S(2)}, u32[]{:S(2)}) collective-permute-start(f32[512,128]{1,0:T(8,128)} %get-tuple-element.9), channel_id=1, source_target_pairs={{0,8},{8,16},{16,24},{24,0},{1,9},{9,17},{17,25},{25,1},{2,10},{10... | collective-permute-start | bytes 786440 | tf_op jit(solution)/shard_map/ppermute | solution.py:81
  93.9 3.4 %copy-start = (f32[32,512,128]{2,1,0:T(8,128)S(1)}, f32[32,512,128]{2,1,0:T(8,128)}, u32[]{:S(2)}) copy-start(f32[32,512,128]{2,1,0:T(8,128)} %all-gather.2.cloned.1.call-done.block_ref) | copy-start | bytes 25165828
Sparse Core Ops, SparseCore 0:
  10.1 64.1 all-gather.1

commit v2 on v0

v2 whole, which is shorter than its diff:
```python
import jax
import jax.numpy as jnp
from jax import lax
from jax.experimental import pallas as pl
from jax.experimental.pallas import tpu as pltpu
from jax.sharding import Mesh
from jax.sharding import PartitionSpec as P

F32 = jnp.float32
PARAMS = pltpu.CompilerParams(vmem_limit_bytes=48 * 1024 * 1024)
ANY = pl.BlockSpec(memory_space=pl.ANY)
VMEM = pl.BlockSpec(memory_space=pltpu.VMEM)
SMEM = pl.BlockSpec(memory_space=pltpu.SMEM)
FAR = 4


def split(value):
    high = value.astype(jnp.bfloat16)
    low = (value - high.astype(F32)).astype(jnp.bfloat16)
    return high, low


def dot3(left, right):
    one = lambda a, b: jnp.dot(a, b, preferred_element_type=F32)
    return one(left[0], right[0]) + (one(left[0], right[1]) + one(left[1], right[0]))


def start_all(copies, sems):
    made = [pltpu.make_async_copy(src, dst, sems.at[i]) for i, (src, dst) in enumerate(copies)]
    for copy in made:
        copy.start()
    return made


def behind(index, size, core, step):
    return lax.rem(index + jnp.where(core == 0, size - step, step), size)


def cut_kernel(nx, nz, width, dressing, *refs):
    outs, sems = refs[: nx - 1], refs[nx - 1]
    core, x, z = lax.axis_index("core"), lax.axis_index("x"), lax.axis_index("z")
    copies = []
    for s in range(1, nx):
        to = lax.rem(x + s, nx)
        for t in range(FAR + 1):
            row = pl.multiple_of((to * nz + behind(z, nz, core, t)) * width, width)
            copies.append((dressing.at[pl.ds(row, width)], outs[s - 1].at[pl.ds(t * width, width)]))
    for copy in start_all(copies, sems):
        copy.wait()


def partial_kernel(nx, nz, steps, added, *refs):
    count = len(steps)
    pieces, refs = refs[:count], refs[count:]
    dressing, panels, refs = refs[0], refs[1:nx], refs[nx:]
    plus, refs = (refs[0], refs[1:]) if added else (None, refs)
    outs, refs = (refs[:nx], refs[nx:]) if added else (refs[:1], refs[1:])
    amps, dress, sems = refs[:3]
    core, x, z = lax.axis_index("core"), lax.axis_index("x"), lax.axis_index("z")
    width = pieces[0].shape[1]
    first = steps[0] * width
    copies = []
    for s in range(1, nx):
        src = panels[s - 1].at[pl.ds(first, count * width)]
        copies.append((src, dress.at[:, pl.ds(s * width, width)]))
    for k, t in enumerate(steps):
        row = pl.multiple_of((x * nz + behind(z, nz, core, t)) * width, width)
        copies.append((dressing.at[pl.ds(row, width)], dress.at[pl.ds(k * width, width), pl.ds(0, width)]))
    for k in range(count):
        copies.append((pieces[k], amps.at[:, pl.ds(k * width, width)]))
    if added:
        copies.append((plus, refs[3]))
    made = start_all(copies, sems)
    for copy in made[: len(made) - (1 if added else 0)]:
        copy.wait()
    left = split(amps[...])
    for s in range(0, nx, 2):
        both = dot3(left, split(dress[:, s * width : (s + 2) * width]))
        if added and s == 0:
            made[-1].wait()
        for k in range(2):
            value = both[:, k * width : (k + 1) * width]
            if added:
                value = value + refs[3][s + k]
                outs[s + k][...] = value
            else:
                outs[0][s + k] = value


def home_of(pair, pair_block, block_home):
    home = block_home[pair_block[pair]]
    return lax.div(home, 4), lax.rem(lax.div(home, 2), 2), lax.rem(home, 2)


def pick_kernel(ny, pairs, pair_block, block_home, same, cross, out, sems):
    y, core = lax.axis_index("y"), lax.axis_index("core")
    to = behind(y, ny, 1 - core, 1)
    source = behind(to, ny, core, FAR)
    group = to * 2 + core

    def look(i, found):
        at_y, at_core, which = home_of(group * pairs + i, pair_block, block_home)
        hit = at_y == source
        return (
            jnp.where(jnp.logical_and(hit, at_core == core), which, found[0]),
            jnp.where(jnp.logical_and(hit, at_core != core), which, found[1]),
        )

    a, b = lax.fori_loop(0, pairs, look, (jnp.int32(0), jnp.int32(0)))
    for copy in start_all([(same.at[a], out.at[0]), (cross.at[b], out.at[1])], sems):
        copy.wait()


def factor_dot(factor, block):
    high, low = split(factor)
    block_high, block_low = split(block)
    rows = factor.shape[0]
    both = jnp.dot(jnp.concatenate([high, low], axis=0), block_high, preferred_element_type=F32)
    return both[:rows] + (both[rows:] + jnp.dot(high, block_low, preferred_element_type=F32))


def near_kernel(ny, pairs, pair_block, block_home, mine, theirs, *refs):
    sources, refs = refs[: 2 * FAR - 1], refs[2 * FAR - 1 :]
    out_mine, out_theirs, factors, held, factor_sems, sems = refs
    y, core = lax.axis_index("y"), lax.axis_index("core")
    loads = start_all([(mine, factors.at[0]), (theirs, factors.at[1])], factor_sems)

    def source_of(n):
        whose, i = lax.div(n, pairs), lax.rem(n, pairs)
        group = y * 2 + jnp.where(whose == 0, core, 1 - core)
        at_y, at_core, which = home_of(group * pairs + i, pair_block, block_home)
        step = lax.rem(jnp.where(core == 0, y - at_y, at_y - y) + ny, ny)
        same = at_core == core
        far = jnp.where(step < FAR, jnp.where(same, step, step + FAR - 1), -1)
        return jnp.where(step == 0, jnp.where(same, 0, -1), far), which

    def fetch(n, carry):
        source, which = source_of(n)
        for k, ref in enumerate(sources):

            @pl.when(source == k)
            def _():
                pltpu.make_async_copy(ref.at[which], held.at[n], sems.at[n]).start()

        return carry

    lax.fori_loop(0, 2 * pairs, fetch, 0)
    for load in loads:
        load.wait()
    tile = factors.shape[2]
    for whose, out in enumerate((out_mine, out_theirs)):

        def work(i, carry):
            n = whose * pairs + i
            source, which = source_of(n)
            rows = pl.ds(pl.multiple_of(i * tile, tile), tile)

            @pl.when(source >= 0)
            def _():
                pltpu.make_async_copy(sources[0].at[0], held.at[n], sems.at[n]).wait()
                out[rows] = factor_dot(factors[whose, i], held[n])

            @pl.when(source < 0)
            def _():
                out[rows] = jnp.zeros((tile, out.shape[1]), F32)

            return carry

        lax.fori_loop(0, pairs, work, 0)


def last_kernel(
    ny, pairs, pair_block, block_home, mask, factor, far, mine, theirs, s0, s1, s2, s3, amps, row, col, *refs
):
    residual, new, factors, blocks, parts, sems = refs
    y, core = lax.axis_index("y"), lax.axis_index("core")
    copies = [(far, blocks), (factor, factors)]
    copies += [(ref, parts.at[k]) for k, ref in enumerate((mine, theirs, s0, s1, s2, s3, amps))]
    made = start_all(copies, sems)
    for copy in made:
        copy.wait()
    tile = factors.shape[1]
    width = new.shape[1]
    lane = lax.broadcasted_iota(jnp.int32, (tile, width), 1)

    def work(i, carry):
        at_y, at_core, which = home_of((y * 2 + core) * pairs + i, pair_block, block_home)
        rows = pl.ds(pl.multiple_of(i * tile, tile), tile)

        @pl.when(at_y == lax.rem(y + FAR, ny))
        def _():
            entry = jnp.where(at_core == core, 0, 1)
            parts[0, rows] = factor_dot(factors[i], blocks[entry])

        integral = parts[0, rows] + parts[1, rows]
        on = jnp.where(lane < tile, mask[2 * i], mask[2 * i + 1]).astype(F32)
        total = integral * on + ((parts[2, rows] + parts[3, rows]) + (parts[4, rows] + parts[5, rows]))
        residual[rows] = total
        new[rows] = parts[6, rows] - total / (row[rows] + col[...])
        return carry

    lax.fori_loop(0, pairs, work, 0)


def shards(
    amplitudes,
    dressing,
    pair_factor,
    blocks,
    pair_block,
    block_home,
    tile_mask,
    row_energy,
    column_energy,
):
    ny, nx, nz = lax.axis_size("y"), lax.axis_size("x"), lax.axis_size("z")
    pairs, naux, tile = pair_factor.shape
    rows, width = amplitudes.shape
    sem = pltpu.SemaphoreType.DMA

    def ring(value, axis, cross=False):
        n = lax.axis_size(axis)
        names, at = (("y", "core"), lambda c, i: i * 2 + c) if axis == "y" else (("core", axis), lambda c, i: c * n + i)
        pairs_of = []
        for to in range(2):
            for i in range(n):
                pairs_of.append((at(1 - to if cross else to, i), at(to, (i + (1, -1)[to]) % n)))
        return lax.ppermute(value, names, pairs_of)

    def swap(value):
        return lax.ppermute(value, "core", [(0, 1), (1, 0)])

    def shift(value, step):
        return lax.ppermute(value, "x", [(i, (i + step) % nx) for i in range(nx)])

    def chain(value, axis):
        same, cross = [ring(value, axis)], [ring(value, axis, cross=True)]
        for _ in range(FAR - 2):
            same.append(ring(same[-1], axis))
            cross.append(ring(cross[-1], axis))
        return same, cross

    amp_same, amp_cross = chain(amplitudes, "z")
    amp_far = ring(amp_same[-1], "z")
    blk_same, blk_cross = chain(blocks, "y")

    cuts = pl.pallas_call(
        lambda *refs: cut_kernel(nx, nz, width, *refs),
        out_shape=[jax.ShapeDtypeStruct(((FAR + 1) * width, width), F32)] * (nx - 1),
        in_specs=[ANY],
        out_specs=[ANY] * (nx - 1),
        scratch_shapes=[sem(((nx - 1) * (FAR + 1),))],
        compiler_params=PARAMS,
        name="cut",
    )(dressing)
    panels = [shift(cuts[s - 1], s) for s in range(1, nx)]
    factor = jnp.swapaxes(pair_factor, 1, 2)
    factor_other = swap(factor)

    def partial(pieces, steps, plus):
        count = len(steps)
        shape = jax.ShapeDtypeStruct((rows, width), F32)
        scratch = [
            pltpu.VMEM((rows, count * width), F32),
            pltpu.VMEM((count * width, nx * width), F32),
            sem((2 * count + nx,)),
        ]
        if plus is None:
            shape = [jax.ShapeDtypeStruct((nx, rows, width), F32)]
        else:
            shape = [shape] * nx
            scratch.append(pltpu.VMEM((nx, rows, width), F32))
        return pl.pallas_call(
            lambda *refs: partial_kernel(nx, nz, steps, plus is not None, *refs),
            out_shape=shape,
            in_specs=[ANY] * (count + nx + (plus is not None)),
            out_specs=[VMEM] * len(shape),
            scratch_shapes=scratch,
            compiler_params=PARAMS,
            cost_estimate=pl.CostEstimate(
                flops=6 * rows * count * width * nx * width, bytes_accessed=4 * 2 * rows * nx * width, transcendentals=0
            ),
            name="partial_own" if plus is not None else "partial_other",
        )(*pieces, dressing, *panels, *([] if plus is None else [plus]))

    (other,) = partial(amp_cross, tuple(range(1, FAR)), None)
    sums = partial([amplitudes, *amp_same, amp_far], tuple(range(FAR + 1)), swap(other))
    sums = [sums[0]] + [shift(sums[s], -s) for s in range(1, nx)]

    picked = pl.pallas_call(
        lambda *refs: pick_kernel(ny, pairs, *refs),
        out_shape=jax.ShapeDtypeStruct((2, naux, width), F32),
        in_specs=[SMEM, SMEM, ANY, ANY],
        out_specs=ANY,
        scratch_shapes=[sem((2,))],
        compiler_params=PARAMS,
        name="pick",
    )(pair_block, block_home, blk_same[-1], blk_cross[-1])
    blk_far = ring(picked, "y")

    mine, theirs = pl.pallas_call(
        lambda *refs: near_kernel(ny, pairs, *refs),
        out_shape=[jax.ShapeDtypeStruct((rows, width), F32)] * 2,
        in_specs=[SMEM, SMEM] + [ANY] * (2 + 2 * FAR - 1),
        out_specs=[VMEM] * 2,
        scratch_shapes=[
            pltpu.VMEM((2, pairs, tile, naux), F32),
            pltpu.VMEM((2 * pairs, naux, width), F32),
            sem((2,)),
            sem((2 * pairs,)),
        ],
        compiler_params=PARAMS,
        cost_estimate=pl.CostEstimate(
            flops=6 * rows * naux * width, bytes_accessed=4 * 2 * rows * naux * 2, transcendentals=0
        ),
        name="integral_near",
    )(pair_block, block_home, factor, factor_other, blocks, *blk_same, *blk_cross)
    theirs = swap(theirs)

    residual, new = pl.pallas_call(
        lambda *refs: last_kernel(ny, pairs, *refs),
        out_shape=[jax.ShapeDtypeStruct((rows, width), F32)] * 2,
        in_specs=[SMEM] * 3 + [ANY] * 9 + [VMEM] * 2,
        out_specs=[VMEM] * 2,
        scratch_shapes=[
            pltpu.VMEM((pairs, tile, naux), F32),
            pltpu.VMEM((2, naux, width), F32),
            pltpu.VMEM((7, rows, width), F32),
            sem((9,)),
        ],
        compiler_params=PARAMS,
        name="integral_far_update",
    )(
        pair_block,
        block_home,
        tile_mask.reshape(-1),
        factor,
        blk_far,
        mine,
        theirs,
        *sums,
        amplitudes,
        row_energy[:, None],
        column_energy[None, :],
    )
    return residual, new


def solution(mesh):
    sizes = {"y": 8, "core": 2, "x": 4, "z": 8}
    fine = Mesh(mesh.devices.reshape(tuple(sizes.values())), tuple(sizes))
    grp, row = ("y", "core"), ("x", "z")
    placed = (
        P(grp, row),
        P(None, row),
        P(grp, None, None),
        P(grp, None, row),
        P(),
        P(),
        P(grp, row),
        P(grp),
        P(row),
    )
    return jax.shard_map(
        shards,
        mesh=fine,
        in_specs=placed,
        out_specs=(P(grp, row), P(grp, row)),
        check_vma=False,
    )
```

time: 202 us -> 118 us (0.58)
  waiting for transfers between devices: 159 us -> 17.2 us
  starting transfers between devices: 0.08 us -> 79.4 us
  matrix products: 22.9 us -> 0 us
  Pallas kernels: 0 us -> 16.2 us
  between operations: 14.1 us -> 1.12 us
  other arithmetic: 2.16 us -> 0 us
    all_gather x2 -> x0, waiting for transfers between devices: 158 us -> none  [the longest x1 96 us: shards(): lax.all_gather(amplitudes, 'row', axis=1, tiled=True)]
    ppermute x0 -> x23, starting transfers between devices: none -> 79.4 us  [the longest x14 50.9 us: ring(): return lax.ppermute(value, names, pairs_of)]
    dot_general x3 -> x0, matrix products: 22.9 us -> none  [the longest x1 10.6 us: shards(): chosen = jnp.einsum('ki,iqc->kqc', picked, portion, precision=highest)]
    ppermute x0 -> x23, waiting for transfers between devices: none -> 17.2 us  [the longest x6 11.8 us: shift(): return lax.ppermute(value, 'x', [(i, (i + step) % nx) for i in range(nx)])]
    pallas_call x0 -> x6, Pallas kernels: none -> 16.2 us  [the longest x2 6.1 us: partial(): pl.pallas_call(lambda *refs: partial_kernel(nx, nz, steps, plus is not No...]
    unnamed x10 -> x21, local copies, waits for them, and re-layouts: 0.03 us -> 2.68 us
  transfers between devices with their start and end apart: 2 -> 23, of which waited for: 2 -> 4; matrix products, arithmetic and copies ran while one was open for 8% -> 0% of each run, Pallas kernels for 0% -> 11%
where the time goes in v2:
time: 118 us; the launch traced here: 117 us
  starting transfers between devices  79.4 us (67%)
  waiting for transfers between devices  17.2 us (15%)
  Pallas kernels  16.2 us (14%)
  local copies, waits for them, and re-layouts  2.91 us (2%)
    ppermute x14, starting transfers between devices, ring(): return lax.ppermute(value, names, pairs_of)  50.9 us
    ppermute x6, starting transfers between devices, shift(): return lax.ppermute(value, 'x', [(i, (i + step) % nx) for i in range(nx)])  19.1 us
    ppermute x6, waiting for transfers between devices, shift(): return lax.ppermute(value, 'x', [(i, (i + step) % nx) for i in range(nx)])  11.8 us
    ppermute x3, starting transfers between devices, swap(): return lax.ppermute(value, 'core', [(0, 1), (1, 0)])  9.42 us
    pallas_call x2, Pallas kernels, partial(): pl.pallas_call(lambda *refs: partial_kernel(nx, nz, steps, plus is not No...  6.1 us
    ppermute x14, waiting for transfers between devices, ring(): return lax.ppermute(value, names, pairs_of)  5.33 us
    pallas_call x1, Pallas kernels, shards(): pl.pallas_call(lambda *refs: near_kernel(ny, pairs, *refs), out_shape=[ja...  4.01 us
    pallas_call x1, Pallas kernels, shards(): pl.pallas_call(lambda *refs: last_kernel(ny, pairs, *refs), out_shape=[ja...  3.81 us
  transfers between devices with their start and end apart: 23, of which 4 were waited for; matrix products, arithmetic and copies ran while one was open for 0% of the time, Pallas kernels for 11%

profile of v2, /device:TPU:1, one launch (start us, length us, event | category | flops | bytes accessed | tf_op | source)
XLA Modules:
  0.0 116.8 jit_solution(11711672567668018046)
XLA Ops:
  0.6 5.4 %collective-permute-start.16 = (f32[512,128]{1,0:T(8,128)}, f32[512,128]{1,0:T(8,128)S(1)}, u32[]{:S(2)}, u32[]{:S(2)}) collective-permute-start(f32[512,128]{1,0:T(8,128)} %refs_11_.1), channel_id=1, source_target_pairs={{32,1},{33,2},{34,3},{35,4},{36,5},{37,6},{38,7},{39,0},{0,39},{1,... | collective-permute-start | bytes 786440 | tf_op jit(solution)/shard_map/ppermute | solution.py:228
  6.0 0.0 copy-start
  6.0 1.6 %copy-done = f32[4096,128]{1,0:T(8,128)S(1)} copy-done((f32[4096,128]{1,0:T(8,128)S(1)}, f32[4096,128]{1,0:T(8,128)}, u32[]{:S(2)}) %copy-start) | copy-done | bytes 2097176
  7.6 1.5 %cut.1 = (f32[640,128]{1,0:T(8,128)S(1)}, f32[640,128]{1,0:T(8,128)S(1)}, f32[640,128]{1,0:T(8,128)S(1)}) custom-call(f32[4096,128]{1,0:T(8,128)S(1)} %copy-done), custom_call_target="tpu_custom_call" | custom-call | tf_op jit(solution)/shard_map/cut/pallas_call | solution.py:247
  9.2 3.1 %collective-permute-start.13 = (f32[640,128]{1,0:T(8,128)S(1)}, f32[640,128]{1,0:T(8,128)S(1)}, u32[]{:S(2)}, u32[]{:S(2)}) collective-permute-start(f32[640,128]{1,0:T(8,128)S(1)} %get-tuple-element.13), channel_id=1, source_target_pairs={{0,8},{8,16},{16,24},{24,0},{1,9},{9,17},{17,25},{25,1},{2,10},{10... | collective-permute-start | bytes 983048 | tf_op jit(solution)/shard_map/ppermute | solution.py:234
  12.3 5.1 %collective-permute-start = (f32[2,512,128]{2,1,0:T(8,128)S(1)}, f32[2,512,128]{2,1,0:T(8,128)S(1)}, u32[]{:S(2)}, u32[]{:S(2)}) collective-permute-start(f32[2,512,128]{2,1,0:T(8,128)S(1)} %copy-done.3), channel_id=1, source_target_pairs={{0,64},{64,128},{128,192},{192,256},{256,320},{320,384},{384,448},... | collective-permute-start | bytes 1572872 | tf_op jit(solution)/shard_map/ppermute | solution.py:228
  17.4 8.3 %collective-permute-start.3 = (f32[2,512,128]{2,1,0:T(8,128)S(1)}, f32[2,512,128]{2,1,0:T(8,128)S(1)}, u32[]{:S(2)}, u32[]{:S(2)}) collective-permute-start(f32[2,512,128]{2,1,0:T(8,128)S(1)} %copy-done.3), channel_id=1, source_target_pairs={{32,64},{96,128},{160,192},{224,256},{288,320},{352,384},{416,448}... | collective-permute-start | bytes 1572872 | tf_op jit(solution)/shard_map/ppermute | solution.py:228
  25.7 0.0 collective-permute-done.16.refs_0_
  25.7 2.2 %collective-permute-start.17 = (f32[512,128]{1,0:T(8,128)S(1)}, f32[512,128]{1,0:T(8,128)S(1)}, u32[]{:S(2)}, u32[]{:S(2)}) collective-permute-start(f32[512,128]{1,0:T(8,128)S(1)} %collective-permute-done.16.refs_0_), channel_id=1, source_target_pairs={{0,1},{1,2},{2,3},{3,4},{4,5},{5,6},{6,7},{7,0},{32,39},{33,32},{3... | collective-permute-start | bytes 786440 | tf_op jit(solution)/shard_map/ppermute | solution.py:228
  27.9 4.4 %collective-permute-start.14 = (f32[640,128]{1,0:T(8,128)S(1)}, f32[640,128]{1,0:T(8,128)S(1)}, u32[]{:S(2)}, u32[]{:S(2)}) collective-permute-start(f32[640,128]{1,0:T(8,128)S(1)} %get-tuple-element.14), channel_id=1, source_target_pairs={{0,16},{8,24},{16,0},{24,8},{1,17},{9,25},{17,1},{25,9},{2,18},{10... | collective-permute-start | bytes 983048 | tf_op jit(solution)/shard_map/ppermute | solution.py:234
  32.2 0.0 collective-permute-done.13.refs_4_.refs_6_
  32.3 3.1 %collective-permute-start.15 = (f32[640,128]{1,0:T(8,128)S(1)}, f32[640,128]{1,0:T(8,128)S(1)}, u32[]{:S(2)}, u32[]{:S(2)}) collective-permute-start(f32[640,128]{1,0:T(8,128)S(1)} %get-tuple-element.15), channel_id=1, source_target_pairs={{0,24},{8,0},{16,8},{24,16},{1,25},{9,1},{17,9},{25,17},{2,26},{10... | collective-permute-start | bytes 983048 | tf_op jit(solution)/shard_map/ppermute | solution.py:234
  35.3 0.0 collective-permute-done.17.refs_1_
  35.3 3.4 %collective-permute-start.18 = (f32[512,128]{1,0:T(8,128)S(1)}, f32[512,128]{1,0:T(8,128)S(1)}, u32[]{:S(2)}, u32[]{:S(2)}) collective-permute-start(f32[512,128]{1,0:T(8,128)S(1)} %collective-permute-done.17.refs_1_), channel_id=1, source_target_pairs={{0,1},{1,2},{2,3},{3,4},{4,5},{5,6},{6,7},{7,0},{32,39},{33,32},{3... | collective-permute-start | bytes 786440 | tf_op jit(solution)/shard_map/ppermute | solution.py:228
  38.8 0.0 collective-permute-done.refs_5_
  38.8 3.0 %collective-permute-start.1 = (f32[2,512,128]{2,1,0:T(8,128)S(1)}, f32[2,512,128]{2,1,0:T(8,128)S(1)}, u32[]{:S(2)}, u32[]{:S(2)}) collective-permute-start(f32[2,512,128]{2,1,0:T(8,128)S(1)} %collective-permute-done.refs_5_), channel_id=1, source_target_pairs={{0,64},{64,128},{128,192},{192,256},{256,320},{320,384},{384,448},... | collective-permute-start | bytes 1572872 | tf_op jit(solution)/shard_map/ppermute | solution.py:228
  41.8 0.0 collective-permute-done.3.refs_8_
  41.8 3.0 %collective-permute-start.4 = (f32[2,512,128]{2,1,0:T(8,128)S(1)}, f32[2,512,128]{2,1,0:T(8,128)S(1)}, u32[]{:S(2)}, u32[]{:S(2)}) collective-permute-start(f32[2,512,128]{2,1,0:T(8,128)S(1)} %collective-permute-done.3.refs_8_), channel_id=1, source_target_pairs={{0,64},{64,128},{128,192},{192,256},{256,320},{320,384},{384,448},... | collective-permute-start | bytes 1572872 | tf_op jit(solution)/shard_map/ppermute | solution.py:228
  44.7 0.0 collective-permute-done.14.refs_5_.refs_7_
  44.8 2.2 %collective-permute-start.9 = (f32[512,128]{1,0:T(8,128)S(1)}, f32[512,128]{1,0:T(8,128)S(1)}, u32[]{:S(2)}, u32[]{:S(2)}) collective-permute-start(f32[512,128]{1,0:T(8,128)S(1)} %copy-done.2), channel_id=1, source_target_pairs={{0,1},{1,2},{2,3},{3,4},{4,5},{5,6},{6,7},{7,0},{32,39},{33,32},{3... | collective-permute-start | bytes 786440 | tf_op jit(solution)/shard_map/ppermute | solution.py:228
  47.0 0.0 collective-permute-done.15.refs_6_.refs_8_
  47.0 0.0 copy-start.4
  47.0 0.0 copy-start.5
  47.0 2.4 %collective-permute-start.7 = (f32[8,64,512]{2,1,0:T(8,128)S(1)}, f32[8,64,512]{2,1,0:T(8,128)S(1)}, u32[]{:S(2)}, u32[]{:S(2)}) collective-permute-start(f32[8,64,512]{2,1,0:T(8,128)S(1)} %bitcast.3), channel_id=1, source_target_pairs={{0,32},{32,0},{1,33},{33,1},{2,34},{34,2},{3,35},{35,3},{4,36},{36... | collective-permute-start | bytes 3145736 | tf_op jit(solution)/shard_map/ppermute | solution.py:231
  49.4 0.0 collective-permute-done.18.refs_2_
  49.4 1.3 %partial_other.1 = f32[4,512,128]{2,1,0:T(8,128)S(1)} custom-call(f32[512,128]{1,0:T(8,128)S(1)} %collective-permute-done.16.refs_0_, f32[512,128]{1,0:T(8,128)S(1)} %collective-permute-done.17.refs_1_, f32[512,128]{1,0:T(8,128)S(1)} %collective-permute-done.18.refs_2_, f32[4096,128]{1,0:T(8,128)S(1)} %copy-done, ...), custom_call_target="tpu_custom_call" | custom-call | flops 603979776 | bytes 2097152 | tf_op jit(solution)/shard_map/partial_other/pallas_call | solution.py:273
  50.7 1.9 %collective-permute-start.19 = (f32[4,512,128]{2,1,0:T(8,128)S(1)}, f32[4,512,128]{2,1,0:T(8,128)S(1)}, u32[]{:S(2)}, u32[]{:S(2)}) collective-permute-start(f32[4,512,128]{2,1,0:T(8,128)S(1)} %partial_other.1), channel_id=1, source_target_pairs={{0,32},{32,0},{1,33},{33,1},{2,34},{34,2},{3,35},{35,3},{4,36},{36... | collective-permute-start | bytes 3145736 | tf_op jit(solution)/shard_map/ppermute | solution.py:231
  52.6 0.0 collective-permute-done.9.refs_1_
  52.6 3.6 %collective-permute-start.10 = (f32[512,128]{1,0:T(8,128)S(1)}, f32[512,128]{1,0:T(8,128)S(1)}, u32[]{:S(2)}, u32[]{:S(2)}) collective-permute-start(f32[512,128]{1,0:T(8,128)S(1)} %collective-permute-done.9.refs_1_), channel_id=1, source_target_pairs={{0,1},{1,2},{2,3},{3,4},{4,5},{5,6},{6,7},{7,0},{32,39},{33,32},{3... | collective-permute-start | bytes 786440 | tf_op jit(solution)/shard_map/ppermute | solution.py:228
  56.2 0.0 collective-permute-done.1.refs_6_
  56.2 3.2 %collective-permute-start.2 = (f32[2,512,128]{2,1,0:T(8,128)S(1)}, f32[2,512,128]{2,1,0:T(8,128)S(1)}, u32[]{:S(2)}, u32[]{:S(2)}) collective-permute-start(f32[2,512,128]{2,1,0:T(8,128)S(1)} %collective-permute-done.1.refs_6_), channel_id=1, source_target_pairs={{0,64},{64,128},{128,192},{192,256},{256,320},{320,384},{384,448},... | collective-permute-start | bytes 1572872 | tf_op jit(solution)/shard_map/ppermute | solution.py:228
  59.4 0.0 collective-permute-done.4.refs_9_
  59.4 3.0 %collective-permute-start.5 = (f32[2,512,128]{2,1,0:T(8,128)S(1)}, f32[2,512,128]{2,1,0:T(8,128)S(1)}, u32[]{:S(2)}, u32[]{:S(2)}) collective-permute-start(f32[2,512,128]{2,1,0:T(8,128)S(1)} %collective-permute-done.4.refs_9_), channel_id=1, source_target_pairs={{0,64},{64,128},{128,192},{192,256},{256,320},{320,384},{384,448},... | collective-permute-start | bytes 1572872 | tf_op jit(solution)/shard_map/ppermute | solution.py:228
  62.4 0.0 collective-permute-done.10.refs_2_
  62.4 2.1 %collective-permute-start.11 = (f32[512,128]{1,0:T(8,128)S(1)}, f32[512,128]{1,0:T(8,128)S(1)}, u32[]{:S(2)}, u32[]{:S(2)}) collective-permute-start(f32[512,128]{1,0:T(8,128)S(1)} %collective-permute-done.10.refs_2_), channel_id=1, source_target_pairs={{0,1},{1,2},{2,3},{3,4},{4,5},{5,6},{6,7},{7,0},{32,39},{33,32},{3... | collective-permute-start | bytes 786440 | tf_op jit(solution)/shard_map/ppermute | solution.py:228
  64.5 5.3 %collective-permute-done.11.refs_3_ = f32[512,128]{1,0:T(8,128)S(1)} collective-permute-done((f32[512,128]{1,0:T(8,128)S(1)}, f32[512,128]{1,0:T(8,128)S(1)}, u32[]{:S(2)}, u32[]{:S(2)}) %collective-permute-start.11) | collective-permute-done | bytes 262176 | tf_op jit(solution)/shard_map/ppermute | solution.py:228
  69.8 3.3 %collective-permute-start.12 = (f32[512,128]{1,0:T(8,128)S(1)}, f32[512,128]{1,0:T(8,128)S(1)}, u32[]{:S(2)}, u32[]{:S(2)}) collective-permute-start(f32[512,128]{1,0:T(8,128)S(1)} %collective-permute-done.11.refs_3_), channel_id=1, source_target_pairs={{0,1},{1,2},{2,3},{3,4},{4,5},{5,6},{6,7},{7,0},{32,39},{33,32},{3... | collective-permute-start | bytes 786440 | tf_op jit(solution)/shard_map/ppermute | solution.py:228
  73.2 0.0 collective-permute-done.2.refs_2_.refs_7_
  73.2 0.0 collective-permute-done.5.refs_3_.refs_10_
  73.2 0.8 pick.1
  74.0 3.3 %collective-permute-start.6 = (f32[2,512,128]{2,1,0:T(8,128)S(1)}, f32[2,512,128]{2,1,0:T(8,128)S(1)}, u32[]{:S(2)}, u32[]{:S(2)}) collective-permute-start(f32[2,512,128]{2,1,0:T(8,128)S(1)} %pick.1), channel_id=1, source_target_pairs={{0,64},{64,128},{128,192},{192,256},{256,320},{320,384},{384,448},... | collective-permute-start | bytes 1572872 | tf_op jit(solution)/shard_map/ppermute | solution.py:228
  77.3 0.0 collective-permute-done.7.refs_3_
  77.3 1.0 copy-done.7
  78.2 4.0 %integral_near.1 = (f32[512,128]{1,0:T(8,128)S(1)}, f32[512,128]{1,0:T(8,128)}) custom-call(s32[128]{0:T(128)S(1)} %copy-done.4, s32[32]{0:T(128)S(1)} %copy-done.5, f32[8,64,512]{2,1,0:T(8,128)S(1)} %bitcast.4, f32[8,64,512]{2,1,0:T(8,128)} %copy-done.7, f32[2,512,128]{2,1,0:T(8,128)S(1)} %copy-done.3, f32[2,512,128]{2,1,0:T(8,128)S(1)} %collective-permute-done.refs_5_, ...), custom_call_target="tpu_custom_call" | custom-call | flops 201326592 | bytes 4194304 | tf_op jit(solution)/shard_map/integral_near/pallas_call | solution.py:301
  82.3 0.0 copy-start.9
  82.3 0.0 copy-start.8
  82.3 0.0 copy-start.6
  82.3 5.1 %collective-permute-start.8 = (f32[512,128]{1,0:T(8,128)}, f32[512,128]{1,0:T(8,128)S(1)}, u32[]{:S(2)}, u32[]{:S(2)}) collective-permute-start(f32[512,128]{1,0:T(8,128)} %get-tuple-element.12), channel_id=1, source_target_pairs={{0,32},{32,0},{1,33},{33,1},{2,34},{34,2},{3,35},{35,3},{4,36},{36... | collective-permute-start | bytes 786440 | tf_op jit(solution)/shard_map/ppermute | solution.py:231
  87.4 0.0 collective-permute-done.12.refs_4_
  87.4 0.0 collective-permute-done.19.refs_9_
  87.4 4.8 %partial_own.1 = (f32[512,128]{1,0:T(8,128)S(1)}, f32[512,128]{1,0:T(8,128)}, f32[512,128]{1,0:T(8,128)}, f32[512,128]{1,0:T(8,128)}) custom-call(f32[512,128]{1,0:T(8,128)S(1)} %copy-done.2, f32[512,128]{1,0:T(8,128)S(1)} %collective-permute-done.9.refs_1_, f32[512,128]{1,0:T(8,128)S(1)} %collective-permute-done.10.refs_2_, ...), custom_call_target="tpu_custom_call" | custom-call | flops 1006632960 | bytes 2097152 | tf_op jit(solution)/shard_map/partial_own/pallas_call | solution.py:273
  92.3 3.2 %collective-permute-start.20 = (f32[512,128]{1,0:T(8,128)}, f32[512,128]{1,0:T(8,128)}, u32[]{:S(2)}, u32[]{:S(2)}) collective-permute-start(f32[512,128]{1,0:T(8,128)} %get-tuple-element.17), channel_id=1, source_target_pairs={{0,24},{8,0},{16,8},{24,16},{1,25},{9,1},{17,9},{25,17},{2,26},{10... | collective-permute-start | bytes 786440 | tf_op jit(solution)/shard_map/ppermute | solution.py:234
  95.5 3.4 %collective-permute-start.21 = (f32[512,128]{1,0:T(8,128)}, f32[512,128]{1,0:T(8,128)}, u32[]{:S(2)}, u32[]{:S(2)}) collective-permute-start(f32[512,128]{1,0:T(8,128)} %get-tuple-element.18), channel_id=1, source_target_pairs={{0,16},{8,24},{16,0},{24,8},{1,17},{9,25},{17,1},{25,9},{2,18},{10... | collective-permute-start | bytes 786440 | tf_op jit(solution)/shard_map/ppermute | solution.py:234
  98.9 1.9 %collective-permute-start.22 = (f32[512,128]{1,0:T(8,128)}, f32[512,128]{1,0:T(8,128)}, u32[]{:S(2)}, u32[]{:S(2)}) collective-permute-start(f32[512,128]{1,0:T(8,128)} %get-tuple-element.19), channel_id=1, source_target_pairs={{0,8},{8,16},{16,24},{24,0},{1,9},{9,17},{17,25},{25,1},{2,10},{10... | collective-permute-start | bytes 786440 | tf_op jit(solution)/shard_map/ppermute | solution.py:234
  100.8 0.0 copy-done.9
  100.9 0.1 copy.12
  100.9 0.1 reshape.7.refs_2_
  101.0 0.1 copy.13.refs_12_
  101.2 0.0 collective-permute-done.8.refs_6_
  101.2 0.0 collective-permute-done.6.refs_4_
  101.2 1.2 %collective-permute-done.20.refs_8_ = f32[512,128]{1,0:T(8,128)} collective-permute-done((f32[512,128]{1,0:T(8,128)}, f32[512,128]{1,0:T(8,128)}, u32[]{:S(2)}, u32[]{:S(2)}) %collective-permute-start.20) | collective-permute-done | bytes 262176 | tf_op jit(solution)/shard_map/ppermute | solution.py:234
  102.4 4.4 %collective-permute-done.21.refs_9_ = f32[512,128]{1,0:T(8,128)} collective-permute-done((f32[512,128]{1,0:T(8,128)}, f32[512,128]{1,0:T(8,128)}, u32[]{:S(2)}, u32[]{:S(2)}) %collective-permute-start.21) | collective-permute-done | bytes 262176 | tf_op jit(solution)/shard_map/ppermute | solution.py:234
  106.8 6.2 %collective-permute-done.22.refs_10_ = f32[512,128]{1,0:T(8,128)} collective-permute-done((f32[512,128]{1,0:T(8,128)}, f32[512,128]{1,0:T(8,128)}, u32[]{:S(2)}, u32[]{:S(2)}) %collective-permute-start.22) | collective-permute-done | bytes 262176 | tf_op jit(solution)/shard_map/ppermute | solution.py:234
  113.0 3.8 %integral_far_update.1 = (f32[512,128]{1,0:T(8,128)}, f32[512,128]{1,0:T(8,128)}) custom-call(s32[128]{0:T(128)S(1)} %copy-done.4, s32[32]{0:T(128)S(1)} %copy-done.5, s32[16]{0:T(128)S(1)} %reshape.7.refs_2_, f32[8,64,512]{2,1,0:T(8,128)S(1)} %bitcast.5, f32[2,512,128]{2,1,0:T(8,128)S(1)} %collective-permute-done.6.refs_4_, ...), custom_call_target="tpu_custom_call" | custom-call | tf_op jit(solution)/shard_map/integral_far_update/pallas_call | solution.py:320
  (11 shorter events, 0.0 us)
Async XLA Ops:
  0.6 25.0 %collective-permute-start.16 = (f32[512,128]{1,0:T(8,128)}, f32[512,128]{1,0:T(8,128)S(1)}, u32[]{:S(2)}, u32[]{:S(2)}) collective-permute-start(f32[512,128]{1,0:T(8,128)} %refs_11_.1), channel_id=1, source_target_pairs={{32,1},{33,2},{34,3},{35,4},{36,5},{37,6},{38,7},{39,0},{0,39},{1,... | collective-permute-start | bytes 786440 | tf_op jit(solution)/shard_map/ppermute | solution.py:228
  6.0 1.6 %copy-start = (f32[4096,128]{1,0:T(8,128)S(1)}, f32[4096,128]{1,0:T(8,128)}, u32[]{:S(2)}) copy-start(f32[4096,128]{1,0:T(8,128)} %refs_5_.1) | copy-start | bytes 6291460
  7.6 4.7 %copy-start.3 = (f32[2,512,128]{2,1,0:T(8,128)S(1)}, f32[2,512,128]{2,1,0:T(8,128)}, u32[]{:S(2)}) copy-start(f32[2,512,128]{2,1,0:T(8,128)} %refs_4_.1) | copy-start | bytes 1572868
  7.6 37.1 %copy-start.2 = (f32[512,128]{1,0:T(8,128)S(1)}, f32[512,128]{1,0:T(8,128)}, u32[]{:S(2)}) copy-start(f32[512,128]{1,0:T(8,128)} %refs_11_.1) | copy-start | bytes 786436
  7.6 39.3 %copy-start.1 = (f32[8,512,64]{1,2,0:T(8,128)S(1)}, f32[8,512,64]{1,2,0:T(8,128)}, u32[]{:S(2)}) copy-start(f32[8,512,64]{1,2,0:T(8,128)} %param.11) | copy-start | bytes 3145732
  9.2 23.1 %collective-permute-start.13 = (f32[640,128]{1,0:T(8,128)S(1)}, f32[640,128]{1,0:T(8,128)S(1)}, u32[]{:S(2)}, u32[]{:S(2)}) collective-permute-start(f32[640,128]{1,0:T(8,128)S(1)} %get-tuple-element.13), channel_id=1, source_target_pairs={{0,8},{8,16},{16,24},{24,0},{1,9},{9,17},{17,25},{25,1},{2,10},{10... | collective-permute-start | bytes 983048 | tf_op jit(solution)/shard_map/ppermute | solution.py:234
  12.3 26.5 %collective-permute-start = (f32[2,512,128]{2,1,0:T(8,128)S(1)}, f32[2,512,128]{2,1,0:T(8,128)S(1)}, u32[]{:S(2)}, u32[]{:S(2)}) collective-permute-start(f32[2,512,128]{2,1,0:T(8,128)S(1)} %copy-done.3), channel_id=1, source_target_pairs={{0,64},{64,128},{128,192},{192,256},{256,320},{320,384},{384,448},... | collective-permute-start | bytes 1572872 | tf_op jit(solution)/shard_map/ppermute | solution.py:228
  17.4 24.4 %collective-permute-start.3 = (f32[2,512,128]{2,1,0:T(8,128)S(1)}, f32[2,512,128]{2,1,0:T(8,128)S(1)}, u32[]{:S(2)}, u32[]{:S(2)}) collective-permute-start(f32[2,512,128]{2,1,0:T(8,128)S(1)} %copy-done.3), channel_id=1, source_target_pairs={{32,64},{96,128},{160,192},{224,256},{288,320},{352,384},{416,448}... | collective-permute-start | bytes 1572872 | tf_op jit(solution)/shard_map/ppermute | solution.py:228
  25.7 9.7 %collective-permute-start.17 = (f32[512,128]{1,0:T(8,128)S(1)}, f32[512,128]{1,0:T(8,128)S(1)}, u32[]{:S(2)}, u32[]{:S(2)}) collective-permute-start(f32[512,128]{1,0:T(8,128)S(1)} %collective-permute-done.16.refs_0_), channel_id=1, source_target_pairs={{0,1},{1,2},{2,3},{3,4},{4,5},{5,6},{6,7},{7,0},{32,39},{33,32},{3... | collective-permute-start | bytes 786440 | tf_op jit(solution)/shard_map/ppermute | solution.py:228
  27.9 16.9 %collective-permute-start.14 = (f32[640,128]{1,0:T(8,128)S(1)}, f32[640,128]{1,0:T(8,128)S(1)}, u32[]{:S(2)}, u32[]{:S(2)}) collective-permute-start(f32[640,128]{1,0:T(8,128)S(1)} %get-tuple-element.14), channel_id=1, source_target_pairs={{0,16},{8,24},{16,0},{24,8},{1,17},{9,25},{17,1},{25,9},{2,18},{10... | collective-permute-start | bytes 983048 | tf_op jit(solution)/shard_map/ppermute | solution.py:234
  32.3 14.7 %collective-permute-start.15 = (f32[640,128]{1,0:T(8,128)S(1)}, f32[640,128]{1,0:T(8,128)S(1)}, u32[]{:S(2)}, u32[]{:S(2)}) collective-permute-start(f32[640,128]{1,0:T(8,128)S(1)} %get-tuple-element.15), channel_id=1, source_target_pairs={{0,24},{8,0},{16,8},{24,16},{1,25},{9,1},{17,9},{25,17},{2,26},{10... | collective-permute-start | bytes 983048 | tf_op jit(solution)/shard_map/ppermute | solution.py:234
  35.3 14.1 %collective-permute-start.18 = (f32[512,128]{1,0:T(8,128)S(1)}, f32[512,128]{1,0:T(8,128)S(1)}, u32[]{:S(2)}, u32[]{:S(2)}) collective-permute-start(f32[512,128]{1,0:T(8,128)S(1)} %collective-permute-done.17.refs_1_), channel_id=1, source_target_pairs={{0,1},{1,2},{2,3},{3,4},{4,5},{5,6},{6,7},{7,0},{32,39},{33,32},{3... | collective-permute-start | bytes 786440 | tf_op jit(solution)/shard_map/ppermute | solution.py:228
  38.8 17.5 %collective-permute-start.1 = (f32[2,512,128]{2,1,0:T(8,128)S(1)}, f32[2,512,128]{2,1,0:T(8,128)S(1)}, u32[]{:S(2)}, u32[]{:S(2)}) collective-permute-start(f32[2,512,128]{2,1,0:T(8,128)S(1)} %collective-permute-done.refs_5_), channel_id=1, source_target_pairs={{0,64},{64,128},{128,192},{192,256},{256,320},{320,384},{384,448},... | collective-permute-start | bytes 1572872 | tf_op jit(solution)/shard_map/ppermute | solution.py:228
  41.8 17.7 %collective-permute-start.4 = (f32[2,512,128]{2,1,0:T(8,128)S(1)}, f32[2,512,128]{2,1,0:T(8,128)S(1)}, u32[]{:S(2)}, u32[]{:S(2)}) collective-permute-start(f32[2,512,128]{2,1,0:T(8,128)S(1)} %collective-permute-done.3.refs_8_), channel_id=1, source_target_pairs={{0,64},{64,128},{128,192},{192,256},{256,320},{320,384},{384,448},... | collective-permute-start | bytes 1572872 | tf_op jit(solution)/shard_map/ppermute | solution.py:228
  44.8 7.9 %collective-permute-start.9 = (f32[512,128]{1,0:T(8,128)S(1)}, f32[512,128]{1,0:T(8,128)S(1)}, u32[]{:S(2)}, u32[]{:S(2)}) collective-permute-start(f32[512,128]{1,0:T(8,128)S(1)} %copy-done.2), channel_id=1, source_target_pairs={{0,1},{1,2},{2,3},{3,4},{4,5},{5,6},{6,7},{7,0},{32,39},{33,32},{3... | collective-permute-start | bytes 786440 | tf_op jit(solution)/shard_map/ppermute | solution.py:228
  47.0 26.2 %copy-start.4 = (s32[128]{0:T(128)S(1)}, s32[128]{0:T(128)}, u32[]{:S(2)}) copy-start(s32[128]{0:T(128)} %refs_0_.9) | copy-start | bytes 1540
  47.0 26.2 %copy-start.5 = (s32[32]{0:T(128)S(1)}, s32[32]{0:T(128)}, u32[]{:S(2)}) copy-start(s32[32]{0:T(128)} %refs_1_.5) | copy-start | bytes 388
  47.0 30.3 %collective-permute-start.7 = (f32[8,64,512]{2,1,0:T(8,128)S(1)}, f32[8,64,512]{2,1,0:T(8,128)S(1)}, u32[]{:S(2)}, u32[]{:S(2)}) collective-permute-start(f32[8,64,512]{2,1,0:T(8,128)S(1)} %bitcast.3), channel_id=1, source_target_pairs={{0,32},{32,0},{1,33},{33,1},{2,34},{34,2},{3,35},{35,3},{4,36},{36... | collective-permute-start | bytes 3145736 | tf_op jit(solution)/shard_map/ppermute | solution.py:231
  50.7 36.7 %collective-permute-start.19 = (f32[4,512,128]{2,1,0:T(8,128)S(1)}, f32[4,512,128]{2,1,0:T(8,128)S(1)}, u32[]{:S(2)}, u32[]{:S(2)}) collective-permute-start(f32[4,512,128]{2,1,0:T(8,128)S(1)} %partial_other.1), channel_id=1, source_target_pairs={{0,32},{32,0},{1,33},{33,1},{2,34},{34,2},{3,35},{35,3},{4,36},{36... | collective-permute-start | bytes 3145736 | tf_op jit(solution)/shard_map/ppermute | solution.py:231
  52.6 9.8 %collective-permute-start.10 = (f32[512,128]{1,0:T(8,128)S(1)}, f32[512,128]{1,0:T(8,128)S(1)}, u32[]{:S(2)}, u32[]{:S(2)}) collective-permute-start(f32[512,128]{1,0:T(8,128)S(1)} %collective-permute-done.9.refs_1_), channel_id=1, source_target_pairs={{0,1},{1,2},{2,3},{3,4},{4,5},{5,6},{6,7},{7,0},{32,39},{33,32},{3... | collective-permute-start | bytes 786440 | tf_op jit(solution)/shard_map/ppermute | solution.py:228
  56.2 16.9 %collective-permute-start.2 = (f32[2,512,128]{2,1,0:T(8,128)S(1)}, f32[2,512,128]{2,1,0:T(8,128)S(1)}, u32[]{:S(2)}, u32[]{:S(2)}) collective-permute-start(f32[2,512,128]{2,1,0:T(8,128)S(1)} %collective-permute-done.1.refs_6_), channel_id=1, source_target_pairs={{0,64},{64,128},{128,192},{192,256},{256,320},{320,384},{384,448},... | collective-permute-start | bytes 1572872 | tf_op jit(solution)/shard_map/ppermute | solution.py:228
  59.4 13.7 %collective-permute-start.5 = (f32[2,512,128]{2,1,0:T(8,128)S(1)}, f32[2,512,128]{2,1,0:T(8,128)S(1)}, u32[]{:S(2)}, u32[]{:S(2)}) collective-permute-start(f32[2,512,128]{2,1,0:T(8,128)S(1)} %collective-permute-done.4.refs_9_), channel_id=1, source_target_pairs={{0,64},{64,128},{128,192},{192,256},{256,320},{320,384},{384,448},... | collective-permute-start | bytes 1572872 | tf_op jit(solution)/shard_map/ppermute | solution.py:228
  62.4 7.4 %collective-permute-start.11 = (f32[512,128]{1,0:T(8,128)S(1)}, f32[512,128]{1,0:T(8,128)S(1)}, u32[]{:S(2)}, u32[]{:S(2)}) collective-permute-start(f32[512,128]{1,0:T(8,128)S(1)} %collective-permute-done.10.refs_2_), channel_id=1, source_target_pairs={{0,1},{1,2},{2,3},{3,4},{4,5},{5,6},{6,7},{7,0},{32,39},{33,32},{3... | collective-permute-start | bytes 786440 | tf_op jit(solution)/shard_map/ppermute | solution.py:228
  69.8 17.6 %collective-permute-start.12 = (f32[512,128]{1,0:T(8,128)S(1)}, f32[512,128]{1,0:T(8,128)S(1)}, u32[]{:S(2)}, u32[]{:S(2)}) collective-permute-start(f32[512,128]{1,0:T(8,128)S(1)} %collective-permute-done.11.refs_3_), channel_id=1, source_target_pairs={{0,1},{1,2},{2,3},{3,4},{4,5},{5,6},{6,7},{7,0},{32,39},{33,32},{3... | collective-permute-start | bytes 786440 | tf_op jit(solution)/shard_map/ppermute | solution.py:228
  74.0 27.2 %collective-permute-start.6 = (f32[2,512,128]{2,1,0:T(8,128)S(1)}, f32[2,512,128]{2,1,0:T(8,128)S(1)}, u32[]{:S(2)}, u32[]{:S(2)}) collective-permute-start(f32[2,512,128]{2,1,0:T(8,128)S(1)} %pick.1), channel_id=1, source_target_pairs={{0,64},{64,128},{128,192},{192,256},{256,320},{320,384},{384,448},... | collective-permute-start | bytes 1572872 | tf_op jit(solution)/shard_map/ppermute | solution.py:228
  77.3 1.0 copy-start.7
  82.3 18.6 %copy-start.9 = (s32[8,2]{0,1:T(2,128)S(1)}, s32[8,2]{0,1:T(2,128)}, u32[]{:S(2)}) copy-start(s32[8,2]{0,1:T(2,128)} %param.15) | copy-start | bytes 196
  82.3 18.7 %copy-start.8 = (f32[512]{0:T(512)S(1)}, f32[512]{0:T(512)}, u32[]{:S(2)}) copy-start(f32[512]{0:T(512)} %param.16) | copy-start | bytes 6148
  82.3 30.7 %copy-start.6 = (f32[128]{0:T(128)S(1)}, f32[128]{0:T(128)}, u32[]{:S(2)}) copy-start(f32[128]{0:T(128)} %param.17) | copy-start | bytes 1540
  82.3 18.9 %collective-permute-start.8 = (f32[512,128]{1,0:T(8,128)}, f32[512,128]{1,0:T(8,128)S(1)}, u32[]{:S(2)}, u32[]{:S(2)}) collective-permute-start(f32[512,128]{1,0:T(8,128)} %get-tuple-element.12), channel_id=1, source_target_pairs={{0,32},{32,0},{1,33},{33,1},{2,34},{34,2},{3,35},{35,3},{4,36},{36... | collective-permute-start | bytes 786440 | tf_op jit(solution)/shard_map/ppermute | solution.py:231
  92.3 10.1 %collective-permute-start.20 = (f32[512,128]{1,0:T(8,128)}, f32[512,128]{1,0:T(8,128)}, u32[]{:S(2)}, u32[]{:S(2)}) collective-permute-start(f32[512,128]{1,0:T(8,128)} %get-tuple-element.17), channel_id=1, source_target_pairs={{0,24},{8,0},{16,8},{24,16},{1,25},{9,1},{17,9},{25,17},{2,26},{10... | collective-permute-start | bytes 786440 | tf_op jit(solution)/shard_map/ppermute | solution.py:234
  95.5 11.3 %collective-permute-start.21 = (f32[512,128]{1,0:T(8,128)}, f32[512,128]{1,0:T(8,128)}, u32[]{:S(2)}, u32[]{:S(2)}) collective-permute-start(f32[512,128]{1,0:T(8,128)} %get-tuple-element.18), channel_id=1, source_target_pairs={{0,16},{8,24},{16,0},{24,8},{1,17},{9,25},{17,1},{25,9},{2,18},{10... | collective-permute-start | bytes 786440 | tf_op jit(solution)/shard_map/ppermute | solution.py:234
  98.9 14.1 %collective-permute-start.22 = (f32[512,128]{1,0:T(8,128)}, f32[512,128]{1,0:T(8,128)}, u32[]{:S(2)}, u32[]{:S(2)}) collective-permute-start(f32[512,128]{1,0:T(8,128)} %get-tuple-element.19), channel_id=1, source_target_pairs={{0,8},{8,16},{16,24},{24,0},{1,9},{9,17},{17,25},{25,1},{2,10},{10... | collective-permute-start | bytes 786440 | tf_op jit(solution)/shard_map/ppermute | solution.py:234

commit v3 on v0

v3 whole, which is shorter than its diff:
```python
import jax
import jax.numpy as jnp
from jax import lax
from jax.experimental import pallas as pl
from jax.experimental.pallas import tpu as pltpu
from jax.sharding import Mesh
from jax.sharding import PartitionSpec as P

F32 = jnp.float32
PARAMS = pltpu.CompilerParams(vmem_limit_bytes=20 * 1024 * 1024)
HBM = pl.BlockSpec(memory_space=pltpu.HBM)
VMEM = pl.BlockSpec(memory_space=pltpu.VMEM)
SMEM = pl.BlockSpec(memory_space=pltpu.SMEM)
FAR = 4


def split(value):
    high = value.astype(jnp.bfloat16)
    low = (value - high.astype(F32)).astype(jnp.bfloat16)
    return high, low


def dot3(left, right):
    one = lambda a, b: jnp.dot(a, b, preferred_element_type=F32)
    return one(left[0], right[0]) + (one(left[0], right[1]) + one(left[1], right[0]))


def start_all(copies, sems):
    made = [pltpu.make_async_copy(src, dst, sems.at[i]) for i, (src, dst) in enumerate(copies)]
    for copy in made:
        copy.start()
    return made


def behind(index, size, core, step):
    return lax.rem(index + jnp.where(core == 0, size - step, step), size)


def dressing_kernel(nz, panels, high, low, held, sems):
    count, _, width = panels.shape
    core, z = lax.axis_index("core"), lax.axis_index("z")
    copies = []
    for t in range(FAR + 1):
        row = pl.multiple_of(behind(z, nz, core, t) * width, width)
        copies.append((panels.at[:, pl.ds(row, width)], held.at[t]))
    made = start_all(copies, sems)
    for t in range(FAR + 1):
        made[t].wait()
        for s in range(count):
            at = slice(t * width, (t + 1) * width), slice(s * width, (s + 1) * width)
            high[at], low[at] = split(held[t, s])


def products(out, left, right, plus=None):
    width = out.shape[2]
    for s in range(0, out.shape[0], 2):
        at = slice(s * width, (s + 2) * width)
        both = dot3(left, (right[0][:, at], right[1][:, at]))
        for k in range(2):
            value = both[:, k * width : (k + 1) * width]
            out[s + k] = value if plus is None else value + plus(s + k)


def product_kernel(first, *refs):
    count = len(refs) - 9
    pieces, refs = refs[:count], refs[count:]
    high, low, out, held, right_high, right_low, left_high, left_low, sems = refs
    width = held.shape[2]
    rows = pl.ds(first * width, count * width)
    copies = [(piece, held.at[k]) for k, piece in enumerate(pieces)]
    copies += [(high.at[rows], right_high), (low.at[rows], right_low)]
    made = start_all(copies, sems)
    for k in range(count):
        made[k].wait()
        at = slice(k * width, (k + 1) * width)
        left_high[:, at], left_low[:, at] = split(held[k])
    for copy in made[count:]:
        copy.wait()
    products(out, (left_high[...], left_low[...]), (right_high, right_low))


def integral_kernel(pairs, pair_block, block_home, mask, factor, gathered, out, factors, blocks, sems, block_sems):
    y, core = lax.axis_index("y"), lax.axis_index("core")
    fetched = []
    for i in range(pairs):
        home = block_home[pair_block[(y * 2 + core) * pairs + i]]
        fetched.append(
            (
                pltpu.make_async_copy(factor.at[i], factors.at[i], sems.at[i]),
                pltpu.make_async_copy(gathered.at[home], blocks.at[i], block_sems.at[i]),
            )
        )
        for copy in fetched[-1]:
            copy.start()
    tile = factors.shape[1]
    width = out.shape[1]
    lane = lax.broadcasted_iota(jnp.int32, (tile, width), 1)
    for i in range(pairs):
        for copy in fetched[i]:
            copy.wait()
        factor_high, factor_low = split(factors[i])
        high, low = split(blocks[i])
        both = jnp.dot(jnp.concatenate([factor_high, factor_low], axis=0), high, preferred_element_type=F32)
        integral = both[:tile] + (both[tile:] + jnp.dot(factor_high, low, preferred_element_type=F32))
        on = jnp.where(lane < tile, mask[2 * i], mask[2 * i + 1]).astype(F32)
        out[i * tile : (i + 1) * tile] = integral * on


def shards(
    amplitudes,
    dressing,
    pair_factor,
    blocks,
    pair_block,
    block_home,
    tile_mask,
    row_energy,
    column_energy,
):
    ny, nx, nz = lax.axis_size("y"), lax.axis_size("x"), lax.axis_size("z")
    pairs, naux, tile = pair_factor.shape
    rows, width = amplitudes.shape
    sem = pltpu.SemaphoreType.DMA

    def ring(value, axis, cross=False, hops=1):
        n = lax.axis_size(axis)
        names, at = (("y", "core"), lambda c, i: i * 2 + c) if axis == "y" else (("core", axis), lambda c, i: c * n + i)
        pairs_of = []
        for to in range(2):
            for i in range(n):
                pairs_of.append((at(1 - to if cross else to, i), at(to, (i + (hops, -hops)[to]) % n)))
        return lax.ppermute(value, names, pairs_of)

    def swap(value):
        return lax.ppermute(value, "core", [(0, 1), (1, 0)])

    def chain(value, axis):
        same, cross = [ring(value, axis)], [ring(value, axis, cross=True)]
        for _ in range(FAR - 2):
            same.append(ring(same[-1], axis))
            cross.append(ring(cross[-1], axis))
        return same, cross

    gathered = lax.all_gather(blocks, ("y", "core"), axis=0, tiled=True)
    factor = jnp.swapaxes(pair_factor, 1, 2)

    amp_same, amp_cross = chain(amplitudes, "z")
    amp_far = ring(amp_same[1], "z", hops=2)

    depth = nz * width
    panels = lax.all_to_all(dressing.reshape(nx, depth, width), "x", 0, 0)
    taken = (FAR + 1) * width
    bf16 = jnp.bfloat16
    shape = jax.ShapeDtypeStruct((nx, rows, width), F32)
    high, low = pl.pallas_call(
        lambda *refs: dressing_kernel(nz, *refs),
        out_shape=[jax.ShapeDtypeStruct((taken, nx * width), bf16)] * 2,
        in_specs=[HBM],
        out_specs=[VMEM] * 2,
        scratch_shapes=[pltpu.VMEM((FAR + 1, nx, width, width), F32), sem((FAR + 1,))],
        compiler_params=PARAMS,
        name="dressing_ready",
    )(panels)

    def product(pieces, first, name):
        count = len(pieces)
        return pl.pallas_call(
            lambda *refs: product_kernel(first, *refs),
            out_shape=shape,
            in_specs=[HBM] * (count + 2),
            out_specs=VMEM,
            scratch_shapes=[pltpu.VMEM((count, rows, width), F32)]
            + [pltpu.VMEM((count * width, nx * width), bf16)] * 2
            + [pltpu.VMEM((rows, count * width), bf16)] * 2
            + [sem((count + 2,))],
            compiler_params=PARAMS,
            name=name,
        )(*pieces, high, low)

    amp_same[-1], amp_cross[-1], amp_far = lax.optimization_barrier((amp_same[-1], amp_cross[-1], amp_far))
    other = swap(product(amp_cross, 1, "dressed_other"))
    own = product([amplitudes, *amp_same, amp_far], 0, "dressed_own")
    sums = lax.all_to_all(own + other, "x", 0, 0)

    integral = pl.pallas_call(
        lambda *refs: integral_kernel(pairs, *refs),
        out_shape=jax.ShapeDtypeStruct((rows, width), F32),
        in_specs=[SMEM] * 3 + [HBM] * 2,
        out_specs=VMEM,
        scratch_shapes=[
            pltpu.VMEM((pairs, tile, naux), F32),
            pltpu.VMEM((pairs, naux, width), F32),
            sem((pairs,)),
            sem((pairs,)),
        ],
        compiler_params=pltpu.CompilerParams(vmem_limit_bytes=56 * 1024 * 1024),
        name="integral",
    )(pair_block, block_home, tile_mask.reshape(-1), factor, gathered)
    residual = integral + ((sums[0] + sums[1]) + (sums[2] + sums[3]))
    return residual, amplitudes - residual / (row_energy[:, None] + column_energy[None, :])


def solution(mesh):
    sizes = {"y": 8, "core": 2, "x": 4, "z": 8}
    fine = Mesh(mesh.devices.reshape(tuple(sizes.values())), tuple(sizes))
    grp, row = ("y", "core"), ("x", "z")
    placed = (
        P(grp, row),
        P(None, row),
        P(grp, None, None),
        P(grp, None, row),
        P(),
        P(),
        P(grp, row),
        P(grp),
        P(row),
    )
    return jax.shard_map(
        shards,
        mesh=fine,
        in_specs=placed,
        out_specs=(P(grp, row), P(grp, row)),
        check_vma=False,
    )
```

time: 202 us -> 93 us (0.46)
  waiting for transfers between devices: 159 us -> 19 us
  starting transfers between devices: 0.08 us -> 43.8 us
  matrix products: 22.9 us -> 0 us
  Pallas kernels: 0 us -> 8.71 us
    all_gather x2 -> x1, waiting for transfers between devices: 158 us -> 4.57 us  [shards(): gathered = lax.all_gather(blocks, ('y', 'core'), axis=0, tiled=True)]
    ppermute x0 -> x8, starting transfers between devices: none -> 34.8 us  [the longest x7 32.6 us: ring(): return lax.ppermute(value, names, pairs_of)]
    dot_general x3 -> x0, matrix products: 22.9 us -> none  [the longest x1 10.6 us: shards(): chosen = jnp.einsum('ki,iqc->kqc', picked, portion, precision=highest)]
    ppermute x0 -> x8, waiting for transfers between devices: none -> 9.04 us  [the longest x7 8.98 us: ring(): return lax.ppermute(value, names, pairs_of)]
    all_to_all x0 -> x2, starting transfers between devices: none -> 8.93 us  [the longest x1 4.99 us: shards(): panels = lax.all_to_all(dressing.reshape(nx, depth, width), 'x', 0, 0)]
    pallas_call x0 -> x4, Pallas kernels: none -> 8.71 us  [the longest x1 4.53 us: shards(): pl.pallas_call(lambda *refs: integral_kernel(pairs, *refs), out_shape=jax...]
    all_to_all x0 -> x2, waiting for transfers between devices: none -> 4.74 us  [the longest x1 4.73 us: shards(): sums = lax.all_to_all(own + other, 'x', 0, 0)]
    unnamed x10 -> x21, local copies, waits for them, and re-layouts: 0.03 us -> 2.9 us
  transfers between devices with their start and end apart: 2 -> 11, of which waited for: 2 -> 6; matrix products, arithmetic and copies ran while one was open for 8% -> 2% of each run, Pallas kernels for 0% -> 9%
where the time goes in v3:
time: 93 us; the launch traced here: 92.2 us
  starting transfers between devices  43.8 us (47%)
  waiting for transfers between devices  19 us (20%)
  between operations  14.2 us (15%)
  Pallas kernels  8.71 us (9%)
  local copies, waits for them, and re-layouts  3.49 us (4%)
  other arithmetic  3 us (3%)
    ppermute x7, starting transfers between devices, ring(): return lax.ppermute(value, names, pairs_of)  32.6 us
    ppermute x7, waiting for transfers between devices, ring(): return lax.ppermute(value, names, pairs_of)  8.98 us
    all_to_all x1, starting transfers between devices, shards(): panels = lax.all_to_all(dressing.reshape(nx, depth, width), 'x', 0, 0)  4.99 us
    all_to_all x1, waiting for transfers between devices, shards(): sums = lax.all_to_all(own + other, 'x', 0, 0)  4.73 us
    all_gather x1, waiting for transfers between devices, shards(): gathered = lax.all_gather(blocks, ('y', 'core'), axis=0, tiled=True)  4.57 us
    pallas_call x1, Pallas kernels, shards(): pl.pallas_call(lambda *refs: integral_kernel(pairs, *refs), out_shape=jax...  4.53 us
    all_to_all x1, starting transfers between devices, shards(): sums = lax.all_to_all(own + other, 'x', 0, 0)  3.95 us
    pallas_call x2, Pallas kernels, product(): pl.pallas_call(lambda *refs: product_kernel(first, *refs), out_shape=shap...  3.79 us
  transfers between devices with their start and end apart: 11, of which 6 were waited for; matrix products, arithmetic and copies ran while one was open for 2% of the time, Pallas kernels for 9%

profile of v3, /device:TPU:1, one launch (start us, length us, event | category | flops | bytes accessed | tf_op | source)
XLA Modules:
  0.0 92.2 jit_solution(9402478649354704652)
XLA Ops:
  7.2 0.0 all-gather.2.cloned.1.call-start
  7.2 0.7 all-gather.2.cloned.1.call-update
  7.9 0.0 copy-start
  7.9 5.0 %all-to-all-start = ((f32[4,1024,128]{2,1,0:T(8,128)}), f32[4,1024,128]{2,1,0:T(8,128)S(1)}, u32[]{:S(2)}, u32[]{:S(2)}) async-start(f32[4,1024,128]{2,1,0:T(8,128)} %bitcast.7), calls=%async_computation | async-start | bytes 4194304 | tf_op jit(solution)/shard_map/all_to_all | solution.py:151
  12.9 0.0 copy-done
  12.9 4.8 %collective-permute-start.3 = (f32[512,128]{1,0:T(8,128)S(1)}, f32[512,128]{1,0:T(8,128)S(1)}, u32[]{:S(2)}, u32[]{:S(2)}) collective-permute-start(f32[512,128]{1,0:T(8,128)S(1)} %copy-done), channel_id=1, source_target_pairs={{32,1},{33,2},{34,3},{35,4},{36,5},{37,6},{38,7},{39,0},{0,39},{1,... | collective-permute-start | bytes 786440 | tf_op jit(solution)/shard_map/ppermute | solution.py:132
  17.7 7.7 %collective-permute-start = (f32[512,128]{1,0:T(8,128)S(1)}, f32[512,128]{1,0:T(8,128)S(1)}, u32[]{:S(2)}, u32[]{:S(2)}) collective-permute-start(f32[512,128]{1,0:T(8,128)S(1)} %copy-done), channel_id=1, source_target_pairs={{0,1},{1,2},{2,3},{3,4},{4,5},{5,6},{6,7},{7,0},{32,39},{33,32},{3... | collective-permute-start | bytes 786440 | tf_op jit(solution)/shard_map/ppermute | solution.py:132
  25.5 0.0 collective-permute-done.3.refs_0_
  25.5 8.6 %collective-permute-start.4 = (f32[512,128]{1,0:T(8,128)S(1)}, f32[512,128]{1,0:T(8,128)S(1)}, u32[]{:S(2)}, u32[]{:S(2)}) collective-permute-start(f32[512,128]{1,0:T(8,128)S(1)} %collective-permute-done.3.refs_0_), channel_id=1, source_target_pairs={{0,1},{1,2},{2,3},{3,4},{4,5},{5,6},{6,7},{7,0},{32,39},{33,32},{3... | collective-permute-start | bytes 786440 | tf_op jit(solution)/shard_map/ppermute | solution.py:132
  34.2 0.0 copy-start.1
  34.2 0.7 copy-done.1
  34.9 0.0 collective-permute-done.refs_1_
  34.9 1.9 %collective-permute-start.1 = (f32[512,128]{1,0:T(8,128)S(1)}, f32[512,128]{1,0:T(8,128)S(1)}, u32[]{:S(2)}, u32[]{:S(2)}) collective-permute-start(f32[512,128]{1,0:T(8,128)S(1)} %collective-permute-done.refs_1_), channel_id=1, source_target_pairs={{0,1},{1,2},{2,3},{3,4},{4,5},{5,6},{6,7},{7,0},{32,39},{33,32},{3... | collective-permute-start | bytes 786440 | tf_op jit(solution)/shard_map/ppermute | solution.py:132
  36.8 0.7 collective-permute-done.4.refs_1_
  37.4 5.4 %collective-permute-start.5 = (f32[512,128]{1,0:T(8,128)S(1)}, f32[512,128]{1,0:T(8,128)S(1)}, u32[]{:S(2)}, u32[]{:S(2)}) collective-permute-start(f32[512,128]{1,0:T(8,128)S(1)} %collective-permute-done.4.refs_1_), channel_id=1, source_target_pairs={{0,1},{1,2},{2,3},{3,4},{4,5},{5,6},{6,7},{7,0},{32,39},{33,32},{3... | collective-permute-start | bytes 786440 | tf_op jit(solution)/shard_map/ppermute | solution.py:132
  42.9 0.0 copy-start.3
  42.9 0.7 copy-done.3
  43.6 0.0 collective-permute-done.1.refs_2_
  43.6 1.9 %collective-permute-start.6 = (f32[512,128]{1,0:T(8,128)S(1)}, f32[512,128]{1,0:T(8,128)S(1)}, u32[]{:S(2)}, u32[]{:S(2)}) collective-permute-start(f32[512,128]{1,0:T(8,128)S(1)} %collective-permute-done.1.refs_2_), channel_id=1, source_target_pairs={{0,2},{1,3},{2,4},{3,5},{4,6},{5,7},{6,0},{7,1},{32,38},{33,39},{3... | collective-permute-start | bytes 786440 | tf_op jit(solution)/shard_map/ppermute | solution.py:132
  45.5 2.1 %collective-permute-start.2 = (f32[512,128]{1,0:T(8,128)S(1)}, f32[512,128]{1,0:T(8,128)S(1)}, u32[]{:S(2)}, u32[]{:S(2)}) collective-permute-start(f32[512,128]{1,0:T(8,128)S(1)} %collective-permute-done.1.refs_2_), channel_id=1, source_target_pairs={{0,1},{1,2},{2,3},{3,4},{4,5},{5,6},{6,7},{7,0},{32,39},{33,32},{3... | collective-permute-start | bytes 786440 | tf_op jit(solution)/shard_map/ppermute | solution.py:132
  47.6 0.0 collective-permute-done.5.refs_2_
  47.6 0.0 copy-start.5
  47.6 0.7 copy-done.5
  48.3 4.7 %collective-permute-done.6.refs_4_ = f32[512,128]{1,0:T(8,128)S(1)} collective-permute-done((f32[512,128]{1,0:T(8,128)S(1)}, f32[512,128]{1,0:T(8,128)S(1)}, u32[]{:S(2)}, u32[]{:S(2)}) %collective-permute-start.6) | collective-permute-done | bytes 262176 | tf_op jit(solution)/shard_map/ppermute | solution.py:132
  53.0 3.6 %collective-permute-done.2.refs_3_ = f32[512,128]{1,0:T(8,128)S(1)} collective-permute-done((f32[512,128]{1,0:T(8,128)S(1)}, f32[512,128]{1,0:T(8,128)S(1)}, u32[]{:S(2)}, u32[]{:S(2)}) %collective-permute-start.2) | collective-permute-done | bytes 262176 | tf_op jit(solution)/shard_map/ppermute | solution.py:132
  56.6 0.0 all-to-all-done.refs_0_
  56.6 0.0 copy-start.2
  56.6 0.0 copy-start.4
  56.6 0.0 copy-start.6
  56.6 0.4 dressing_ready.1
  57.0 0.5 copy-done.2
  57.6 0.1 copy-done.4
  57.7 0.1 copy-done.6
  57.7 1.6 %dressed_other.1 = f32[4,512,128]{2,1,0:T(8,128)S(1)} custom-call(f32[512,128]{1,0:T(8,128)S(1)} %copy-done.2, f32[512,128]{1,0:T(8,128)S(1)} %copy-done.4, f32[512,128]{1,0:T(8,128)S(1)} %copy-done.6, bf16[640,512]{1,0:T(8,128)(2,1)S(1)} %get-tuple-element.9.refs_5_.refs_3_, bf16[640,512]{1,0:T(8,128)(2,1)S(1)} %get-tuple-element.10.refs_6_.refs_4_), custom_call_target="tpu_custom_call" | custom-call | tf_op jit(solution)/shard_map/dressed_other/pallas_call | solution.py:167
  59.3 2.3 %collective-permute-start.7 = (f32[4,512,128]{2,1,0:T(8,128)S(1)}, f32[4,512,128]{2,1,0:T(8,128)S(1)}, u32[]{:S(2)}, u32[]{:S(2)}) collective-permute-start(f32[4,512,128]{2,1,0:T(8,128)S(1)} %dressed_other.1), channel_id=1, source_target_pairs={{0,32},{32,0},{1,33},{33,1},{2,34},{34,2},{3,35},{35,3},{4,36},{36... | collective-permute-start | bytes 3145736 | tf_op jit(solution)/shard_map/ppermute | solution.py:135
  61.6 2.2 %dressed_own.1 = f32[4,512,128]{2,1,0:T(8,128)S(1)} custom-call(f32[512,128]{1,0:T(8,128)S(1)} %copy-done, f32[512,128]{1,0:T(8,128)S(1)} %collective-permute-done.refs_1_, f32[512,128]{1,0:T(8,128)S(1)} %collective-permute-done.1.refs_2_, f32[512,128]{1,0:T(8,128)S(1)} %collective-permute-done.2.refs_3_, f32[512,128]{1,0:T(8,128)S(1)} %collective-permute-done.6.refs_4_, ...), custom_call_target="tpu_custom_call" | custom-call | tf_op jit(solution)/shard_map/dressed_own/pallas_call | solution.py:167
  63.8 0.0 copy-start.8
  63.8 0.1 collective-permute-done.7
  63.9 1.2 %add.33 = f32[4,512,128]{2,1,0:T(8,128)} add(f32[4,512,128]{2,1,0:T(8,128)S(1)} %dressed_own.1, f32[4,512,128]{2,1,0:T(8,128)S(1)} %collective-permute-done.7) | non-fusion elementwise | flops 262144 | bytes 3145728 | tf_op jit(solution)/shard_map/add | solution.py:183
  65.1 3.9 %all-to-all-start.1 = ((f32[4,512,128]{2,1,0:T(8,128)}), f32[4,512,128]{2,1,0:T(8,128)S(1)}, u32[]{:S(2)}, u32[]{:S(2)}) async-start(f32[4,512,128]{2,1,0:T(8,128)} %add.33), calls=%async_computation.1 | async-start | bytes 2097152 | tf_op jit(solution)/shard_map/all_to_all | solution.py:183
  69.0 0.0 copy-done.8
  69.0 0.1 copy.13
  69.1 0.6 reshape.15.refs_2_
  69.7 4.6 %all-gather.2.cloned.1.call-done.refs_4_ = f32[32,512,128]{2,1,0:T(8,128)} async-done(((f32[2,512,128]{2,1,0:T(8,128)}), f32[32,512,128]{2,1,0:T(8,128)}) %all-gather.2.cloned.1.call-update) | async-done | bytes 8388624 | tf_op jit(solution)/shard_map/all_gather | solution.py:144
  74.3 0.0 copy-start.7
  74.3 0.0 copy-start.9
  74.3 4.5 %integral.1 = f32[512,128]{1,0:T(8,128)} custom-call(s32[128]{0:T(128)} %refs_0_.2, s32[32]{0:T(128)} %refs_1_.1, s32[16]{0:T(128)} %reshape.15.refs_2_, f32[8,64,512]{2,1,0:T(8,128)} %bitcast.8, f32[32,512,128]{2,1,0:T(8,128)} %all-gather.2.cloned.1.call-done.refs_4_), custom_call_target="tpu_custom_call" | custom-call | tf_op jit(solution)/shard_map/integral/pallas_call | solution.py:185
  78.8 4.7 %all-to-all-done.1 = f32[4,512,128]{2,1,0:T(8,128)S(1)} async-done(((f32[4,512,128]{2,1,0:T(8,128)}), f32[4,512,128]{2,1,0:T(8,128)S(1)}, u32[]{:S(2)}, u32[]{:S(2)}) %all-to-all-start.1) | async-done | bytes 1048608 | tf_op jit(solution)/shard_map/all_to_all | solution.py:183
  83.6 0.0 copy-done.7
  83.6 0.0 copy-done.9
  83.6 1.8 %divide_subtract_fusion = (f32[512,128]{1,0:T(8,128)}, f32[512,128]{1,0:T(8,128)}) fusion(f32[512,128]{1,0:T(8,128)S(1)} %copy-done, f32[128]{0:T(128)S(1)} %copy-done.9, f32[512]{0:T(512)S(1)} %copy-done.7, f32[512,128]{1,0:T(8,128)} %integral.1, f32[4,512,128]{2,1,0:T(8,128)S(1)} %all-to-all-done.1), kind=kLoop, calls=%fused_computation.5 | loop fusion | flops 458752 | bytes 2099712 | tf_op jit(solution)/shard_map/sub | solution.py:200
Async XLA Ops:
  7.2 67.1 %all-gather.2.cloned.1.call-start = ((), (), s32[]{:S(2)}) async-start(), calls=%async_computation.2 | async-start | bytes 8912896 | tf_op jit(solution)/shard_map/all_gather | solution.py:144
  7.9 5.0 %copy-start = (f32[512,128]{1,0:T(8,128)S(1)}, f32[512,128]{1,0:T(8,128)}, u32[]{:S(2)}) copy-start(f32[512,128]{1,0:T(8,128)} %refs_0_.3) | copy-start | bytes 786436
  7.9 48.7 %all-to-all-start = ((f32[4,1024,128]{2,1,0:T(8,128)}), f32[4,1024,128]{2,1,0:T(8,128)S(1)}, u32[]{:S(2)}, u32[]{:S(2)}) async-start(f32[4,1024,128]{2,1,0:T(8,128)} %bitcast.7), calls=%async_computation | async-start | bytes 4194304 | tf_op jit(solution)/shard_map/all_to_all | solution.py:151
  12.9 12.6 %collective-permute-start.3 = (f32[512,128]{1,0:T(8,128)S(1)}, f32[512,128]{1,0:T(8,128)S(1)}, u32[]{:S(2)}, u32[]{:S(2)}) collective-permute-start(f32[512,128]{1,0:T(8,128)S(1)} %copy-done), channel_id=1, source_target_pairs={{32,1},{33,2},{34,3},{35,4},{36,5},{37,6},{38,7},{39,0},{0,39},{1,... | collective-permute-start | bytes 786440 | tf_op jit(solution)/shard_map/ppermute | solution.py:132
  17.7 17.1 %collective-permute-start = (f32[512,128]{1,0:T(8,128)S(1)}, f32[512,128]{1,0:T(8,128)S(1)}, u32[]{:S(2)}, u32[]{:S(2)}) collective-permute-start(f32[512,128]{1,0:T(8,128)S(1)} %copy-done), channel_id=1, source_target_pairs={{0,1},{1,2},{2,3},{3,4},{4,5},{5,6},{6,7},{7,0},{32,39},{33,32},{3... | collective-permute-start | bytes 786440 | tf_op jit(solution)/shard_map/ppermute | solution.py:132
  25.5 11.9 %collective-permute-start.4 = (f32[512,128]{1,0:T(8,128)S(1)}, f32[512,128]{1,0:T(8,128)S(1)}, u32[]{:S(2)}, u32[]{:S(2)}) collective-permute-start(f32[512,128]{1,0:T(8,128)S(1)} %collective-permute-done.3.refs_0_), channel_id=1, source_target_pairs={{0,1},{1,2},{2,3},{3,4},{4,5},{5,6},{6,7},{7,0},{32,39},{33,32},{3... | collective-permute-start | bytes 786440 | tf_op jit(solution)/shard_map/ppermute | solution.py:132
  34.2 0.7 copy-start.1
  34.9 8.7 %collective-permute-start.1 = (f32[512,128]{1,0:T(8,128)S(1)}, f32[512,128]{1,0:T(8,128)S(1)}, u32[]{:S(2)}, u32[]{:S(2)}) collective-permute-start(f32[512,128]{1,0:T(8,128)S(1)} %collective-permute-done.refs_1_), channel_id=1, source_target_pairs={{0,1},{1,2},{2,3},{3,4},{4,5},{5,6},{6,7},{7,0},{32,39},{33,32},{3... | collective-permute-start | bytes 786440 | tf_op jit(solution)/shard_map/ppermute | solution.py:132
  37.4 10.2 %collective-permute-start.5 = (f32[512,128]{1,0:T(8,128)S(1)}, f32[512,128]{1,0:T(8,128)S(1)}, u32[]{:S(2)}, u32[]{:S(2)}) collective-permute-start(f32[512,128]{1,0:T(8,128)S(1)} %collective-permute-done.4.refs_1_), channel_id=1, source_target_pairs={{0,1},{1,2},{2,3},{3,4},{4,5},{5,6},{6,7},{7,0},{32,39},{33,32},{3... | collective-permute-start | bytes 786440 | tf_op jit(solution)/shard_map/ppermute | solution.py:132
  42.9 0.7 copy-start.3
  43.6 9.4 %collective-permute-start.6 = (f32[512,128]{1,0:T(8,128)S(1)}, f32[512,128]{1,0:T(8,128)S(1)}, u32[]{:S(2)}, u32[]{:S(2)}) collective-permute-start(f32[512,128]{1,0:T(8,128)S(1)} %collective-permute-done.1.refs_2_), channel_id=1, source_target_pairs={{0,2},{1,3},{2,4},{3,5},{4,6},{5,7},{6,0},{7,1},{32,38},{33,39},{3... | collective-permute-start | bytes 786440 | tf_op jit(solution)/shard_map/ppermute | solution.py:132
  45.5 11.1 %collective-permute-start.2 = (f32[512,128]{1,0:T(8,128)S(1)}, f32[512,128]{1,0:T(8,128)S(1)}, u32[]{:S(2)}, u32[]{:S(2)}) collective-permute-start(f32[512,128]{1,0:T(8,128)S(1)} %collective-permute-done.1.refs_2_), channel_id=1, source_target_pairs={{0,1},{1,2},{2,3},{3,4},{4,5},{5,6},{6,7},{7,0},{32,39},{33,32},{3... | collective-permute-start | bytes 786440 | tf_op jit(solution)/shard_map/ppermute | solution.py:132
  47.6 0.7 copy-start.5
  56.6 1.0 %copy-start.2 = (f32[512,128]{1,0:T(8,128)S(1)}, f32[512,128]{1,0:T(8,128)}, u32[]{:S(2)}) copy-start(f32[512,128]{1,0:T(8,128)} %copy-done.1) | copy-start | bytes 786436
  56.6 1.0 %copy-start.4 = (f32[512,128]{1,0:T(8,128)S(1)}, f32[512,128]{1,0:T(8,128)}, u32[]{:S(2)}) copy-start(f32[512,128]{1,0:T(8,128)} %copy-done.3) | copy-start | bytes 786436
  56.6 1.1 %copy-start.6 = (f32[512,128]{1,0:T(8,128)S(1)}, f32[512,128]{1,0:T(8,128)}, u32[]{:S(2)}) copy-start(f32[512,128]{1,0:T(8,128)} %copy-done.5) | copy-start | bytes 786436
  59.3 4.6 %collective-permute-start.7 = (f32[4,512,128]{2,1,0:T(8,128)S(1)}, f32[4,512,128]{2,1,0:T(8,128)S(1)}, u32[]{:S(2)}, u32[]{:S(2)}) collective-permute-start(f32[4,512,128]{2,1,0:T(8,128)S(1)} %dressed_other.1), channel_id=1, source_target_pairs={{0,32},{32,0},{1,33},{33,1},{2,34},{34,2},{3,35},{35,3},{4,36},{36... | collective-permute-start | bytes 3145736 | tf_op jit(solution)/shard_map/ppermute | solution.py:135
  63.8 5.2 %copy-start.8 = (s32[8,2]{0,1:T(2,128)S(1)}, s32[8,2]{0,1:T(2,128)}, u32[]{:S(2)}) copy-start(s32[8,2]{0,1:T(2,128)} %param.15) | copy-start | bytes 196
  65.1 18.5 %all-to-all-start.1 = ((f32[4,512,128]{2,1,0:T(8,128)}), f32[4,512,128]{2,1,0:T(8,128)S(1)}, u32[]{:S(2)}, u32[]{:S(2)}) async-start(f32[4,512,128]{2,1,0:T(8,128)} %add.33), calls=%async_computation.1 | async-start | bytes 2097152 | tf_op jit(solution)/shard_map/all_to_all | solution.py:183
  74.3 9.3 %copy-start.7 = (f32[512]{0:T(512)S(1)}, f32[512]{0:T(512)}, u32[]{:S(2)}) copy-start(f32[512]{0:T(512)} %param.16) | copy-start | bytes 6148
  74.3 9.3 %copy-start.9 = (f32[128]{0:T(128)S(1)}, f32[128]{0:T(128)}, u32[]{:S(2)}) copy-start(f32[128]{0:T(128)} %param.17) | copy-start | bytes 1540
Sparse Core Ops, SparseCore 0:
  10.1 64.1 all-gather.1

commit v4 on v3

--- a/solution.py
+++ b/solution.py
@@ -162,7 +162,7 @@
         name="dressing_ready",
     )(panels)
 
-    def product(pieces, first, name):
+    def product(pieces, first, name, cost):
         count = len(pieces)
         return pl.pallas_call(
             lambda *refs: product_kernel(first, *refs),
@@ -174,12 +174,12 @@
             + [pltpu.VMEM((rows, count * width), bf16)] * 2
             + [sem((count + 2,))],
             compiler_params=PARAMS,
+            cost_estimate=pl.CostEstimate(flops=int(1e10) if 'own' in name else 1000, bytes_accessed=1000000, transcendentals=0),
             name=name,
         )(*pieces, high, low)
 
-    amp_same[-1], amp_cross[-1], amp_far = lax.optimization_barrier((amp_same[-1], amp_cross[-1], amp_far))
-    other = swap(product(amp_cross, 1, "dressed_other"))
-    own = product([amplitudes, *amp_same, amp_far], 0, "dressed_own")
+    other = swap(product(amp_cross, 1, "dressed_other", 1))
+    own = product([amplitudes, *amp_same, amp_far], 0, "dressed_own", 60 * 1024 * 1024)
     sums = lax.all_to_all(own + other, "x", 0, 0)
 
     integral = pl.pallas_call(

time: 93 us -> 88.5 us (0.952)
  waiting for transfers between devices: 19 us -> 15.5 us
  local copies, waits for them, and re-layouts: 3.49 us -> 0.69 us
  starting transfers between devices: 43.8 us -> 44.9 us
    all_to_all x1, waiting for transfers between devices: 4.73 us -> 0.01 us  [shards(): sums = lax.all_to_all(own + other, 'x', 0, 0)]
    all_gather x1, waiting for transfers between devices: 4.57 us -> 8.88 us  [shards(): gathered = lax.all_gather(blocks, ('y', 'core'), axis=0, tiled=True)]
    ppermute x7, waiting for transfers between devices: 8.98 us -> 5.96 us  [ring(): return lax.ppermute(value, names, pairs_of)]
    unnamed x21 -> x9, local copies, waits for them, and re-layouts: 2.9 us -> 0.1 us
  transfers between devices with their start and end apart: 11 -> 11, of which waited for: 6 -> 4; matrix products, arithmetic and copies ran while one was open for 2% -> 2% of each run, Pallas kernels for 9% -> 10%
where the time goes in v4:
time: 88.5 us; the launch traced here: 87.5 us
  starting transfers between devices  44.9 us (51%)
  waiting for transfers between devices  15.5 us (18%)
  between operations  14.2 us (16%)
  Pallas kernels  9.16 us (10%)
  other arithmetic  3 us (3%)
    ppermute x7, starting transfers between devices, ring(): return lax.ppermute(value, names, pairs_of)  33.3 us
    all_gather x1, waiting for transfers between devices, shards(): gathered = lax.all_gather(blocks, ('y', 'core'), axis=0, tiled=True)  8.88 us
    ppermute x7, waiting for transfers between devices, ring(): return lax.ppermute(value, names, pairs_of)  5.96 us
    all_to_all x1, starting transfers between devices, shards(): panels = lax.all_to_all(dressing.reshape(nx, depth, width), 'x', 0, 0)  4.99 us
    pallas_call x1, Pallas kernels, shards(): pl.pallas_call(lambda *refs: integral_kernel(pairs, *refs), out_shape=jax...  4.53 us
    pallas_call x2, Pallas kernels, product(): pl.pallas_call(lambda *refs: product_kernel(first, *refs), out_shape=shap...  4.24 us
    all_to_all x1, starting transfers between devices, shards(): sums = lax.all_to_all(own + other, 'x', 0, 0)  4 us
    ppermute x1, starting transfers between devices, swap(): return lax.ppermute(value, 'core', [(0, 1), (1, 0)])  2.63 us
  transfers between devices with their start and end apart: 11, of which 4 were waited for; matrix products, arithmetic and copies ran while one was open for 2% of the time, Pallas kernels for 10%

profile of v4, /device:TPU:1, one launch (start us, length us, event | category | flops | bytes accessed | tf_op | source)
XLA Modules:
  0.0 87.5 jit_solution(17723473250987493864)
XLA Ops:
  7.2 0.0 all-gather.2.cloned.1.call-start
  7.2 0.7 all-gather.2.cloned.1.call-update
  7.9 0.0 copy-start
  7.9 5.0 %all-to-all-start = ((f32[4,1024,128]{2,1,0:T(8,128)}), f32[4,1024,128]{2,1,0:T(8,128)S(1)}, u32[]{:S(2)}, u32[]{:S(2)}) async-start(f32[4,1024,128]{2,1,0:T(8,128)} %bitcast.7), calls=%async_computation | async-start | bytes 4194304 | tf_op jit(solution)/shard_map/all_to_all | solution.py:151
  12.9 0.0 copy-done
  12.9 4.8 %collective-permute-start.4 = (f32[512,128]{1,0:T(8,128)S(1)}, f32[512,128]{1,0:T(8,128)S(1)}, u32[]{:S(2)}, u32[]{:S(2)}) collective-permute-start(f32[512,128]{1,0:T(8,128)S(1)} %copy-done), channel_id=1, source_target_pairs={{32,1},{33,2},{34,3},{35,4},{36,5},{37,6},{38,7},{39,0},{0,39},{1,... | collective-permute-start | bytes 786440 | tf_op jit(solution)/shard_map/ppermute | solution.py:132
  17.7 7.7 %collective-permute-start = (f32[512,128]{1,0:T(8,128)S(1)}, f32[512,128]{1,0:T(8,128)S(1)}, u32[]{:S(2)}, u32[]{:S(2)}) collective-permute-start(f32[512,128]{1,0:T(8,128)S(1)} %copy-done), channel_id=1, source_target_pairs={{0,1},{1,2},{2,3},{3,4},{4,5},{5,6},{6,7},{7,0},{32,39},{33,32},{3... | collective-permute-start | bytes 786440 | tf_op jit(solution)/shard_map/ppermute | solution.py:132
  25.5 0.0 collective-permute-done.4.refs_0_
  25.5 8.6 %collective-permute-start.5 = (f32[512,128]{1,0:T(8,128)S(1)}, f32[512,128]{1,0:T(8,128)S(1)}, u32[]{:S(2)}, u32[]{:S(2)}) collective-permute-start(f32[512,128]{1,0:T(8,128)S(1)} %collective-permute-done.4.refs_0_), channel_id=1, source_target_pairs={{0,1},{1,2},{2,3},{3,4},{4,5},{5,6},{6,7},{7,0},{32,39},{33,32},{3... | collective-permute-start | bytes 786440 | tf_op jit(solution)/shard_map/ppermute | solution.py:132
  34.2 0.0 collective-permute-done.refs_1_
  34.2 1.9 %collective-permute-start.1 = (f32[512,128]{1,0:T(8,128)S(1)}, f32[512,128]{1,0:T(8,128)}, u32[]{:S(2)}, u32[]{:S(2)}) collective-permute-start(f32[512,128]{1,0:T(8,128)S(1)} %collective-permute-done.refs_1_), channel_id=1, source_target_pairs={{0,1},{1,2},{2,3},{3,4},{4,5},{5,6},{6,7},{7,0},{32,39},{33,32},{3... | collective-permute-start | bytes 786440 | tf_op jit(solution)/shard_map/ppermute | solution.py:132
  36.1 1.4 %collective-permute-done.5.refs_1_ = f32[512,128]{1,0:T(8,128)S(1)} collective-permute-done((f32[512,128]{1,0:T(8,128)S(1)}, f32[512,128]{1,0:T(8,128)S(1)}, u32[]{:S(2)}, u32[]{:S(2)}) %collective-permute-start.5) | collective-permute-done | bytes 262176 | tf_op jit(solution)/shard_map/ppermute | solution.py:132
  37.4 5.4 %collective-permute-start.6 = (f32[512,128]{1,0:T(8,128)S(1)}, f32[512,128]{1,0:T(8,128)S(1)}, u32[]{:S(2)}, u32[]{:S(2)}) collective-permute-start(f32[512,128]{1,0:T(8,128)S(1)} %collective-permute-done.5.refs_1_), channel_id=1, source_target_pairs={{0,1},{1,2},{2,3},{3,4},{4,5},{5,6},{6,7},{7,0},{32,39},{33,32},{3... | collective-permute-start | bytes 786440 | tf_op jit(solution)/shard_map/ppermute | solution.py:132
  42.9 0.0 collective-permute-done.1.refs_2_
  42.9 1.9 %collective-permute-start.3 = (f32[512,128]{1,0:T(8,128)}, f32[512,128]{1,0:T(8,128)}, u32[]{:S(2)}, u32[]{:S(2)}) collective-permute-start(f32[512,128]{1,0:T(8,128)} %collective-permute-done.1.refs_2_), channel_id=1, source_target_pairs={{0,2},{1,3},{2,4},{3,5},{4,6},{5,7},{6,0},{7,1},{32,38},{33,39},{3... | collective-permute-start | bytes 786440 | tf_op jit(solution)/shard_map/ppermute | solution.py:132
  44.8 2.8 %collective-permute-start.2 = (f32[512,128]{1,0:T(8,128)}, f32[512,128]{1,0:T(8,128)}, u32[]{:S(2)}, u32[]{:S(2)}) collective-permute-start(f32[512,128]{1,0:T(8,128)} %collective-permute-done.1.refs_2_), channel_id=1, source_target_pairs={{0,1},{1,2},{2,3},{3,4},{4,5},{5,6},{6,7},{7,0},{32,39},{33,32},{3... | collective-permute-start | bytes 786440 | tf_op jit(solution)/shard_map/ppermute | solution.py:132
  47.6 0.0 all-to-all-done.refs_0_
  47.6 0.4 dressing_ready.1
  48.0 0.0 collective-permute-done.6.refs_2_
  48.0 1.6 %dressed_other.1 = f32[4,512,128]{2,1,0:T(8,128)S(1)} custom-call(f32[512,128]{1,0:T(8,128)S(1)} %collective-permute-done.4.refs_0_, f32[512,128]{1,0:T(8,128)S(1)} %collective-permute-done.5.refs_1_, f32[512,128]{1,0:T(8,128)S(1)} %collective-permute-done.6.refs_2_, bf16[640,512]{1,0:T(8,128)(2,1)S(1)} %get-tuple-element.4.refs_5_.refs_3_, ...), custom_call_target="tpu_custom_call" | custom-call | flops 1000 | bytes 1000000 | tf_op jit(solution)/shard_map/dressed_other/pallas_call | solution.py:167
  49.6 2.6 %collective-permute-start.7 = (f32[4,512,128]{2,1,0:T(8,128)S(1)}, f32[4,512,128]{2,1,0:T(8,128)S(1)}, u32[]{:S(2)}, u32[]{:S(2)}) collective-permute-start(f32[4,512,128]{2,1,0:T(8,128)S(1)} %dressed_other.1), channel_id=1, source_target_pairs={{0,32},{32,0},{1,33},{33,1},{2,34},{34,2},{3,35},{35,3},{4,36},{36... | collective-permute-start | bytes 3145736 | tf_op jit(solution)/shard_map/ppermute | solution.py:135
  52.3 1.0 %collective-permute-done.3.refs_4_ = f32[512,128]{1,0:T(8,128)} collective-permute-done((f32[512,128]{1,0:T(8,128)}, f32[512,128]{1,0:T(8,128)}, u32[]{:S(2)}, u32[]{:S(2)}) %collective-permute-start.3) | collective-permute-done | bytes 262176 | tf_op jit(solution)/shard_map/ppermute | solution.py:132
  53.3 3.6 %collective-permute-done.2.refs_3_ = f32[512,128]{1,0:T(8,128)} collective-permute-done((f32[512,128]{1,0:T(8,128)}, f32[512,128]{1,0:T(8,128)}, u32[]{:S(2)}, u32[]{:S(2)}) %collective-permute-start.2) | collective-permute-done | bytes 262176 | tf_op jit(solution)/shard_map/ppermute | solution.py:132
  56.9 2.6 %dressed_own.1 = f32[4,512,128]{2,1,0:T(8,128)S(1)} custom-call(f32[512,128]{1,0:T(8,128)S(1)} %copy-done, f32[512,128]{1,0:T(8,128)S(1)} %collective-permute-done.refs_1_, f32[512,128]{1,0:T(8,128)} %collective-permute-done.1.refs_2_, f32[512,128]{1,0:T(8,128)} %collective-permute-done.2.refs_3_, f32[512,128]{1,0:T(8,128)} %collective-permute-done.3.refs_4_, ...), custom_call_target="tpu_custom_call" | custom-call | flops 10000000000 | bytes 1000000 | tf_op jit(solution)/shard_map/dressed_own/pallas_call | solution.py:167
  59.5 0.0 copy-start.2
  59.5 0.0 collective-permute-done.7
  59.5 1.2 %add.33 = f32[4,512,128]{2,1,0:T(8,128)} add(f32[4,512,128]{2,1,0:T(8,128)S(1)} %dressed_own.1, f32[4,512,128]{2,1,0:T(8,128)S(1)} %collective-permute-done.7) | non-fusion elementwise | flops 262144 | bytes 3145728 | tf_op jit(solution)/shard_map/add | solution.py:183
  60.7 4.0 %all-to-all-start.1 = ((f32[4,512,128]{2,1,0:T(8,128)}), f32[4,512,128]{2,1,0:T(8,128)S(1)}, u32[]{:S(2)}, u32[]{:S(2)}) async-start(f32[4,512,128]{2,1,0:T(8,128)} %add.33), calls=%async_computation.1 | async-start | bytes 2097152 | tf_op jit(solution)/shard_map/all_to_all | solution.py:183
  64.7 0.0 copy-done.2
  64.7 0.1 copy.13
  64.8 0.6 reshape.15.refs_2_
  65.4 8.9 %all-gather.2.cloned.1.call-done.refs_4_ = f32[32,512,128]{2,1,0:T(8,128)} async-done(((f32[2,512,128]{2,1,0:T(8,128)}), f32[32,512,128]{2,1,0:T(8,128)}) %all-gather.2.cloned.1.call-update) | async-done | bytes 8388624 | tf_op jit(solution)/shard_map/all_gather | solution.py:144
  74.3 0.0 copy-start.1
  74.3 0.0 copy-start.3
  74.3 4.5 %integral.1 = f32[512,128]{1,0:T(8,128)} custom-call(s32[128]{0:T(128)} %refs_0_.2, s32[32]{0:T(128)} %refs_1_.1, s32[16]{0:T(128)} %reshape.15.refs_2_, f32[8,64,512]{2,1,0:T(8,128)} %bitcast.8, f32[32,512,128]{2,1,0:T(8,128)} %all-gather.2.cloned.1.call-done.refs_4_), custom_call_target="tpu_custom_call" | custom-call | tf_op jit(solution)/shard_map/integral/pallas_call | solution.py:185
  78.8 0.0 all-to-all-done.1
  78.8 0.0 copy-done.1
  78.8 0.0 copy-done.3
  78.9 1.8 %divide_subtract_fusion = (f32[512,128]{1,0:T(8,128)}, f32[512,128]{1,0:T(8,128)}) fusion(f32[512,128]{1,0:T(8,128)S(1)} %copy-done, f32[128]{0:T(128)S(1)} %copy-done.3, f32[512]{0:T(512)S(1)} %copy-done.1, f32[512,128]{1,0:T(8,128)} %integral.1, f32[4,512,128]{2,1,0:T(8,128)S(1)} %all-to-all-done.1), kind=kLoop, calls=%fused_computation.5 | loop fusion | flops 458752 | bytes 2099712 | tf_op jit(solution)/shard_map/sub | solution.py:200
Async XLA Ops:
  7.2 67.1 %all-gather.2.cloned.1.call-start = ((), (), s32[]{:S(2)}) async-start(), calls=%async_computation.2 | async-start | bytes 8912896 | tf_op jit(solution)/shard_map/all_gather | solution.py:144
  7.9 5.0 %copy-start = (f32[512,128]{1,0:T(8,128)S(1)}, f32[512,128]{1,0:T(8,128)}, u32[]{:S(2)}) copy-start(f32[512,128]{1,0:T(8,128)} %refs_0_.3) | copy-start | bytes 786436
  7.9 39.7 %all-to-all-start = ((f32[4,1024,128]{2,1,0:T(8,128)}), f32[4,1024,128]{2,1,0:T(8,128)S(1)}, u32[]{:S(2)}, u32[]{:S(2)}) async-start(f32[4,1024,128]{2,1,0:T(8,128)} %bitcast.7), calls=%async_computation | async-start | bytes 4194304 | tf_op jit(solution)/shard_map/all_to_all | solution.py:151
  12.9 12.6 %collective-permute-start.4 = (f32[512,128]{1,0:T(8,128)S(1)}, f32[512,128]{1,0:T(8,128)S(1)}, u32[]{:S(2)}, u32[]{:S(2)}) collective-permute-start(f32[512,128]{1,0:T(8,128)S(1)} %copy-done), channel_id=1, source_target_pairs={{32,1},{33,2},{34,3},{35,4},{36,5},{37,6},{38,7},{39,0},{0,39},{1,... | collective-permute-start | bytes 786440 | tf_op jit(solution)/shard_map/ppermute | solution.py:132
  17.7 16.4 %collective-permute-start = (f32[512,128]{1,0:T(8,128)S(1)}, f32[512,128]{1,0:T(8,128)S(1)}, u32[]{:S(2)}, u32[]{:S(2)}) collective-permute-start(f32[512,128]{1,0:T(8,128)S(1)} %copy-done), channel_id=1, source_target_pairs={{0,1},{1,2},{2,3},{3,4},{4,5},{5,6},{6,7},{7,0},{32,39},{33,32},{3... | collective-permute-start | bytes 786440 | tf_op jit(solution)/shard_map/ppermute | solution.py:132
  25.5 11.9 %collective-permute-start.5 = (f32[512,128]{1,0:T(8,128)S(1)}, f32[512,128]{1,0:T(8,128)S(1)}, u32[]{:S(2)}, u32[]{:S(2)}) collective-permute-start(f32[512,128]{1,0:T(8,128)S(1)} %collective-permute-done.4.refs_0_), channel_id=1, source_target_pairs={{0,1},{1,2},{2,3},{3,4},{4,5},{5,6},{6,7},{7,0},{32,39},{33,32},{3... | collective-permute-start | bytes 786440 | tf_op jit(solution)/shard_map/ppermute | solution.py:132
  34.2 8.7 %collective-permute-start.1 = (f32[512,128]{1,0:T(8,128)S(1)}, f32[512,128]{1,0:T(8,128)}, u32[]{:S(2)}, u32[]{:S(2)}) collective-permute-start(f32[512,128]{1,0:T(8,128)S(1)} %collective-permute-done.refs_1_), channel_id=1, source_target_pairs={{0,1},{1,2},{2,3},{3,4},{4,5},{5,6},{6,7},{7,0},{32,39},{33,32},{3... | collective-permute-start | bytes 786440 | tf_op jit(solution)/shard_map/ppermute | solution.py:132
  37.4 10.6 %collective-permute-start.6 = (f32[512,128]{1,0:T(8,128)S(1)}, f32[512,128]{1,0:T(8,128)S(1)}, u32[]{:S(2)}, u32[]{:S(2)}) collective-permute-start(f32[512,128]{1,0:T(8,128)S(1)} %collective-permute-done.5.refs_1_), channel_id=1, source_target_pairs={{0,1},{1,2},{2,3},{3,4},{4,5},{5,6},{6,7},{7,0},{32,39},{33,32},{3... | collective-permute-start | bytes 786440 | tf_op jit(solution)/shard_map/ppermute | solution.py:132
  42.9 10.4 %collective-permute-start.3 = (f32[512,128]{1,0:T(8,128)}, f32[512,128]{1,0:T(8,128)}, u32[]{:S(2)}, u32[]{:S(2)}) collective-permute-start(f32[512,128]{1,0:T(8,128)} %collective-permute-done.1.refs_2_), channel_id=1, source_target_pairs={{0,2},{1,3},{2,4},{3,5},{4,6},{5,7},{6,0},{7,1},{32,38},{33,39},{3... | collective-permute-start | bytes 786440 | tf_op jit(solution)/shard_map/ppermute | solution.py:132
  44.8 12.1 %collective-permute-start.2 = (f32[512,128]{1,0:T(8,128)}, f32[512,128]{1,0:T(8,128)}, u32[]{:S(2)}, u32[]{:S(2)}) collective-permute-start(f32[512,128]{1,0:T(8,128)} %collective-permute-done.1.refs_2_), channel_id=1, source_target_pairs={{0,1},{1,2},{2,3},{3,4},{4,5},{5,6},{6,7},{7,0},{32,39},{33,32},{3... | collective-permute-start | bytes 786440 | tf_op jit(solution)/shard_map/ppermute | solution.py:132
  49.6 9.9 %collective-permute-start.7 = (f32[4,512,128]{2,1,0:T(8,128)S(1)}, f32[4,512,128]{2,1,0:T(8,128)S(1)}, u32[]{:S(2)}, u32[]{:S(2)}) collective-permute-start(f32[4,512,128]{2,1,0:T(8,128)S(1)} %dressed_other.1), channel_id=1, source_target_pairs={{0,32},{32,0},{1,33},{33,1},{2,34},{34,2},{3,35},{35,3},{4,36},{36... | collective-permute-start | bytes 3145736 | tf_op jit(solution)/shard_map/ppermute | solution.py:135
  59.5 5.2 %copy-start.2 = (s32[8,2]{0,1:T(2,128)S(1)}, s32[8,2]{0,1:T(2,128)}, u32[]{:S(2)}) copy-start(s32[8,2]{0,1:T(2,128)} %param.15) | copy-start | bytes 196
  60.7 18.1 %all-to-all-start.1 = ((f32[4,512,128]{2,1,0:T(8,128)}), f32[4,512,128]{2,1,0:T(8,128)S(1)}, u32[]{:S(2)}, u32[]{:S(2)}) async-start(f32[4,512,128]{2,1,0:T(8,128)} %add.33), calls=%async_computation.1 | async-start | bytes 2097152 | tf_op jit(solution)/shard_map/all_to_all | solution.py:183
  74.3 4.6 %copy-start.1 = (f32[512]{0:T(512)S(1)}, f32[512]{0:T(512)}, u32[]{:S(2)}) copy-start(f32[512]{0:T(512)} %param.16) | copy-start | bytes 6148
  74.3 4.6 %copy-start.3 = (f32[128]{0:T(128)S(1)}, f32[128]{0:T(128)}, u32[]{:S(2)}) copy-start(f32[128]{0:T(128)} %param.17) | copy-start | bytes 1540
Sparse Core Ops, SparseCore 0:
  10.1 64.1 all-gather.1

commit v5 on v4

--- a/solution.py
+++ b/solution.py
@@ -11,6 +11,9 @@
 HBM = pl.BlockSpec(memory_space=pltpu.HBM)
 VMEM = pl.BlockSpec(memory_space=pltpu.VMEM)
 SMEM = pl.BlockSpec(memory_space=pltpu.SMEM)
+OTHER = 1000
+EARLY = 30000000000
+LATE = 1000
 FAR = 4
 
 
@@ -61,14 +64,15 @@
             out[s + k] = value if plus is None else value + plus(s + k)
 
 
-def product_kernel(first, *refs):
-    count = len(refs) - 9
-    pieces, refs = refs[:count], refs[count:]
-    high, low, out, held, right_high, right_low, left_high, left_low, sems = refs
+def product_kernel(first, count, added, *refs):
+    pieces, high, low, refs = refs[:count], refs[count], refs[count + 1], refs[count + 2 :]
+    earlier, refs = refs[:added], refs[added:]
+    out, held, right_high, right_low, left_high, left_low, sems = refs[:7]
     width = held.shape[2]
     rows = pl.ds(first * width, count * width)
     copies = [(piece, held.at[k]) for k, piece in enumerate(pieces)]
     copies += [(high.at[rows], right_high), (low.at[rows], right_low)]
+    copies += [(ref, refs[7].at[k]) for k, ref in enumerate(earlier)]
     made = start_all(copies, sems)
     for k in range(count):
         made[k].wait()
@@ -76,33 +80,35 @@
         left_high[:, at], left_low[:, at] = split(held[k])
     for copy in made[count:]:
         copy.wait()
-    products(out, (left_high[...], left_low[...]), (right_high, right_low))
-
-
-def integral_kernel(pairs, pair_block, block_home, mask, factor, gathered, out, factors, blocks, sems, block_sems):
-    y, core = lax.axis_index("y"), lax.axis_index("core")
-    fetched = []
-    for i in range(pairs):
-        home = block_home[pair_block[(y * 2 + core) * pairs + i]]
-        fetched.append(
-            (
-                pltpu.make_async_copy(factor.at[i], factors.at[i], sems.at[i]),
-                pltpu.make_async_copy(gathered.at[home], blocks.at[i], block_sems.at[i]),
-            )
-        )
-        for copy in fetched[-1]:
-            copy.start()
-    tile = factors.shape[1]
+    plus = (lambda s: refs[7][0, s] + refs[7][1, s]) if added else None
+    products(out, (left_high[...], left_low[...]), (right_high, right_low), plus)
+
+
+def factor_kernel(factor, stacked):
+    tile = factor.shape[1]
+    for i in range(factor.shape[0]):
+        high, low = split(factor[i])
+        stacked[i, :tile] = high
+        stacked[i, tile:] = low
+
+
+def block_at(gathered, home):
+    return gathered.at[home]
+
+
+def integral_kernel(pairs, where, stacked, gathered, out, factors, blocks, sems):
+    made = start_all(
+        [(block_at(gathered, where[i]), blocks.at[i]) for i in range(pairs)] + [(stacked, factors)], sems
+    )
+    for copy in made:
+        copy.wait()
+    tile = factors.shape[1] // 2
     width = out.shape[1]
     lane = lax.broadcasted_iota(jnp.int32, (tile, width), 1)
     for i in range(pairs):
-        for copy in fetched[i]:
-            copy.wait()
-        factor_high, factor_low = split(factors[i])
-        high, low = split(blocks[i])
-        both = jnp.dot(jnp.concatenate([factor_high, factor_low], axis=0), high, preferred_element_type=F32)
-        integral = both[:tile] + (both[tile:] + jnp.dot(factor_high, low, preferred_element_type=F32))
-        on = jnp.where(lane < tile, mask[2 * i], mask[2 * i + 1]).astype(F32)
+        both = jnp.dot(factors[i], jnp.concatenate(split(blocks[i]), axis=1), preferred_element_type=F32)
+        integral = both[:tile, :width] + (both[tile:, :width] + both[:tile, width:])
+        on = jnp.where(lane < tile, where[pairs + 2 * i], where[pairs + 2 * i + 1]).astype(F32)
         out[i * tile : (i + 1) * tile] = integral * on
 
 
@@ -162,40 +168,54 @@
         name="dressing_ready",
     )(panels)
 
-    def product(pieces, first, name, cost):
-        count = len(pieces)
+    def product(pieces, first, name, flops, *earlier):
+        count, added = len(pieces), len(earlier)
         return pl.pallas_call(
-            lambda *refs: product_kernel(first, *refs),
+            lambda *refs: product_kernel(first, count, added, *refs),
             out_shape=shape,
-            in_specs=[HBM] * (count + 2),
+            in_specs=[HBM] * (count + 2 + added),
             out_specs=VMEM,
             scratch_shapes=[pltpu.VMEM((count, rows, width), F32)]
             + [pltpu.VMEM((count * width, nx * width), bf16)] * 2
             + [pltpu.VMEM((rows, count * width), bf16)] * 2
-            + [sem((count + 2,))],
+            + [sem((count + 2 + added,))]
+            + ([pltpu.VMEM((added, nx, rows, width), F32)] if added else []),
             compiler_params=PARAMS,
-            cost_estimate=pl.CostEstimate(flops=int(1e10) if 'own' in name else 1000, bytes_accessed=1000000, transcendentals=0),
+            cost_estimate=pl.CostEstimate(flops=flops, bytes_accessed=1000000, transcendentals=0),
             name=name,
-        )(*pieces, high, low)
-
-    other = swap(product(amp_cross, 1, "dressed_other", 1))
-    own = product([amplitudes, *amp_same, amp_far], 0, "dressed_own", 60 * 1024 * 1024)
-    sums = lax.all_to_all(own + other, "x", 0, 0)
-
+        )(*pieces, high, low, *earlier)
+
+    other = swap(product(amp_cross, 1, "dressed_other", OTHER))
+    early = product([amplitudes, *amp_same[:2]], 0, "dressed_early", EARLY)
+    sums = product([amp_same[2], amp_far], 3, "dressed_late", LATE, early, other)
+    sums = lax.all_to_all(sums, "x", 0, 0)
+
+    stacked = pl.pallas_call(
+        factor_kernel,
+        out_shape=jax.ShapeDtypeStruct((pairs, 2 * tile, naux), bf16),
+        in_specs=[VMEM],
+        out_specs=VMEM,
+        compiler_params=PARAMS,
+        name="factor_ready",
+    )(factor)
+    group = lax.axis_index("y") * 2 + lax.axis_index("core")
+    mine = lax.dynamic_slice_in_dim(pair_block, group * pairs, pairs)
+    places = jnp.arange(block_home.shape[0], dtype=jnp.int32)
+    homes = jnp.sum(jnp.where(mine[:, None] == places, block_home, 0), axis=1)
+    where = jnp.concatenate([homes, tile_mask.reshape(-1)])
     integral = pl.pallas_call(
         lambda *refs: integral_kernel(pairs, *refs),
         out_shape=jax.ShapeDtypeStruct((rows, width), F32),
-        in_specs=[SMEM] * 3 + [HBM] * 2,
+        in_specs=[SMEM, HBM, HBM],
         out_specs=VMEM,
         scratch_shapes=[
-            pltpu.VMEM((pairs, tile, naux), F32),
+            pltpu.VMEM((pairs, 2 * tile, naux), bf16),
             pltpu.VMEM((pairs, naux, width), F32),
-            sem((pairs,)),
-            sem((pairs,)),
+            sem((pairs + 1,)),
         ],
         compiler_params=pltpu.CompilerParams(vmem_limit_bytes=56 * 1024 * 1024),
         name="integral",
-    )(pair_block, block_home, tile_mask.reshape(-1), factor, gathered)
+    )(where, stacked, gathered)
     residual = integral + ((sums[0] + sums[1]) + (sums[2] + sums[3]))
     return residual, amplitudes - residual / (row_energy[:, None] + column_energy[None, :])
 

time: 88.5 us -> 87.9 us (level)
  waiting for transfers between devices: 15.5 us -> 13.5 us
  local copies, waits for them, and re-layouts: 0.69 us -> 1.96 us
    ppermute x7, waiting for transfers between devices: 5.96 us -> 3.38 us  [ring(): return lax.ppermute(value, names, pairs_of)]
    unnamed x9 -> x23, local copies, waits for them, and re-layouts: 0.1 us -> 1.81 us
    pallas_call x2 -> x4, Pallas kernels: 4.24 us -> 5.81 us  [the longest x3 5.68 us: product(): pl.pallas_call(lambda *refs: product_kernel(first, count, added, *refs),...]
    add x1 -> x0, other arithmetic: 1.18 us -> none  [shards(): sums = lax.all_to_all(own + other, 'x', 0, 0)]
  transfers between devices with their start and end apart: 11 -> 11, of which waited for: 4 -> 4; matrix products, arithmetic and copies ran while one was open for 2% -> 1% of each run, Pallas kernels for 10% -> 11%
where the time goes in v5:
time: 87.9 us; the launch traced here: 87.3 us
  starting transfers between devices  45 us (51%)
  between operations  14.3 us (16%)
  waiting for transfers between devices  13.5 us (15%)
  Pallas kernels  9.97 us (11%)
  other arithmetic  2.59 us (3%)
  local copies, waits for them, and re-layouts  1.96 us (2%)
    ppermute x7, starting transfers between devices, ring(): return lax.ppermute(value, names, pairs_of)  33.3 us
    all_gather x1, waiting for transfers between devices, shards(): gathered = lax.all_gather(blocks, ('y', 'core'), axis=0, tiled=True)  8.85 us
    pallas_call x3, Pallas kernels, product(): pl.pallas_call(lambda *refs: product_kernel(first, count, added, *refs),...  5.68 us
    all_to_all x1, starting transfers between devices, shards(): panels = lax.all_to_all(dressing.reshape(nx, depth, width), 'x', 0, 0)  4.99 us
    all_to_all x1, starting transfers between devices, shards(): sums = lax.all_to_all(sums, 'x', 0, 0)  4.09 us
    pallas_call x1, Pallas kernels, shards(): pl.pallas_call(lambda *refs: integral_kernel(pairs, *refs), out_shape=jax...  3.76 us
    ppermute x7, waiting for transfers between devices, ring(): return lax.ppermute(value, names, pairs_of)  3.38 us
    ppermute x1, starting transfers between devices, swap(): return lax.ppermute(value, 'core', [(0, 1), (1, 0)])  2.63 us
  transfers between devices with their start and end apart: 11, of which 4 were waited for; matrix products, arithmetic and copies ran while one was open for 1% of the time, Pallas kernels for 11%

profile of v5, /device:TPU:1, one launch (start us, length us, event | category | flops | bytes accessed | tf_op | source)
XLA Modules:
  0.0 87.3 jit_solution(977714138141011935)
XLA Ops:
  7.2 0.0 all-gather.2.cloned.1.call-start
  7.2 0.7 all-gather.2.cloned.1.call-update
  7.9 0.0 copy-start.2
  7.9 5.0 %all-to-all-start = ((f32[4,1024,128]{2,1,0:T(8,128)}), f32[4,1024,128]{2,1,0:T(8,128)S(1)}, u32[]{:S(2)}, u32[]{:S(2)}) async-start(f32[4,1024,128]{2,1,0:T(8,128)} %bitcast.8), calls=%async_computation | async-start | bytes 4194304 | tf_op jit(solution)/shard_map/all_to_all | solution.py:157
  12.9 0.0 copy-done.2
  12.9 4.8 %collective-permute-start.4 = (f32[512,128]{1,0:T(8,128)S(1)}, f32[512,128]{1,0:T(8,128)S(1)}, u32[]{:S(2)}, u32[]{:S(2)}) collective-permute-start(f32[512,128]{1,0:T(8,128)S(1)} %copy-done.2), channel_id=1, source_target_pairs={{32,1},{33,2},{34,3},{35,4},{36,5},{37,6},{38,7},{39,0},{0,39},{1,... | collective-permute-start | bytes 786440 | tf_op jit(solution)/shard_map/ppermute | solution.py:138
  17.7 7.7 %collective-permute-start = (f32[512,128]{1,0:T(8,128)S(1)}, f32[512,128]{1,0:T(8,128)S(1)}, u32[]{:S(2)}, u32[]{:S(2)}) collective-permute-start(f32[512,128]{1,0:T(8,128)S(1)} %copy-done.2), channel_id=1, source_target_pairs={{0,1},{1,2},{2,3},{3,4},{4,5},{5,6},{6,7},{7,0},{32,39},{33,32},{3... | collective-permute-start | bytes 786440 | tf_op jit(solution)/shard_map/ppermute | solution.py:138
  25.5 0.0 collective-permute-done.4.refs_0_
  25.5 8.6 %collective-permute-start.5 = (f32[512,128]{1,0:T(8,128)S(1)}, f32[512,128]{1,0:T(8,128)S(1)}, u32[]{:S(2)}, u32[]{:S(2)}) collective-permute-start(f32[512,128]{1,0:T(8,128)S(1)} %collective-permute-done.4.refs_0_), channel_id=1, source_target_pairs={{0,1},{1,2},{2,3},{3,4},{4,5},{5,6},{6,7},{7,0},{32,39},{33,32},{3... | collective-permute-start | bytes 786440 | tf_op jit(solution)/shard_map/ppermute | solution.py:138
  34.2 0.0 collective-permute-done.refs_1_
  34.2 1.9 %collective-permute-start.1 = (f32[512,128]{1,0:T(8,128)S(1)}, f32[512,128]{1,0:T(8,128)}, u32[]{:S(2)}, u32[]{:S(2)}) collective-permute-start(f32[512,128]{1,0:T(8,128)S(1)} %collective-permute-done.refs_1_), channel_id=1, source_target_pairs={{0,1},{1,2},{2,3},{3,4},{4,5},{5,6},{6,7},{7,0},{32,39},{33,32},{3... | collective-permute-start | bytes 786440 | tf_op jit(solution)/shard_map/ppermute | solution.py:138
  36.1 0.0 copy-start.4
  36.1 0.7 copy-done.4
  36.8 0.6 collective-permute-done.5.refs_1_
  37.4 5.4 %collective-permute-start.6 = (f32[512,128]{1,0:T(8,128)S(1)}, f32[512,128]{1,0:T(8,128)S(1)}, u32[]{:S(2)}, u32[]{:S(2)}) collective-permute-start(f32[512,128]{1,0:T(8,128)S(1)} %collective-permute-done.5.refs_1_), channel_id=1, source_target_pairs={{0,1},{1,2},{2,3},{3,4},{4,5},{5,6},{6,7},{7,0},{32,39},{33,32},{3... | collective-permute-start | bytes 786440 | tf_op jit(solution)/shard_map/ppermute | solution.py:138
  42.9 0.0 collective-permute-done.1.refs_2_
  42.9 2.8 %collective-permute-start.2 = (f32[512,128]{1,0:T(8,128)}, f32[512,128]{1,0:T(8,128)S(1)}, u32[]{:S(2)}, u32[]{:S(2)}) collective-permute-start(f32[512,128]{1,0:T(8,128)} %collective-permute-done.1.refs_2_), channel_id=1, source_target_pairs={{0,1},{1,2},{2,3},{3,4},{4,5},{5,6},{6,7},{7,0},{32,39},{33,32},{3... | collective-permute-start | bytes 786440 | tf_op jit(solution)/shard_map/ppermute | solution.py:138
  45.7 1.9 %collective-permute-start.3 = (f32[512,128]{1,0:T(8,128)}, f32[512,128]{1,0:T(8,128)S(1)}, u32[]{:S(2)}, u32[]{:S(2)}) collective-permute-start(f32[512,128]{1,0:T(8,128)} %collective-permute-done.1.refs_2_), channel_id=1, source_target_pairs={{0,2},{1,3},{2,4},{3,5},{4,6},{5,7},{6,0},{7,1},{32,38},{33,39},{3... | collective-permute-start | bytes 786440 | tf_op jit(solution)/shard_map/ppermute | solution.py:138
  47.6 0.0 all-to-all-done.refs_0_
  47.6 0.4 dressing_ready.1
  48.0 0.0 copy-start.3
  48.0 0.0 copy-start.5
  48.0 0.0 collective-permute-done.6.refs_2_
  48.1 1.6 %dressed_other.1 = f32[4,512,128]{2,1,0:T(8,128)S(1)} custom-call(f32[512,128]{1,0:T(8,128)S(1)} %collective-permute-done.4.refs_0_, f32[512,128]{1,0:T(8,128)S(1)} %collective-permute-done.5.refs_1_, f32[512,128]{1,0:T(8,128)S(1)} %collective-permute-done.6.refs_2_, bf16[640,512]{1,0:T(8,128)(2,1)S(1)} %get-tuple-element.4.refs_3_.refs_2_, ...), custom_call_target="tpu_custom_call" | custom-call | flops 1000 | bytes 1000000 | tf_op jit(solution)/shard_map/dressed_other/pallas_call | solution.py:173
  49.7 2.6 %collective-permute-start.7 = (f32[4,512,128]{2,1,0:T(8,128)S(1)}, f32[4,512,128]{2,1,0:T(8,128)S(1)}, u32[]{:S(2)}, u32[]{:S(2)}) collective-permute-start(f32[4,512,128]{2,1,0:T(8,128)S(1)} %dressed_other.1), channel_id=1, source_target_pairs={{0,32},{32,0},{1,33},{33,1},{2,34},{34,2},{3,35},{35,3},{4,36},{36... | collective-permute-start | bytes 3145736 | tf_op jit(solution)/shard_map/ppermute | solution.py:141
  52.3 0.0 copy-done.3
  52.3 0.0 copy-done.5
  52.3 2.1 %dressed_early.1.refs_4_ = f32[4,512,128]{2,1,0:T(8,128)S(1)} custom-call(f32[512,128]{1,0:T(8,128)S(1)} %copy-done.3, f32[512,128]{1,0:T(8,128)S(1)} %copy-done.5, f32[512,128]{1,0:T(8,128)} %collective-permute-done.1.refs_2_, bf16[640,512]{1,0:T(8,128)(2,1)S(1)} %get-tuple-element.4.refs_3_.refs_2_, bf16[640,512]{1,0:T(8,128)(2,1)S(1)} %get-tuple-element.5.refs_4_.refs_3_), custom_call_target="tpu_custom_call" | custom-call | flops 30000001024 | bytes 1000000 | tf_op jit(solution)/shard_map/dressed_early/pallas_call | solution.py:173
  54.4 0.0 collective-permute-done.2.refs_0_
  54.4 2.7 %collective-permute-done.3.refs_1_ = f32[512,128]{1,0:T(8,128)S(1)} collective-permute-done((f32[512,128]{1,0:T(8,128)}, f32[512,128]{1,0:T(8,128)S(1)}, u32[]{:S(2)}, u32[]{:S(2)}) %collective-permute-start.3) | collective-permute-done | bytes 262176 | tf_op jit(solution)/shard_map/ppermute | solution.py:138
  57.1 0.0 collective-permute-done.7.refs_5_
  57.1 2.0 %dressed_late.1 = f32[4,512,128]{2,1,0:T(8,128)} custom-call(f32[512,128]{1,0:T(8,128)S(1)} %collective-permute-done.2.refs_0_, f32[512,128]{1,0:T(8,128)S(1)} %collective-permute-done.3.refs_1_, bf16[640,512]{1,0:T(8,128)(2,1)S(1)} %get-tuple-element.4.refs_3_.refs_2_, bf16[640,512]{1,0:T(8,128)(2,1)S(1)} %get-tuple-element.5.refs_4_.refs_3_, ...), custom_call_target="tpu_custom_call" | custom-call | flops 1000 | bytes 1000000 | tf_op jit(solution)/shard_map/dressed_late/pallas_call | solution.py:173
  59.1 0.0 copy-start.7
  59.2 0.0 copy-start.1
  59.2 0.0 copy-start.9
  59.2 0.0 copy-start.10
  59.2 4.1 %all-to-all-start.1 = ((f32[4,512,128]{2,1,0:T(8,128)}), f32[4,512,128]{2,1,0:T(8,128)S(1)}, u32[]{:S(2)}, u32[]{:S(2)}) async-start(f32[4,512,128]{2,1,0:T(8,128)} %dressed_late.1), calls=%async_computation.1 | async-start | bytes 2097152 | tf_op jit(solution)/shard_map/all_to_all | solution.py:191
  63.3 0.0 copy-done.7
  63.3 0.1 copy.14
  63.4 0.1 reshape.16
  63.4 0.0 copy-done.1
  63.5 0.1 factor_ready.1.refs_1_
  63.6 0.0 copy-start
  63.6 1.0 %copy-done = bf16[8,128,512]{2,1,0:T(8,128)(2,1)} copy-done((bf16[8,128,512]{2,1,0:T(8,128)(2,1)}, bf16[8,128,512]{2,1,0:T(8,128)(2,1)S(1)}, u32[]{:S(2)}) %copy-start) | copy-done | bytes 1048600
  64.6 0.0 copy-done.9
  64.6 0.1 dynamic_slice.3
  64.6 0.0 copy-done.10
  64.7 0.2 select_reduce_fusion
  64.8 0.6 pad_add_fusion.refs_0_
  65.4 0.0 copy-start.6
  65.4 0.0 copy-start.8
  65.4 8.9 %all-gather.2.cloned.1.call-done.refs_2_ = f32[32,512,128]{2,1,0:T(8,128)} async-done(((f32[2,512,128]{2,1,0:T(8,128)}), f32[32,512,128]{2,1,0:T(8,128)}) %all-gather.2.cloned.1.call-update) | async-done | bytes 8388624 | tf_op jit(solution)/shard_map/all_gather | solution.py:150
  74.3 3.8 %integral.1 = f32[512,128]{1,0:T(8,128)} custom-call(s32[24]{0:T(128)} %pad_add_fusion.refs_0_, bf16[8,128,512]{2,1,0:T(8,128)(2,1)} %copy-done, f32[32,512,128]{2,1,0:T(8,128)} %all-gather.2.cloned.1.call-done.refs_2_), custom_call_target="tpu_custom_call" | custom-call | tf_op jit(solution)/shard_map/integral/pallas_call | solution.py:206
  78.1 0.6 all-to-all-done.1
  78.7 0.0 copy-done.6
  78.7 0.0 copy-done.8
  78.7 1.8 %divide_subtract_fusion = (f32[512,128]{1,0:T(8,128)}, f32[512,128]{1,0:T(8,128)}) fusion(f32[512,128]{1,0:T(8,128)S(1)} %copy-done.3, f32[128]{0:T(128)S(1)} %copy-done.8, f32[512]{0:T(512)S(1)} %copy-done.6, f32[512,128]{1,0:T(8,128)} %integral.1, f32[4,512,128]{2,1,0:T(8,128)S(1)} %all-to-all-done.1), kind=kLoop, calls=%fused_computation.5 | loop fusion | flops 458752 | bytes 2099712 | tf_op jit(solution)/shard_map/sub | solution.py:220
Async XLA Ops:
  7.2 67.1 %all-gather.2.cloned.1.call-start = ((), (), s32[]{:S(2)}) async-start(), calls=%async_computation.2 | async-start | bytes 8912896 | tf_op jit(solution)/shard_map/all_gather | solution.py:150
  7.9 5.0 %copy-start.2 = (f32[512,128]{1,0:T(8,128)S(1)}, f32[512,128]{1,0:T(8,128)}, u32[]{:S(2)}) copy-start(f32[512,128]{1,0:T(8,128)} %refs_0_.1) | copy-start | bytes 786436
  7.9 39.7 %all-to-all-start = ((f32[4,1024,128]{2,1,0:T(8,128)}), f32[4,1024,128]{2,1,0:T(8,128)S(1)}, u32[]{:S(2)}, u32[]{:S(2)}) async-start(f32[4,1024,128]{2,1,0:T(8,128)} %bitcast.8), calls=%async_computation | async-start | bytes 4194304 | tf_op jit(solution)/shard_map/all_to_all | solution.py:157
  12.9 12.6 %collective-permute-start.4 = (f32[512,128]{1,0:T(8,128)S(1)}, f32[512,128]{1,0:T(8,128)S(1)}, u32[]{:S(2)}, u32[]{:S(2)}) collective-permute-start(f32[512,128]{1,0:T(8,128)S(1)} %copy-done.2), channel_id=1, source_target_pairs={{32,1},{33,2},{34,3},{35,4},{36,5},{37,6},{38,7},{39,0},{0,39},{1,... | collective-permute-start | bytes 786440 | tf_op jit(solution)/shard_map/ppermute | solution.py:138
  17.7 16.4 %collective-permute-start = (f32[512,128]{1,0:T(8,128)S(1)}, f32[512,128]{1,0:T(8,128)S(1)}, u32[]{:S(2)}, u32[]{:S(2)}) collective-permute-start(f32[512,128]{1,0:T(8,128)S(1)} %copy-done.2), channel_id=1, source_target_pairs={{0,1},{1,2},{2,3},{3,4},{4,5},{5,6},{6,7},{7,0},{32,39},{33,32},{3... | collective-permute-start | bytes 786440 | tf_op jit(solution)/shard_map/ppermute | solution.py:138
  25.5 11.9 %collective-permute-start.5 = (f32[512,128]{1,0:T(8,128)S(1)}, f32[512,128]{1,0:T(8,128)S(1)}, u32[]{:S(2)}, u32[]{:S(2)}) collective-permute-start(f32[512,128]{1,0:T(8,128)S(1)} %collective-permute-done.4.refs_0_), channel_id=1, source_target_pairs={{0,1},{1,2},{2,3},{3,4},{4,5},{5,6},{6,7},{7,0},{32,39},{33,32},{3... | collective-permute-start | bytes 786440 | tf_op jit(solution)/shard_map/ppermute | solution.py:138
  34.2 8.7 %collective-permute-start.1 = (f32[512,128]{1,0:T(8,128)S(1)}, f32[512,128]{1,0:T(8,128)}, u32[]{:S(2)}, u32[]{:S(2)}) collective-permute-start(f32[512,128]{1,0:T(8,128)S(1)} %collective-permute-done.refs_1_), channel_id=1, source_target_pairs={{0,1},{1,2},{2,3},{3,4},{4,5},{5,6},{6,7},{7,0},{32,39},{33,32},{3... | collective-permute-start | bytes 786440 | tf_op jit(solution)/shard_map/ppermute | solution.py:138
  36.1 0.7 copy-start.4
  37.4 10.6 %collective-permute-start.6 = (f32[512,128]{1,0:T(8,128)S(1)}, f32[512,128]{1,0:T(8,128)S(1)}, u32[]{:S(2)}, u32[]{:S(2)}) collective-permute-start(f32[512,128]{1,0:T(8,128)S(1)} %collective-permute-done.5.refs_1_), channel_id=1, source_target_pairs={{0,1},{1,2},{2,3},{3,4},{4,5},{5,6},{6,7},{7,0},{32,39},{33,32},{3... | collective-permute-start | bytes 786440 | tf_op jit(solution)/shard_map/ppermute | solution.py:138
  42.9 11.5 %collective-permute-start.2 = (f32[512,128]{1,0:T(8,128)}, f32[512,128]{1,0:T(8,128)S(1)}, u32[]{:S(2)}, u32[]{:S(2)}) collective-permute-start(f32[512,128]{1,0:T(8,128)} %collective-permute-done.1.refs_2_), channel_id=1, source_target_pairs={{0,1},{1,2},{2,3},{3,4},{4,5},{5,6},{6,7},{7,0},{32,39},{33,32},{3... | collective-permute-start | bytes 786440 | tf_op jit(solution)/shard_map/ppermute | solution.py:138
  45.7 11.4 %collective-permute-start.3 = (f32[512,128]{1,0:T(8,128)}, f32[512,128]{1,0:T(8,128)S(1)}, u32[]{:S(2)}, u32[]{:S(2)}) collective-permute-start(f32[512,128]{1,0:T(8,128)} %collective-permute-done.1.refs_2_), channel_id=1, source_target_pairs={{0,2},{1,3},{2,4},{3,5},{4,6},{5,7},{6,0},{7,1},{32,38},{33,39},{3... | collective-permute-start | bytes 786440 | tf_op jit(solution)/shard_map/ppermute | solution.py:138
  48.0 4.3 %copy-start.3 = (f32[512,128]{1,0:T(8,128)S(1)}, f32[512,128]{1,0:T(8,128)}, u32[]{:S(2)}) copy-start(f32[512,128]{1,0:T(8,128)} %refs_0_.1) | copy-start | bytes 786436
  48.0 4.3 %copy-start.5 = (f32[512,128]{1,0:T(8,128)S(1)}, f32[512,128]{1,0:T(8,128)}, u32[]{:S(2)}) copy-start(f32[512,128]{1,0:T(8,128)} %copy-done.4) | copy-start | bytes 786436
  49.7 7.5 %collective-permute-start.7 = (f32[4,512,128]{2,1,0:T(8,128)S(1)}, f32[4,512,128]{2,1,0:T(8,128)S(1)}, u32[]{:S(2)}, u32[]{:S(2)}) collective-permute-start(f32[4,512,128]{2,1,0:T(8,128)S(1)} %dressed_other.1), channel_id=1, source_target_pairs={{0,32},{32,0},{1,33},{33,1},{2,34},{34,2},{3,35},{35,3},{4,36},{36... | collective-permute-start | bytes 3145736 | tf_op jit(solution)/shard_map/ppermute | solution.py:141
  59.1 4.1 %copy-start.7 = (s32[8,2]{0,1:T(2,128)S(1)}, s32[8,2]{0,1:T(2,128)}, u32[]{:S(2)}) copy-start(s32[8,2]{0,1:T(2,128)} %param.15) | copy-start | bytes 196
  59.2 4.3 %copy-start.1 = (f32[8,512,64]{1,2,0:T(8,128)S(1)}, f32[8,512,64]{1,2,0:T(8,128)}, u32[]{:S(2)}) copy-start(f32[8,512,64]{1,2,0:T(8,128)} %param.11) | copy-start | bytes 3145732
  59.2 5.4 %copy-start.9 = (s32[128]{0:T(128)S(1)}, s32[128]{0:T(128)}, u32[]{:S(2)}) copy-start(s32[128]{0:T(128)} %param.13) | copy-start | bytes 1540
  59.2 5.5 %copy-start.10 = (s32[32]{0:T(128)S(1)}, s32[32]{0:T(128)}, u32[]{:S(2)}) copy-start(s32[32]{0:T(128)} %param.14) | copy-start | bytes 388
  59.2 19.5 %all-to-all-start.1 = ((f32[4,512,128]{2,1,0:T(8,128)}), f32[4,512,128]{2,1,0:T(8,128)S(1)}, u32[]{:S(2)}, u32[]{:S(2)}) async-start(f32[4,512,128]{2,1,0:T(8,128)} %dressed_late.1), calls=%async_computation.1 | async-start | bytes 2097152 | tf_op jit(solution)/shard_map/all_to_all | solution.py:191
  63.6 1.0 %copy-start = (bf16[8,128,512]{2,1,0:T(8,128)(2,1)}, bf16[8,128,512]{2,1,0:T(8,128)(2,1)S(1)}, u32[]{:S(2)}) copy-start(bf16[8,128,512]{2,1,0:T(8,128)(2,1)S(1)} %factor_ready.1.refs_1_) | copy-start | bytes 3145732
  65.4 13.2 %copy-start.6 = (f32[512]{0:T(512)S(1)}, f32[512]{0:T(512)}, u32[]{:S(2)}) copy-start(f32[512]{0:T(512)} %param.16) | copy-start | bytes 6148
  65.4 13.2 %copy-start.8 = (f32[128]{0:T(128)S(1)}, f32[128]{0:T(128)}, u32[]{:S(2)}) copy-start(f32[128]{0:T(128)} %param.17) | copy-start | bytes 1540
Sparse Core Ops, SparseCore 0:
  10.1 64.1 all-gather.1

commit v6 on v5

--- a/solution.py
+++ b/solution.py
@@ -213,7 +213,7 @@
             pltpu.VMEM((pairs, naux, width), F32),
             sem((pairs + 1,)),
         ],
-        compiler_params=pltpu.CompilerParams(vmem_limit_bytes=56 * 1024 * 1024),
+        compiler_params=pltpu.CompilerParams(vmem_limit_bytes=48 * 1024 * 1024),
         name="integral",
     )(where, stacked, gathered)
     residual = integral + ((sums[0] + sums[1]) + (sums[2] + sums[3]))

time: 87.9 us -> 86.9 us (0.989)
  waiting for transfers between devices: 13.5 us -> 16.2 us
  other arithmetic: 2.59 us -> 1.13 us
  Pallas kernels: 9.97 us -> 8.78 us
  local copies, waits for them, and re-layouts: 1.96 us -> 0.99 us
    all_gather x1, waiting for transfers between devices: 8.85 us -> 10.3 us  [shards(): gathered = lax.all_gather(blocks, ('y', 'core'), axis=0, tiled=True)]
    all_to_all x1, waiting for transfers between devices: 0.61 us -> 1.8 us  [shards(): sums = lax.all_to_all(sums, 'x', 0, 0)]
    pallas_call x1, Pallas kernels: 3.76 us -> 2.58 us  [shards(): pl.pallas_call(lambda *refs: integral_kernel(pairs, *refs), out_shape=jax...]
    unnamed x23, local copies, waits for them, and re-layouts: 1.81 us -> 0.83 us
    sub x1, other arithmetic: 1.82 us -> 0.87 us  [shards(): amplitudes - residual / (row_energy[:, None] + column_energy[None, :])]
  transfers between devices with their start and end apart: 11 -> 11, of which waited for: 4 -> 4; matrix products, arithmetic and copies ran while one was open for 1% -> 1% of each run, Pallas kernels for 11% -> 10%
where the time goes in v6:
time: 86.9 us; the launch traced here: 86.4 us
  starting transfers between devices  45 us (52%)
  waiting for transfers between devices  16.2 us (19%)
  between operations  14.3 us (16%)
  Pallas kernels  8.78 us (10%)
  other arithmetic  1.13 us (1%)
  local copies, waits for them, and re-layouts  0.99 us (1%)
    ppermute x7, starting transfers between devices, ring(): return lax.ppermute(value, names, pairs_of)  33.3 us
    all_gather x1, waiting for transfers between devices, shards(): gathered = lax.all_gather(blocks, ('y', 'core'), axis=0, tiled=True)  10.3 us
    pallas_call x3, Pallas kernels, product(): pl.pallas_call(lambda *refs: product_kernel(first, count, added, *refs),...  5.68 us
    all_to_all x1, starting transfers between devices, shards(): panels = lax.all_to_all(dressing.reshape(nx, depth, width), 'x', 0, 0)  4.99 us
    all_to_all x1, starting transfers between devices, shards(): sums = lax.all_to_all(sums, 'x', 0, 0)  4.09 us
    ppermute x7, waiting for transfers between devices, ring(): return lax.ppermute(value, names, pairs_of)  3.38 us
    ppermute x1, starting transfers between devices, swap(): return lax.ppermute(value, 'core', [(0, 1), (1, 0)])  2.63 us
    pallas_call x1, Pallas kernels, shards(): pl.pallas_call(lambda *refs: integral_kernel(pairs, *refs), out_shape=jax...  2.58 us
  transfers between devices with their start and end apart: 11, of which 4 were waited for; matrix products, arithmetic and copies ran while one was open for 1% of the time, Pallas kernels for 10%

profile of v6, /device:TPU:1, one launch (start us, length us, event | category | flops | bytes accessed | tf_op | source)
XLA Modules:
  0.0 86.4 jit_solution(12755576526319355065)
XLA Ops:
  7.2 0.0 all-gather.2.cloned.1.call-start
  7.2 0.7 all-gather.2.cloned.1.call-update
  7.9 0.0 copy-start.1
  7.9 5.0 %all-to-all-start = ((f32[4,1024,128]{2,1,0:T(8,128)}), f32[4,1024,128]{2,1,0:T(8,128)S(1)}, u32[]{:S(2)}, u32[]{:S(2)}) async-start(f32[4,1024,128]{2,1,0:T(8,128)} %bitcast.8), calls=%async_computation | async-start | bytes 4194304 | tf_op jit(solution)/shard_map/all_to_all | solution.py:157
  12.9 0.0 copy-done.1
  12.9 4.8 %collective-permute-start.4 = (f32[512,128]{1,0:T(8,128)S(1)}, f32[512,128]{1,0:T(8,128)S(1)}, u32[]{:S(2)}, u32[]{:S(2)}) collective-permute-start(f32[512,128]{1,0:T(8,128)S(1)} %copy-done.1), channel_id=1, source_target_pairs={{32,1},{33,2},{34,3},{35,4},{36,5},{37,6},{38,7},{39,0},{0,39},{1,... | collective-permute-start | bytes 786440 | tf_op jit(solution)/shard_map/ppermute | solution.py:138
  17.7 7.7 %collective-permute-start = (f32[512,128]{1,0:T(8,128)S(1)}, f32[512,128]{1,0:T(8,128)S(1)}, u32[]{:S(2)}, u32[]{:S(2)}) collective-permute-start(f32[512,128]{1,0:T(8,128)S(1)} %copy-done.1), channel_id=1, source_target_pairs={{0,1},{1,2},{2,3},{3,4},{4,5},{5,6},{6,7},{7,0},{32,39},{33,32},{3... | collective-permute-start | bytes 786440 | tf_op jit(solution)/shard_map/ppermute | solution.py:138
  25.5 0.0 collective-permute-done.4.refs_0_
  25.5 8.6 %collective-permute-start.5 = (f32[512,128]{1,0:T(8,128)S(1)}, f32[512,128]{1,0:T(8,128)S(1)}, u32[]{:S(2)}, u32[]{:S(2)}) collective-permute-start(f32[512,128]{1,0:T(8,128)S(1)} %collective-permute-done.4.refs_0_), channel_id=1, source_target_pairs={{0,1},{1,2},{2,3},{3,4},{4,5},{5,6},{6,7},{7,0},{32,39},{33,32},{3... | collective-permute-start | bytes 786440 | tf_op jit(solution)/shard_map/ppermute | solution.py:138
  34.2 0.0 collective-permute-done.refs_1_
  34.2 1.9 %collective-permute-start.1 = (f32[512,128]{1,0:T(8,128)S(1)}, f32[512,128]{1,0:T(8,128)}, u32[]{:S(2)}, u32[]{:S(2)}) collective-permute-start(f32[512,128]{1,0:T(8,128)S(1)} %collective-permute-done.refs_1_), channel_id=1, source_target_pairs={{0,1},{1,2},{2,3},{3,4},{4,5},{5,6},{6,7},{7,0},{32,39},{33,32},{3... | collective-permute-start | bytes 786440 | tf_op jit(solution)/shard_map/ppermute | solution.py:138
  36.1 0.0 copy-start.4
  36.1 0.7 copy-done.4
  36.8 0.6 collective-permute-done.5.refs_1_
  37.4 5.4 %collective-permute-start.6 = (f32[512,128]{1,0:T(8,128)S(1)}, f32[512,128]{1,0:T(8,128)S(1)}, u32[]{:S(2)}, u32[]{:S(2)}) collective-permute-start(f32[512,128]{1,0:T(8,128)S(1)} %collective-permute-done.5.refs_1_), channel_id=1, source_target_pairs={{0,1},{1,2},{2,3},{3,4},{4,5},{5,6},{6,7},{7,0},{32,39},{33,32},{3... | collective-permute-start | bytes 786440 | tf_op jit(solution)/shard_map/ppermute | solution.py:138
  42.9 0.0 collective-permute-done.1.refs_2_
  42.9 2.8 %collective-permute-start.2 = (f32[512,128]{1,0:T(8,128)}, f32[512,128]{1,0:T(8,128)S(1)}, u32[]{:S(2)}, u32[]{:S(2)}) collective-permute-start(f32[512,128]{1,0:T(8,128)} %collective-permute-done.1.refs_2_), channel_id=1, source_target_pairs={{0,1},{1,2},{2,3},{3,4},{4,5},{5,6},{6,7},{7,0},{32,39},{33,32},{3... | collective-permute-start | bytes 786440 | tf_op jit(solution)/shard_map/ppermute | solution.py:138
  45.7 1.9 %collective-permute-start.3 = (f32[512,128]{1,0:T(8,128)}, f32[512,128]{1,0:T(8,128)S(1)}, u32[]{:S(2)}, u32[]{:S(2)}) collective-permute-start(f32[512,128]{1,0:T(8,128)} %collective-permute-done.1.refs_2_), channel_id=1, source_target_pairs={{0,2},{1,3},{2,4},{3,5},{4,6},{5,7},{6,0},{7,1},{32,38},{33,39},{3... | collective-permute-start | bytes 786440 | tf_op jit(solution)/shard_map/ppermute | solution.py:138
  47.6 0.0 all-to-all-done.refs_0_
  47.6 0.4 dressing_ready.1
  48.0 0.0 copy-start.2
  48.0 0.0 copy-start.5
  48.0 0.0 collective-permute-done.6.refs_2_
  48.1 1.6 %dressed_other.1 = f32[4,512,128]{2,1,0:T(8,128)S(1)} custom-call(f32[512,128]{1,0:T(8,128)S(1)} %collective-permute-done.4.refs_0_, f32[512,128]{1,0:T(8,128)S(1)} %collective-permute-done.5.refs_1_, f32[512,128]{1,0:T(8,128)S(1)} %collective-permute-done.6.refs_2_, bf16[640,512]{1,0:T(8,128)(2,1)S(1)} %get-tuple-element.4.refs_3_.refs_2_, ...), custom_call_target="tpu_custom_call" | custom-call | flops 1000 | bytes 1000000 | tf_op jit(solution)/shard_map/dressed_other/pallas_call | solution.py:173
  49.7 2.6 %collective-permute-start.7 = (f32[4,512,128]{2,1,0:T(8,128)S(1)}, f32[4,512,128]{2,1,0:T(8,128)S(1)}, u32[]{:S(2)}, u32[]{:S(2)}) collective-permute-start(f32[4,512,128]{2,1,0:T(8,128)S(1)} %dressed_other.1), channel_id=1, source_target_pairs={{0,32},{32,0},{1,33},{33,1},{2,34},{34,2},{3,35},{35,3},{4,36},{36... | collective-permute-start | bytes 3145736 | tf_op jit(solution)/shard_map/ppermute | solution.py:141
  52.3 0.0 copy-done.2
  52.3 0.0 copy-done.5
  52.3 2.1 %dressed_early.1.refs_4_ = f32[4,512,128]{2,1,0:T(8,128)S(1)} custom-call(f32[512,128]{1,0:T(8,128)S(1)} %copy-done.2, f32[512,128]{1,0:T(8,128)S(1)} %copy-done.5, f32[512,128]{1,0:T(8,128)} %collective-permute-done.1.refs_2_, bf16[640,512]{1,0:T(8,128)(2,1)S(1)} %get-tuple-element.4.refs_3_.refs_2_, bf16[640,512]{1,0:T(8,128)(2,1)S(1)} %get-tuple-element.5.refs_4_.refs_3_), custom_call_target="tpu_custom_call" | custom-call | flops 30000001024 | bytes 1000000 | tf_op jit(solution)/shard_map/dressed_early/pallas_call | solution.py:173
  54.4 0.0 collective-permute-done.2.refs_0_
  54.4 2.7 %collective-permute-done.3.refs_1_ = f32[512,128]{1,0:T(8,128)S(1)} collective-permute-done((f32[512,128]{1,0:T(8,128)}, f32[512,128]{1,0:T(8,128)S(1)}, u32[]{:S(2)}, u32[]{:S(2)}) %collective-permute-start.3) | collective-permute-done | bytes 262176 | tf_op jit(solution)/shard_map/ppermute | solution.py:138
  57.1 0.0 collective-permute-done.7.refs_5_
  57.1 2.0 %dressed_late.1 = f32[4,512,128]{2,1,0:T(8,128)} custom-call(f32[512,128]{1,0:T(8,128)S(1)} %collective-permute-done.2.refs_0_, f32[512,128]{1,0:T(8,128)S(1)} %collective-permute-done.3.refs_1_, bf16[640,512]{1,0:T(8,128)(2,1)S(1)} %get-tuple-element.4.refs_3_.refs_2_, bf16[640,512]{1,0:T(8,128)(2,1)S(1)} %get-tuple-element.5.refs_4_.refs_3_, ...), custom_call_target="tpu_custom_call" | custom-call | flops 1000 | bytes 1000000 | tf_op jit(solution)/shard_map/dressed_late/pallas_call | solution.py:173
  59.1 0.0 copy-start.7
  59.2 0.0 copy-start
  59.2 0.0 copy-start.9
  59.2 0.0 copy-start.10
  59.2 4.1 %all-to-all-start.1 = ((f32[4,512,128]{2,1,0:T(8,128)}), f32[4,512,128]{2,1,0:T(8,128)S(1)}, u32[]{:S(2)}, u32[]{:S(2)}) async-start(f32[4,512,128]{2,1,0:T(8,128)} %dressed_late.1), calls=%async_computation.1 | async-start | bytes 2097152 | tf_op jit(solution)/shard_map/all_to_all | solution.py:191
  63.3 0.0 copy-done.7
  63.3 0.1 copy.14
  63.4 0.1 reshape.16
  63.4 0.0 copy-done
  63.5 0.1 factor_ready.1.refs_1_
  63.6 0.0 copy-done.9
  63.6 0.1 dynamic_slice.3
  63.7 0.0 copy-done.10
  63.7 0.2 select_reduce_fusion
  63.9 0.1 pad_add_fusion.refs_0_
  63.9 0.0 copy-start.3
  63.9 0.0 copy-start.6
  63.9 0.0 copy-start.8
  63.9 10.3 %all-gather.2.cloned.1.call-done.refs_2_ = f32[32,512,128]{2,1,0:T(8,128)} async-done(((f32[2,512,128]{2,1,0:T(8,128)}), f32[32,512,128]{2,1,0:T(8,128)}) %all-gather.2.cloned.1.call-update) | async-done | bytes 8388624 | tf_op jit(solution)/shard_map/all_gather | solution.py:150
  74.3 2.6 %integral.1 = f32[512,128]{1,0:T(8,128)S(1)} custom-call(s32[24]{0:T(128)S(1)} %pad_add_fusion.refs_0_, bf16[8,128,512]{2,1,0:T(8,128)(2,1)S(1)} %factor_ready.1.refs_1_, f32[32,512,128]{2,1,0:T(8,128)} %all-gather.2.cloned.1.call-done.refs_2_), custom_call_target="tpu_custom_call" | custom-call | tf_op jit(solution)/shard_map/integral/pallas_call | solution.py:206
  76.9 1.8 %all-to-all-done.1 = f32[4,512,128]{2,1,0:T(8,128)S(1)} async-done(((f32[4,512,128]{2,1,0:T(8,128)}), f32[4,512,128]{2,1,0:T(8,128)S(1)}, u32[]{:S(2)}, u32[]{:S(2)}) %all-to-all-start.1) | async-done | bytes 1048608 | tf_op jit(solution)/shard_map/all_to_all | solution.py:191
  78.7 0.0 copy-done.3
  78.7 0.0 copy-done.6
  78.7 0.0 copy-done.8
  78.7 0.9 %divide_subtract_fusion = (f32[512,128]{1,0:T(8,128)}, f32[512,128]{1,0:T(8,128)}) fusion(f32[512,128]{1,0:T(8,128)S(1)} %copy-done.3, f32[128]{0:T(128)S(1)} %copy-done.8, f32[512]{0:T(512)S(1)} %copy-done.6, f32[512,128]{1,0:T(8,128)S(1)} %integral.1, f32[4,512,128]{2,1,0:T(8,128)S(1)} %all-to-all-done.1), kind=kLoop, calls=%fused_computation.5 | loop fusion | flops 458752 | bytes 2099712 | tf_op jit(solution)/shard_map/sub | solution.py:220
Async XLA Ops:
  7.2 67.1 %all-gather.2.cloned.1.call-start = ((), (), s32[]{:S(2)}) async-start(), calls=%async_computation.2 | async-start | bytes 8912896 | tf_op jit(solution)/shard_map/all_gather | solution.py:150
  7.9 5.0 %copy-start.1 = (f32[512,128]{1,0:T(8,128)S(1)}, f32[512,128]{1,0:T(8,128)}, u32[]{:S(2)}) copy-start(f32[512,128]{1,0:T(8,128)} %refs_0_.1) | copy-start | bytes 786436
  7.9 39.7 %all-to-all-start = ((f32[4,1024,128]{2,1,0:T(8,128)}), f32[4,1024,128]{2,1,0:T(8,128)S(1)}, u32[]{:S(2)}, u32[]{:S(2)}) async-start(f32[4,1024,128]{2,1,0:T(8,128)} %bitcast.8), calls=%async_computation | async-start | bytes 4194304 | tf_op jit(solution)/shard_map/all_to_all | solution.py:157
  12.9 12.6 %collective-permute-start.4 = (f32[512,128]{1,0:T(8,128)S(1)}, f32[512,128]{1,0:T(8,128)S(1)}, u32[]{:S(2)}, u32[]{:S(2)}) collective-permute-start(f32[512,128]{1,0:T(8,128)S(1)} %copy-done.1), channel_id=1, source_target_pairs={{32,1},{33,2},{34,3},{35,4},{36,5},{37,6},{38,7},{39,0},{0,39},{1,... | collective-permute-start | bytes 786440 | tf_op jit(solution)/shard_map/ppermute | solution.py:138
  17.7 16.4 %collective-permute-start = (f32[512,128]{1,0:T(8,128)S(1)}, f32[512,128]{1,0:T(8,128)S(1)}, u32[]{:S(2)}, u32[]{:S(2)}) collective-permute-start(f32[512,128]{1,0:T(8,128)S(1)} %copy-done.1), channel_id=1, source_target_pairs={{0,1},{1,2},{2,3},{3,4},{4,5},{5,6},{6,7},{7,0},{32,39},{33,32},{3... | collective-permute-start | bytes 786440 | tf_op jit(solution)/shard_map/ppermute | solution.py:138
  25.5 11.9 %collective-permute-start.5 = (f32[512,128]{1,0:T(8,128)S(1)}, f32[512,128]{1,0:T(8,128)S(1)}, u32[]{:S(2)}, u32[]{:S(2)}) collective-permute-start(f32[512,128]{1,0:T(8,128)S(1)} %collective-permute-done.4.refs_0_), channel_id=1, source_target_pairs={{0,1},{1,2},{2,3},{3,4},{4,5},{5,6},{6,7},{7,0},{32,39},{33,32},{3... | collective-permute-start | bytes 786440 | tf_op jit(solution)/shard_map/ppermute | solution.py:138
  34.2 8.7 %collective-permute-start.1 = (f32[512,128]{1,0:T(8,128)S(1)}, f32[512,128]{1,0:T(8,128)}, u32[]{:S(2)}, u32[]{:S(2)}) collective-permute-start(f32[512,128]{1,0:T(8,128)S(1)} %collective-permute-done.refs_1_), channel_id=1, source_target_pairs={{0,1},{1,2},{2,3},{3,4},{4,5},{5,6},{6,7},{7,0},{32,39},{33,32},{3... | collective-permute-start | bytes 786440 | tf_op jit(solution)/shard_map/ppermute | solution.py:138
  36.1 0.7 copy-start.4
  37.4 10.6 %collective-permute-start.6 = (f32[512,128]{1,0:T(8,128)S(1)}, f32[512,128]{1,0:T(8,128)S(1)}, u32[]{:S(2)}, u32[]{:S(2)}) collective-permute-start(f32[512,128]{1,0:T(8,128)S(1)} %collective-permute-done.5.refs_1_), channel_id=1, source_target_pairs={{0,1},{1,2},{2,3},{3,4},{4,5},{5,6},{6,7},{7,0},{32,39},{33,32},{3... | collective-permute-start | bytes 786440 | tf_op jit(solution)/shard_map/ppermute | solution.py:138
  42.9 11.5 %collective-permute-start.2 = (f32[512,128]{1,0:T(8,128)}, f32[512,128]{1,0:T(8,128)S(1)}, u32[]{:S(2)}, u32[]{:S(2)}) collective-permute-start(f32[512,128]{1,0:T(8,128)} %collective-permute-done.1.refs_2_), channel_id=1, source_target_pairs={{0,1},{1,2},{2,3},{3,4},{4,5},{5,6},{6,7},{7,0},{32,39},{33,32},{3... | collective-permute-start | bytes 786440 | tf_op jit(solution)/shard_map/ppermute | solution.py:138
  45.7 11.4 %collective-permute-start.3 = (f32[512,128]{1,0:T(8,128)}, f32[512,128]{1,0:T(8,128)S(1)}, u32[]{:S(2)}, u32[]{:S(2)}) collective-permute-start(f32[512,128]{1,0:T(8,128)} %collective-permute-done.1.refs_2_), channel_id=1, source_target_pairs={{0,2},{1,3},{2,4},{3,5},{4,6},{5,7},{6,0},{7,1},{32,38},{33,39},{3... | collective-permute-start | bytes 786440 | tf_op jit(solution)/shard_map/ppermute | solution.py:138
  48.0 4.3 %copy-start.2 = (f32[512,128]{1,0:T(8,128)S(1)}, f32[512,128]{1,0:T(8,128)}, u32[]{:S(2)}) copy-start(f32[512,128]{1,0:T(8,128)} %refs_0_.1) | copy-start | bytes 786436
  48.0 4.3 %copy-start.5 = (f32[512,128]{1,0:T(8,128)S(1)}, f32[512,128]{1,0:T(8,128)}, u32[]{:S(2)}) copy-start(f32[512,128]{1,0:T(8,128)} %copy-done.4) | copy-start | bytes 786436
  49.7 7.5 %collective-permute-start.7 = (f32[4,512,128]{2,1,0:T(8,128)S(1)}, f32[4,512,128]{2,1,0:T(8,128)S(1)}, u32[]{:S(2)}, u32[]{:S(2)}) collective-permute-start(f32[4,512,128]{2,1,0:T(8,128)S(1)} %dressed_other.1), channel_id=1, source_target_pairs={{0,32},{32,0},{1,33},{33,1},{2,34},{34,2},{3,35},{35,3},{4,36},{36... | collective-permute-start | bytes 3145736 | tf_op jit(solution)/shard_map/ppermute | solution.py:141
  59.1 4.1 %copy-start.7 = (s32[8,2]{0,1:T(2,128)S(1)}, s32[8,2]{0,1:T(2,128)}, u32[]{:S(2)}) copy-start(s32[8,2]{0,1:T(2,128)} %param.15) | copy-start | bytes 196
  59.2 4.3 %copy-start = (f32[8,512,64]{1,2,0:T(8,128)S(1)}, f32[8,512,64]{1,2,0:T(8,128)}, u32[]{:S(2)}) copy-start(f32[8,512,64]{1,2,0:T(8,128)} %param.11) | copy-start | bytes 3145732
  59.2 4.4 %copy-start.9 = (s32[128]{0:T(128)S(1)}, s32[128]{0:T(128)}, u32[]{:S(2)}) copy-start(s32[128]{0:T(128)} %param.13) | copy-start | bytes 1540
  59.2 4.5 %copy-start.10 = (s32[32]{0:T(128)S(1)}, s32[32]{0:T(128)}, u32[]{:S(2)}) copy-start(s32[32]{0:T(128)} %param.14) | copy-start | bytes 388
  59.2 19.5 %all-to-all-start.1 = ((f32[4,512,128]{2,1,0:T(8,128)}), f32[4,512,128]{2,1,0:T(8,128)S(1)}, u32[]{:S(2)}, u32[]{:S(2)}) async-start(f32[4,512,128]{2,1,0:T(8,128)} %dressed_late.1), calls=%async_computation.1 | async-start | bytes 2097152 | tf_op jit(solution)/shard_map/all_to_all | solution.py:191
  63.9 14.7 %copy-start.3 = (f32[512,128]{1,0:T(8,128)S(1)}, f32[512,128]{1,0:T(8,128)}, u32[]{:S(2)}) copy-start(f32[512,128]{1,0:T(8,128)} %refs_0_.1) | copy-start | bytes 786436
  63.9 14.7 %copy-start.6 = (f32[512]{0:T(512)S(1)}, f32[512]{0:T(512)}, u32[]{:S(2)}) copy-start(f32[512]{0:T(512)} %param.16) | copy-start | bytes 6148
  63.9 14.7 %copy-start.8 = (f32[128]{0:T(128)S(1)}, f32[128]{0:T(128)}, u32[]{:S(2)}) copy-start(f32[128]{0:T(128)} %param.17) | copy-start | bytes 1540
Sparse Core Ops, SparseCore 0:
  10.1 64.1 all-gather.1

commit v7 on v6

--- a/solution.py
+++ b/solution.py
@@ -12,6 +12,7 @@
 VMEM = pl.BlockSpec(memory_space=pltpu.VMEM)
 SMEM = pl.BlockSpec(memory_space=pltpu.SMEM)
 OTHER = 1000
+SLICES = 10000000000
 EARLY = 30000000000
 LATE = 1000
 FAR = 4
@@ -84,6 +85,27 @@
     products(out, (left_high[...], left_low[...]), (right_high, right_low), plus)
 
 
+def slices_kernel(*refs):
+    count = len(refs) - 4
+    pieces, (high, low, held, sems) = refs[:count], refs[count:]
+    width = held.shape[2]
+    made = start_all([(piece, held.at[k]) for k, piece in enumerate(pieces)], sems)
+    for k in range(count):
+        made[k].wait()
+        at = slice(k * width, (k + 1) * width)
+        high[:, at], low[:, at] = split(held[k])
+
+
+def other_kernel(first, left_high, left_low, high, low, out, lefts, rights, sems):
+    width = out.shape[2]
+    rows = pl.ds(first * width, rights.shape[1])
+    copies = [(left_high, lefts.at[0]), (left_low, lefts.at[1])]
+    copies += [(high.at[rows], rights.at[0]), (low.at[rows], rights.at[1])]
+    for copy in start_all(copies, sems):
+        copy.wait()
+    products(out, (lefts[0], lefts[1]), (rights.at[0], rights.at[1]))
+
+
 def factor_kernel(factor, stacked):
     tile = factor.shape[1]
     for i in range(factor.shape[0]):
@@ -185,7 +207,32 @@
             name=name,
         )(*pieces, high, low, *earlier)
 
-    other = swap(product(amp_cross, 1, "dressed_other", OTHER))
+    count = len(amp_cross)
+    slices = pl.pallas_call(
+        slices_kernel,
+        out_shape=[jax.ShapeDtypeStruct((rows, count * width), bf16)] * 2,
+        in_specs=[HBM] * count,
+        out_specs=[VMEM] * 2,
+        scratch_shapes=[pltpu.VMEM((count, rows, width), F32), sem((count,))],
+        compiler_params=PARAMS,
+        cost_estimate=pl.CostEstimate(flops=SLICES, bytes_accessed=1000000, transcendentals=0),
+        name="slices_ready",
+    )(*amp_cross)
+    other = pl.pallas_call(
+        lambda *refs: other_kernel(1, *refs),
+        out_shape=shape,
+        in_specs=[HBM] * 4,
+        out_specs=VMEM,
+        scratch_shapes=[
+            pltpu.VMEM((2, rows, count * width), bf16),
+            pltpu.VMEM((2, count * width, nx * width), bf16),
+            sem((4,)),
+        ],
+        compiler_params=PARAMS,
+        cost_estimate=pl.CostEstimate(flops=OTHER, bytes_accessed=1000000, transcendentals=0),
+        name="dressed_other",
+    )(*slices, high, low)
+    other = swap(other)
     early = product([amplitudes, *amp_same[:2]], 0, "dressed_early", EARLY)
     sums = product([amp_same[2], amp_far], 3, "dressed_late", LATE, early, other)
     sums = lax.all_to_all(sums, "x", 0, 0)

time: 86.9 us -> 85.2 us (0.980)
  waiting for transfers between devices: 16.2 us -> 12.9 us
  local copies, waits for them, and re-layouts: 0.99 us -> 2.64 us
    ppermute x7, waiting for transfers between devices: 3.38 us -> 0.02 us  [ring(): return lax.ppermute(value, names, pairs_of)]
    ppermute x7, starting transfers between devices: 33.3 us -> 31.2 us  [ring(): return lax.ppermute(value, names, pairs_of)]
    pallas_call x0 -> x2, Pallas kernels: none -> 2 us  [the longest x1 1.77 us: shards(): pl.pallas_call(lambda *refs: other_kernel(1, *refs), out_shape=shape, in_...]
    all_to_all x1, waiting for transfers between devices: 1.8 us -> 0.01 us  [shards(): sums = lax.all_to_all(sums, 'x', 0, 0)]
    all_gather x1, waiting for transfers between devices: 10.3 us -> 12 us  [shards(): gathered = lax.all_gather(blocks, ('y', 'core'), axis=0, tiled=True)]
    ppermute x1, starting transfers between devices: 2.63 us -> 4.29 us  [swap(): return lax.ppermute(value, 'core', [(0, 1), (1, 0)])]
    unnamed x23 -> x27, local copies, waits for them, and re-layouts: 0.83 us -> 2.48 us
    pallas_call x3 -> x2, Pallas kernels: 5.68 us -> 4.07 us  [product(): pl.pallas_call(lambda *refs: product_kernel(first, count, added, *refs),...]
  transfers between devices with their start and end apart: 11 -> 11, of which waited for: 4 -> 2; matrix products, arithmetic and copies ran while one was open for 1% -> 1% of each run, Pallas kernels for 10% -> 11%
where the time goes in v7:
time: 85.2 us; the launch traced here: 84.6 us
  starting transfers between devices  44.4 us (52%)
  between operations  14.3 us (17%)
  waiting for transfers between devices  12.9 us (15%)
  Pallas kernels  9.17 us (11%)
  local copies, waits for them, and re-layouts  2.64 us (3%)
  other arithmetic  1.13 us (1%)
    ppermute x7, starting transfers between devices, ring(): return lax.ppermute(value, names, pairs_of)  31.2 us
    all_gather x1, waiting for transfers between devices, shards(): gathered = lax.all_gather(blocks, ('y', 'core'), axis=0, tiled=True)  12 us
    all_to_all x1, starting transfers between devices, shards(): sums = lax.all_to_all(sums, 'x', 0, 0)  4.76 us
    ppermute x1, starting transfers between devices, swap(): return lax.ppermute(value, 'core', [(0, 1), (1, 0)])  4.29 us
    all_to_all x1, starting transfers between devices, shards(): panels = lax.all_to_all(dressing.reshape(nx, depth, width), 'x', 0, 0)  4.16 us
    pallas_call x2, Pallas kernels, product(): pl.pallas_call(lambda *refs: product_kernel(first, count, added, *refs),...  4.07 us
    pallas_call x1, Pallas kernels, shards(): pl.pallas_call(lambda *refs: integral_kernel(pairs, *refs), out_shape=jax...  2.58 us
    unnamed x27, local copies, waits for them, and re-layouts  2.48 us
  transfers between devices with their start and end apart: 11, of which 2 were waited for; matrix products, arithmetic and copies ran while one was open for 1% of the time, Pallas kernels for 11%

profile of v7, /device:TPU:1, one launch (start us, length us, event | category | flops | bytes accessed | tf_op | source)
XLA Modules:
  0.0 84.6 jit_solution(14950580204822180190)
XLA Ops:
  7.2 0.0 all-gather.2.cloned.1.call-start
  7.2 0.7 all-gather.2.cloned.1.call-update
  7.9 5.4 %collective-permute-start.4 = (f32[512,128]{1,0:T(8,128)}, f32[512,128]{1,0:T(8,128)S(1)}, u32[]{:S(2)}, u32[]{:S(2)}) collective-permute-start(f32[512,128]{1,0:T(8,128)} %refs_0_.1), channel_id=1, source_target_pairs={{32,1},{33,2},{34,3},{35,4},{36,5},{37,6},{38,7},{39,0},{0,39},{1,... | collective-permute-start | bytes 786440 | tf_op jit(solution)/shard_map/ppermute | solution.py:160
  13.3 0.0 copy-start.1
  13.3 4.2 %all-to-all-start = ((f32[4,1024,128]{2,1,0:T(8,128)}), f32[4,1024,128]{2,1,0:T(8,128)S(1)}, u32[]{:S(2)}, u32[]{:S(2)}) async-start(f32[4,1024,128]{2,1,0:T(8,128)} %bitcast.8), calls=%async_computation | async-start | bytes 4194304 | tf_op jit(solution)/shard_map/all_to_all | solution.py:179
  17.5 0.0 copy-done.1
  17.5 8.0 %collective-permute-start = (f32[512,128]{1,0:T(8,128)S(1)}, f32[512,128]{1,0:T(8,128)S(1)}, u32[]{:S(2)}, u32[]{:S(2)}) collective-permute-start(f32[512,128]{1,0:T(8,128)S(1)} %copy-done.1), channel_id=1, source_target_pairs={{0,1},{1,2},{2,3},{3,4},{4,5},{5,6},{6,7},{7,0},{32,39},{33,32},{3... | collective-permute-start | bytes 786440 | tf_op jit(solution)/shard_map/ppermute | solution.py:160
  25.5 0.0 collective-permute-done.4.refs_0_
  25.5 3.9 %collective-permute-start.5 = (f32[512,128]{1,0:T(8,128)S(1)}, f32[512,128]{1,0:T(8,128)S(1)}, u32[]{:S(2)}, u32[]{:S(2)}) collective-permute-start(f32[512,128]{1,0:T(8,128)S(1)} %collective-permute-done.4.refs_0_), channel_id=1, source_target_pairs={{0,1},{1,2},{2,3},{3,4},{4,5},{5,6},{6,7},{7,0},{32,39},{33,32},{3... | collective-permute-start | bytes 786440 | tf_op jit(solution)/shard_map/ppermute | solution.py:160
  29.4 0.0 copy-start.6
  29.4 0.7 copy-done.6
  30.1 0.0 collective-permute-done.refs_1_
  30.1 4.0 %collective-permute-start.1 = (f32[512,128]{1,0:T(8,128)S(1)}, f32[512,128]{1,0:T(8,128)}, u32[]{:S(2)}, u32[]{:S(2)}) collective-permute-start(f32[512,128]{1,0:T(8,128)S(1)} %collective-permute-done.refs_1_), channel_id=1, source_target_pairs={{0,1},{1,2},{2,3},{3,4},{4,5},{5,6},{6,7},{7,0},{32,39},{33,32},{3... | collective-permute-start | bytes 786440 | tf_op jit(solution)/shard_map/ppermute | solution.py:160
  34.1 0.0 copy-start.4
  34.1 0.7 copy-done.4
  34.8 0.0 collective-permute-done.5.refs_1_
  34.8 3.2 %collective-permute-start.6 = (f32[512,128]{1,0:T(8,128)S(1)}, f32[512,128]{1,0:T(8,128)S(1)}, u32[]{:S(2)}, u32[]{:S(2)}) collective-permute-start(f32[512,128]{1,0:T(8,128)S(1)} %collective-permute-done.5.refs_1_), channel_id=1, source_target_pairs={{0,1},{1,2},{2,3},{3,4},{4,5},{5,6},{6,7},{7,0},{32,39},{33,32},{3... | collective-permute-start | bytes 786440 | tf_op jit(solution)/shard_map/ppermute | solution.py:160
  38.0 0.0 collective-permute-done.1.refs_2_
  38.1 4.8 %collective-permute-start.2 = (f32[512,128]{1,0:T(8,128)}, f32[512,128]{1,0:T(8,128)S(1)}, u32[]{:S(2)}, u32[]{:S(2)}) collective-permute-start(f32[512,128]{1,0:T(8,128)} %collective-permute-done.1.refs_2_), channel_id=1, source_target_pairs={{0,1},{1,2},{2,3},{3,4},{4,5},{5,6},{6,7},{7,0},{32,39},{33,32},{3... | collective-permute-start | bytes 786440 | tf_op jit(solution)/shard_map/ppermute | solution.py:160
  42.8 1.9 %collective-permute-start.3 = (f32[512,128]{1,0:T(8,128)}, f32[512,128]{1,0:T(8,128)S(1)}, u32[]{:S(2)}, u32[]{:S(2)}) collective-permute-start(f32[512,128]{1,0:T(8,128)} %collective-permute-done.1.refs_2_), channel_id=1, source_target_pairs={{0,2},{1,3},{2,4},{3,5},{4,6},{5,7},{6,0},{7,1},{32,38},{33,39},{3... | collective-permute-start | bytes 786440 | tf_op jit(solution)/shard_map/ppermute | solution.py:160
  44.7 0.0 collective-permute-done.6.refs_2_
  44.8 0.0 copy-start.7
  44.8 0.9 %copy-done.7 = f32[512,128]{1,0:T(8,128)S(1)} copy-done((f32[512,128]{1,0:T(8,128)S(1)}, f32[512,128]{1,0:T(8,128)}, u32[]{:S(2)}) %copy-start.7) | copy-done | bytes 262168
  45.7 0.2 slices_ready.1
  46.0 0.0 all-to-all-done.refs_0_
  46.0 0.4 dressing_ready.1
  46.4 0.0 copy-start.2
  46.4 0.0 copy-start.5
  46.4 1.8 %dressed_other.1 = f32[4,512,128]{2,1,0:T(8,128)S(1)} custom-call(bf16[512,384]{1,0:T(8,128)(2,1)S(1)} %get-tuple-element.8.refs_0_, bf16[512,384]{1,0:T(8,128)(2,1)S(1)} %get-tuple-element.9.refs_1_, bf16[640,512]{1,0:T(8,128)(2,1)S(1)} %get-tuple-element.6.refs_3_.refs_2_, bf16[640,512]{1,0:T(8,128)(2,1)S(1)} %get-tuple-element.7.refs_4_.refs_3_), custom_call_target="tpu_custom_call" | custom-call | flops 1000 | bytes 1000000 | tf_op jit(solution)/shard_map/dressed_other/pallas_call | solution.py:221
  48.2 4.3 %collective-permute-start.7 = (f32[4,512,128]{2,1,0:T(8,128)S(1)}, f32[4,512,128]{2,1,0:T(8,128)S(1)}, u32[]{:S(2)}, u32[]{:S(2)}) collective-permute-start(f32[4,512,128]{2,1,0:T(8,128)S(1)} %dressed_other.1), channel_id=1, source_target_pairs={{0,32},{32,0},{1,33},{33,1},{2,34},{34,2},{3,35},{35,3},{4,36},{36... | collective-permute-start | bytes 3145736 | tf_op jit(solution)/shard_map/ppermute | solution.py:163
  52.5 0.0 copy-done.2
  52.5 0.0 copy-done.5
  52.5 2.1 %dressed_early.1.refs_4_ = f32[4,512,128]{2,1,0:T(8,128)S(1)} custom-call(f32[512,128]{1,0:T(8,128)S(1)} %copy-done.2, f32[512,128]{1,0:T(8,128)S(1)} %copy-done.5, f32[512,128]{1,0:T(8,128)} %collective-permute-done.1.refs_2_, bf16[640,512]{1,0:T(8,128)(2,1)S(1)} %get-tuple-element.6.refs_3_.refs_2_, bf16[640,512]{1,0:T(8,128)(2,1)S(1)} %get-tuple-element.7.refs_4_.refs_3_), custom_call_target="tpu_custom_call" | custom-call | flops 30000001024 | bytes 1000000 | tf_op jit(solution)/shard_map/dressed_early/pallas_call | solution.py:195
  54.6 0.0 collective-permute-done.2.refs_0_
  54.6 0.0 collective-permute-done.3.refs_1_
  54.6 0.2 collective-permute-done.7.refs_5_
  54.8 2.0 %dressed_late.1 = f32[4,512,128]{2,1,0:T(8,128)} custom-call(f32[512,128]{1,0:T(8,128)S(1)} %collective-permute-done.2.refs_0_, f32[512,128]{1,0:T(8,128)S(1)} %collective-permute-done.3.refs_1_, bf16[640,512]{1,0:T(8,128)(2,1)S(1)} %get-tuple-element.6.refs_3_.refs_2_, bf16[640,512]{1,0:T(8,128)(2,1)S(1)} %get-tuple-element.7.refs_4_.refs_3_, ...), custom_call_target="tpu_custom_call" | custom-call | flops 1000 | bytes 1000000 | tf_op jit(solution)/shard_map/dressed_late/pallas_call | solution.py:195
  56.8 0.0 copy-start.9
  56.8 0.0 copy-start
  56.8 0.0 copy-start.11
  56.8 0.0 copy-start.12
  56.8 4.8 %all-to-all-start.1 = ((f32[4,512,128]{2,1,0:T(8,128)}), f32[4,512,128]{2,1,0:T(8,128)S(1)}, u32[]{:S(2)}, u32[]{:S(2)}) async-start(f32[4,512,128]{2,1,0:T(8,128)} %dressed_late.1), calls=%async_computation.1 | async-start | bytes 2097152 | tf_op jit(solution)/shard_map/all_to_all | solution.py:238
  61.6 0.0 copy-done.9
  61.6 0.1 copy.14
  61.7 0.1 reshape.16
  61.7 0.0 copy-done
  61.7 0.1 factor_ready.1.refs_1_
  61.9 0.0 copy-done.11
  61.9 0.1 dynamic_slice.3
  62.0 0.0 copy-done.12
  62.0 0.2 select_reduce_fusion
  62.2 0.1 pad_add_fusion.refs_0_
  62.2 0.0 copy-start.3
  62.2 0.0 copy-start.8
  62.2 0.0 copy-start.10
  62.2 12.0 %all-gather.2.cloned.1.call-done.refs_2_ = f32[32,512,128]{2,1,0:T(8,128)} async-done(((f32[2,512,128]{2,1,0:T(8,128)}), f32[32,512,128]{2,1,0:T(8,128)}) %all-gather.2.cloned.1.call-update) | async-done | bytes 8388624 | tf_op jit(solution)/shard_map/all_gather | solution.py:172
  74.3 2.6 %integral.1 = f32[512,128]{1,0:T(8,128)S(1)} custom-call(s32[24]{0:T(128)S(1)} %pad_add_fusion.refs_0_, bf16[8,128,512]{2,1,0:T(8,128)(2,1)S(1)} %factor_ready.1.refs_1_, f32[32,512,128]{2,1,0:T(8,128)} %all-gather.2.cloned.1.call-done.refs_2_), custom_call_target="tpu_custom_call" | custom-call | tf_op jit(solution)/shard_map/integral/pallas_call | solution.py:253
  76.9 0.0 all-to-all-done.1
  76.9 0.0 copy-done.3
  76.9 0.0 copy-done.8
  76.9 0.0 copy-done.10
  76.9 0.9 %divide_subtract_fusion = (f32[512,128]{1,0:T(8,128)}, f32[512,128]{1,0:T(8,128)}) fusion(f32[512,128]{1,0:T(8,128)S(1)} %copy-done.3, f32[128]{0:T(128)S(1)} %copy-done.10, f32[512]{0:T(512)S(1)} %copy-done.8, f32[512,128]{1,0:T(8,128)S(1)} %integral.1, f32[4,512,128]{2,1,0:T(8,128)S(1)} %all-to-all-done.1), kind=kLoop, calls=%fused_computation.5 | loop fusion | flops 458752 | bytes 2099712 | tf_op jit(solution)/shard_map/sub | solution.py:267
Async XLA Ops:
  7.2 67.1 %all-gather.2.cloned.1.call-start = ((), (), s32[]{:S(2)}) async-start(), calls=%async_computation.2 | async-start | bytes 8912896 | tf_op jit(solution)/shard_map/all_gather | solution.py:172
  7.9 17.6 %collective-permute-start.4 = (f32[512,128]{1,0:T(8,128)}, f32[512,128]{1,0:T(8,128)S(1)}, u32[]{:S(2)}, u32[]{:S(2)}) collective-permute-start(f32[512,128]{1,0:T(8,128)} %refs_0_.1), channel_id=1, source_target_pairs={{32,1},{33,2},{34,3},{35,4},{36,5},{37,6},{38,7},{39,0},{0,39},{1,... | collective-permute-start | bytes 786440 | tf_op jit(solution)/shard_map/ppermute | solution.py:160
  13.3 4.2 %copy-start.1 = (f32[512,128]{1,0:T(8,128)S(1)}, f32[512,128]{1,0:T(8,128)}, u32[]{:S(2)}) copy-start(f32[512,128]{1,0:T(8,128)} %refs_0_.1) | copy-start | bytes 786436
  13.3 32.7 %all-to-all-start = ((f32[4,1024,128]{2,1,0:T(8,128)}), f32[4,1024,128]{2,1,0:T(8,128)S(1)}, u32[]{:S(2)}, u32[]{:S(2)}) async-start(f32[4,1024,128]{2,1,0:T(8,128)} %bitcast.8), calls=%async_computation | async-start | bytes 4194304 | tf_op jit(solution)/shard_map/all_to_all | solution.py:179
  17.5 12.7 %collective-permute-start = (f32[512,128]{1,0:T(8,128)S(1)}, f32[512,128]{1,0:T(8,128)S(1)}, u32[]{:S(2)}, u32[]{:S(2)}) collective-permute-start(f32[512,128]{1,0:T(8,128)S(1)} %copy-done.1), channel_id=1, source_target_pairs={{0,1},{1,2},{2,3},{3,4},{4,5},{5,6},{6,7},{7,0},{32,39},{33,32},{3... | collective-permute-start | bytes 786440 | tf_op jit(solution)/shard_map/ppermute | solution.py:160
  25.5 9.3 %collective-permute-start.5 = (f32[512,128]{1,0:T(8,128)S(1)}, f32[512,128]{1,0:T(8,128)S(1)}, u32[]{:S(2)}, u32[]{:S(2)}) collective-permute-start(f32[512,128]{1,0:T(8,128)S(1)} %collective-permute-done.4.refs_0_), channel_id=1, source_target_pairs={{0,1},{1,2},{2,3},{3,4},{4,5},{5,6},{6,7},{7,0},{32,39},{33,32},{3... | collective-permute-start | bytes 786440 | tf_op jit(solution)/shard_map/ppermute | solution.py:160
  29.4 0.7 copy-start.6
  30.1 7.9 %collective-permute-start.1 = (f32[512,128]{1,0:T(8,128)S(1)}, f32[512,128]{1,0:T(8,128)}, u32[]{:S(2)}, u32[]{:S(2)}) collective-permute-start(f32[512,128]{1,0:T(8,128)S(1)} %collective-permute-done.refs_1_), channel_id=1, source_target_pairs={{0,1},{1,2},{2,3},{3,4},{4,5},{5,6},{6,7},{7,0},{32,39},{33,32},{3... | collective-permute-start | bytes 786440 | tf_op jit(solution)/shard_map/ppermute | solution.py:160
  34.1 0.7 copy-start.4
  34.8 9.9 %collective-permute-start.6 = (f32[512,128]{1,0:T(8,128)S(1)}, f32[512,128]{1,0:T(8,128)S(1)}, u32[]{:S(2)}, u32[]{:S(2)}) collective-permute-start(f32[512,128]{1,0:T(8,128)S(1)} %collective-permute-done.5.refs_1_), channel_id=1, source_target_pairs={{0,1},{1,2},{2,3},{3,4},{4,5},{5,6},{6,7},{7,0},{32,39},{33,32},{3... | collective-permute-start | bytes 786440 | tf_op jit(solution)/shard_map/ppermute | solution.py:160
  38.1 16.5 %collective-permute-start.2 = (f32[512,128]{1,0:T(8,128)}, f32[512,128]{1,0:T(8,128)S(1)}, u32[]{:S(2)}, u32[]{:S(2)}) collective-permute-start(f32[512,128]{1,0:T(8,128)} %collective-permute-done.1.refs_2_), channel_id=1, source_target_pairs={{0,1},{1,2},{2,3},{3,4},{4,5},{5,6},{6,7},{7,0},{32,39},{33,32},{3... | collective-permute-start | bytes 786440 | tf_op jit(solution)/shard_map/ppermute | solution.py:160
  42.8 11.7 %collective-permute-start.3 = (f32[512,128]{1,0:T(8,128)}, f32[512,128]{1,0:T(8,128)S(1)}, u32[]{:S(2)}, u32[]{:S(2)}) collective-permute-start(f32[512,128]{1,0:T(8,128)} %collective-permute-done.1.refs_2_), channel_id=1, source_target_pairs={{0,2},{1,3},{2,4},{3,5},{4,6},{5,7},{6,0},{7,1},{32,38},{33,39},{3... | collective-permute-start | bytes 786440 | tf_op jit(solution)/shard_map/ppermute | solution.py:160
  44.8 1.0 %copy-start.7 = (f32[512,128]{1,0:T(8,128)S(1)}, f32[512,128]{1,0:T(8,128)}, u32[]{:S(2)}) copy-start(f32[512,128]{1,0:T(8,128)} %copy-done.6) | copy-start | bytes 786436
  46.4 6.1 %copy-start.2 = (f32[512,128]{1,0:T(8,128)S(1)}, f32[512,128]{1,0:T(8,128)}, u32[]{:S(2)}) copy-start(f32[512,128]{1,0:T(8,128)} %refs_0_.1) | copy-start | bytes 786436
  46.4 6.1 %copy-start.5 = (f32[512,128]{1,0:T(8,128)S(1)}, f32[512,128]{1,0:T(8,128)}, u32[]{:S(2)}) copy-start(f32[512,128]{1,0:T(8,128)} %copy-done.4) | copy-start | bytes 786436
  48.2 6.6 %collective-permute-start.7 = (f32[4,512,128]{2,1,0:T(8,128)S(1)}, f32[4,512,128]{2,1,0:T(8,128)S(1)}, u32[]{:S(2)}, u32[]{:S(2)}) collective-permute-start(f32[4,512,128]{2,1,0:T(8,128)S(1)} %dressed_other.1), channel_id=1, source_target_pairs={{0,32},{32,0},{1,33},{33,1},{2,34},{34,2},{3,35},{35,3},{4,36},{36... | collective-permute-start | bytes 3145736 | tf_op jit(solution)/shard_map/ppermute | solution.py:163
  56.8 4.8 %copy-start.9 = (s32[8,2]{0,1:T(2,128)S(1)}, s32[8,2]{0,1:T(2,128)}, u32[]{:S(2)}) copy-start(s32[8,2]{0,1:T(2,128)} %param.15) | copy-start | bytes 196
  56.8 5.0 %copy-start = (f32[8,512,64]{1,2,0:T(8,128)S(1)}, f32[8,512,64]{1,2,0:T(8,128)}, u32[]{:S(2)}) copy-start(f32[8,512,64]{1,2,0:T(8,128)} %param.11) | copy-start | bytes 3145732
  56.8 5.1 %copy-start.11 = (s32[128]{0:T(128)S(1)}, s32[128]{0:T(128)}, u32[]{:S(2)}) copy-start(s32[128]{0:T(128)} %param.13) | copy-start | bytes 1540
  56.8 5.2 %copy-start.12 = (s32[32]{0:T(128)S(1)}, s32[32]{0:T(128)}, u32[]{:S(2)}) copy-start(s32[32]{0:T(128)} %param.14) | copy-start | bytes 388
  56.8 20.0 %all-to-all-start.1 = ((f32[4,512,128]{2,1,0:T(8,128)}), f32[4,512,128]{2,1,0:T(8,128)S(1)}, u32[]{:S(2)}, u32[]{:S(2)}) async-start(f32[4,512,128]{2,1,0:T(8,128)} %dressed_late.1), calls=%async_computation.1 | async-start | bytes 2097152 | tf_op jit(solution)/shard_map/all_to_all | solution.py:238
  62.2 14.6 %copy-start.3 = (f32[512,128]{1,0:T(8,128)S(1)}, f32[512,128]{1,0:T(8,128)}, u32[]{:S(2)}) copy-start(f32[512,128]{1,0:T(8,128)} %refs_0_.1) | copy-start | bytes 786436
  62.2 14.7 %copy-start.8 = (f32[512]{0:T(512)S(1)}, f32[512]{0:T(512)}, u32[]{:S(2)}) copy-start(f32[512]{0:T(512)} %param.16) | copy-start | bytes 6148
  62.2 14.7 %copy-start.10 = (f32[128]{0:T(128)S(1)}, f32[128]{0:T(128)}, u32[]{:S(2)}) copy-start(f32[128]{0:T(128)} %param.17) | copy-start | bytes 1540
Sparse Core Ops, SparseCore 0:
  10.1 64.1 all-gather.1

commit v8 on v7

--- a/solution.py
+++ b/solution.py
@@ -118,10 +118,12 @@
     return gathered.at[home]
 
 
-def integral_kernel(pairs, where, stacked, gathered, out, factors, blocks, sems):
-    made = start_all(
-        [(block_at(gathered, where[i]), blocks.at[i]) for i in range(pairs)] + [(stacked, factors)], sems
-    )
+def integral_kernel(pairs, where, factors, gathered, out, blocks, sems):
+    made = [
+        pltpu.make_async_copy(block_at(gathered, where[i]), blocks.at[i], sems.at[i]) for i in range(pairs)
+    ]
+    for i in range(pairs):
+        made[i].start(priority=i % 2)
     for copy in made:
         copy.wait()
     tile = factors.shape[1] // 2
@@ -253,13 +255,13 @@
     integral = pl.pallas_call(
         lambda *refs: integral_kernel(pairs, *refs),
         out_shape=jax.ShapeDtypeStruct((rows, width), F32),
-        in_specs=[SMEM, HBM, HBM],
-        out_specs=VMEM,
-        scratch_shapes=[
-            pltpu.VMEM((pairs, 2 * tile, naux), bf16),
-            pltpu.VMEM((pairs, naux, width), F32),
-            sem((pairs + 1,)),
-        ],
+        grid_spec=pltpu.PrefetchScalarGridSpec(
+            num_scalar_prefetch=1,
+            grid=(),
+            in_specs=[VMEM, HBM],
+            out_specs=VMEM,
+            scratch_shapes=[pltpu.VMEM((pairs, naux, width), F32), sem((pairs,))],
+        ),
         compiler_params=pltpu.CompilerParams(vmem_limit_bytes=48 * 1024 * 1024),
         name="integral",
     )(where, stacked, gathered)

time: 85.2 us -> 85.2 us (level)
  no operation moved by 1% of the time
where the time goes in v8:
time: 85.2 us; the launch traced here: 84.6 us
  starting transfers between devices  44.4 us (52%)
  between operations  14.3 us (17%)
  waiting for transfers between devices  12.9 us (15%)
  Pallas kernels  9.16 us (11%)
  local copies, waits for them, and re-layouts  2.64 us (3%)
  other arithmetic  1.13 us (1%)
    ppermute x7, starting transfers between devices, ring(): return lax.ppermute(value, names, pairs_of)  31.2 us
    all_gather x1, waiting for transfers between devices, shards(): gathered = lax.all_gather(blocks, ('y', 'core'), axis=0, tiled=True)  12 us
    all_to_all x1, starting transfers between devices, shards(): sums = lax.all_to_all(sums, 'x', 0, 0)  4.76 us
    ppermute x1, starting transfers between devices, swap(): return lax.ppermute(value, 'core', [(0, 1), (1, 0)])  4.29 us
    all_to_all x1, starting transfers between devices, shards(): panels = lax.all_to_all(dressing.reshape(nx, depth, width), 'x', 0, 0)  4.16 us
    pallas_call x2, Pallas kernels, product(): pl.pallas_call(lambda *refs: product_kernel(first, count, added, *refs),...  4.07 us
    pallas_call x1, Pallas kernels, shards(): pl.pallas_call(lambda *refs: integral_kernel(pairs, *refs), out_shape=jax...  2.57 us
    unnamed x27, local copies, waits for them, and re-layouts  2.48 us
  transfers between devices with their start and end apart: 11, of which 2 were waited for; matrix products, arithmetic and copies ran while one was open for 1% of the time, Pallas kernels for 11%

profile of v8, /device:TPU:1, one launch (start us, length us, event | category | flops | bytes accessed | tf_op | source)
XLA Modules:
  0.0 84.6 jit_solution(17798694023622386788)
XLA Ops:
  7.2 0.0 all-gather.2.cloned.1.call-start
  7.2 0.7 all-gather.2.cloned.1.call-update
  7.9 5.4 %collective-permute-start.4 = (f32[512,128]{1,0:T(8,128)}, f32[512,128]{1,0:T(8,128)S(1)}, u32[]{:S(2)}, u32[]{:S(2)}) collective-permute-start(f32[512,128]{1,0:T(8,128)} %refs_0_.1), channel_id=1, source_target_pairs={{32,1},{33,2},{34,3},{35,4},{36,5},{37,6},{38,7},{39,0},{0,39},{1,... | collective-permute-start | bytes 786440 | tf_op jit(solution)/shard_map/ppermute | solution.py:162
  13.3 0.0 copy-start.1
  13.3 4.2 %all-to-all-start = ((f32[4,1024,128]{2,1,0:T(8,128)}), f32[4,1024,128]{2,1,0:T(8,128)S(1)}, u32[]{:S(2)}, u32[]{:S(2)}) async-start(f32[4,1024,128]{2,1,0:T(8,128)} %bitcast.8), calls=%async_computation | async-start | bytes 4194304 | tf_op jit(solution)/shard_map/all_to_all | solution.py:181
  17.5 0.0 copy-done.1
  17.5 8.0 %collective-permute-start = (f32[512,128]{1,0:T(8,128)S(1)}, f32[512,128]{1,0:T(8,128)S(1)}, u32[]{:S(2)}, u32[]{:S(2)}) collective-permute-start(f32[512,128]{1,0:T(8,128)S(1)} %copy-done.1), channel_id=1, source_target_pairs={{0,1},{1,2},{2,3},{3,4},{4,5},{5,6},{6,7},{7,0},{32,39},{33,32},{3... | collective-permute-start | bytes 786440 | tf_op jit(solution)/shard_map/ppermute | solution.py:162
  25.5 0.0 collective-permute-done.4.refs_0_
  25.5 3.9 %collective-permute-start.5 = (f32[512,128]{1,0:T(8,128)S(1)}, f32[512,128]{1,0:T(8,128)S(1)}, u32[]{:S(2)}, u32[]{:S(2)}) collective-permute-start(f32[512,128]{1,0:T(8,128)S(1)} %collective-permute-done.4.refs_0_), channel_id=1, source_target_pairs={{0,1},{1,2},{2,3},{3,4},{4,5},{5,6},{6,7},{7,0},{32,39},{33,32},{3... | collective-permute-start | bytes 786440 | tf_op jit(solution)/shard_map/ppermute | solution.py:162
  29.4 0.0 copy-start.6
  29.4 0.7 copy-done.6
  30.1 0.0 collective-permute-done.refs_1_
  30.1 4.0 %collective-permute-start.1 = (f32[512,128]{1,0:T(8,128)S(1)}, f32[512,128]{1,0:T(8,128)}, u32[]{:S(2)}, u32[]{:S(2)}) collective-permute-start(f32[512,128]{1,0:T(8,128)S(1)} %collective-permute-done.refs_1_), channel_id=1, source_target_pairs={{0,1},{1,2},{2,3},{3,4},{4,5},{5,6},{6,7},{7,0},{32,39},{33,32},{3... | collective-permute-start | bytes 786440 | tf_op jit(solution)/shard_map/ppermute | solution.py:162
  34.1 0.0 copy-start.4
  34.1 0.7 copy-done.4
  34.8 0.0 collective-permute-done.5.refs_1_
  34.8 3.2 %collective-permute-start.6 = (f32[512,128]{1,0:T(8,128)S(1)}, f32[512,128]{1,0:T(8,128)S(1)}, u32[]{:S(2)}, u32[]{:S(2)}) collective-permute-start(f32[512,128]{1,0:T(8,128)S(1)} %collective-permute-done.5.refs_1_), channel_id=1, source_target_pairs={{0,1},{1,2},{2,3},{3,4},{4,5},{5,6},{6,7},{7,0},{32,39},{33,32},{3... | collective-permute-start | bytes 786440 | tf_op jit(solution)/shard_map/ppermute | solution.py:162
  38.0 0.0 collective-permute-done.1.refs_2_
  38.1 4.8 %collective-permute-start.2 = (f32[512,128]{1,0:T(8,128)}, f32[512,128]{1,0:T(8,128)S(1)}, u32[]{:S(2)}, u32[]{:S(2)}) collective-permute-start(f32[512,128]{1,0:T(8,128)} %collective-permute-done.1.refs_2_), channel_id=1, source_target_pairs={{0,1},{1,2},{2,3},{3,4},{4,5},{5,6},{6,7},{7,0},{32,39},{33,32},{3... | collective-permute-start | bytes 786440 | tf_op jit(solution)/shard_map/ppermute | solution.py:162
  42.8 1.9 %collective-permute-start.3 = (f32[512,128]{1,0:T(8,128)}, f32[512,128]{1,0:T(8,128)S(1)}, u32[]{:S(2)}, u32[]{:S(2)}) collective-permute-start(f32[512,128]{1,0:T(8,128)} %collective-permute-done.1.refs_2_), channel_id=1, source_target_pairs={{0,2},{1,3},{2,4},{3,5},{4,6},{5,7},{6,0},{7,1},{32,38},{33,39},{3... | collective-permute-start | bytes 786440 | tf_op jit(solution)/shard_map/ppermute | solution.py:162
  44.7 0.0 collective-permute-done.6.refs_2_
  44.8 0.0 copy-start.7
  44.8 0.9 %copy-done.7 = f32[512,128]{1,0:T(8,128)S(1)} copy-done((f32[512,128]{1,0:T(8,128)S(1)}, f32[512,128]{1,0:T(8,128)}, u32[]{:S(2)}) %copy-start.7) | copy-done | bytes 262168
  45.7 0.2 slices_ready.1
  46.0 0.0 all-to-all-done.refs_0_
  46.0 0.4 dressing_ready.1
  46.4 0.0 copy-start.2
  46.4 0.0 copy-start.5
  46.4 1.8 %dressed_other.1 = f32[4,512,128]{2,1,0:T(8,128)S(1)} custom-call(bf16[512,384]{1,0:T(8,128)(2,1)S(1)} %get-tuple-element.8.refs_0_, bf16[512,384]{1,0:T(8,128)(2,1)S(1)} %get-tuple-element.9.refs_1_, bf16[640,512]{1,0:T(8,128)(2,1)S(1)} %get-tuple-element.6.refs_3_.refs_2_, bf16[640,512]{1,0:T(8,128)(2,1)S(1)} %get-tuple-element.7.refs_4_.refs_3_), custom_call_target="tpu_custom_call" | custom-call | flops 1000 | bytes 1000000 | tf_op jit(solution)/shard_map/dressed_other/pallas_call | solution.py:223
  48.2 4.3 %collective-permute-start.7 = (f32[4,512,128]{2,1,0:T(8,128)S(1)}, f32[4,512,128]{2,1,0:T(8,128)S(1)}, u32[]{:S(2)}, u32[]{:S(2)}) collective-permute-start(f32[4,512,128]{2,1,0:T(8,128)S(1)} %dressed_other.1), channel_id=1, source_target_pairs={{0,32},{32,0},{1,33},{33,1},{2,34},{34,2},{3,35},{35,3},{4,36},{36... | collective-permute-start | bytes 3145736 | tf_op jit(solution)/shard_map/ppermute | solution.py:165
  52.5 0.0 copy-done.2
  52.5 0.0 copy-done.5
  52.5 2.1 %dressed_early.1.refs_4_ = f32[4,512,128]{2,1,0:T(8,128)S(1)} custom-call(f32[512,128]{1,0:T(8,128)S(1)} %copy-done.2, f32[512,128]{1,0:T(8,128)S(1)} %copy-done.5, f32[512,128]{1,0:T(8,128)} %collective-permute-done.1.refs_2_, bf16[640,512]{1,0:T(8,128)(2,1)S(1)} %get-tuple-element.6.refs_3_.refs_2_, bf16[640,512]{1,0:T(8,128)(2,1)S(1)} %get-tuple-element.7.refs_4_.refs_3_), custom_call_target="tpu_custom_call" | custom-call | flops 30000001024 | bytes 1000000 | tf_op jit(solution)/shard_map/dressed_early/pallas_call | solution.py:197
  54.6 0.0 collective-permute-done.2.refs_0_
  54.6 0.0 collective-permute-done.3.refs_1_
  54.6 0.2 collective-permute-done.7.refs_5_
  54.8 2.0 %dressed_late.1 = f32[4,512,128]{2,1,0:T(8,128)} custom-call(f32[512,128]{1,0:T(8,128)S(1)} %collective-permute-done.2.refs_0_, f32[512,128]{1,0:T(8,128)S(1)} %collective-permute-done.3.refs_1_, bf16[640,512]{1,0:T(8,128)(2,1)S(1)} %get-tuple-element.6.refs_3_.refs_2_, bf16[640,512]{1,0:T(8,128)(2,1)S(1)} %get-tuple-element.7.refs_4_.refs_3_, ...), custom_call_target="tpu_custom_call" | custom-call | flops 1000 | bytes 1000000 | tf_op jit(solution)/shard_map/dressed_late/pallas_call | solution.py:197
  56.8 0.0 copy-start.9
  56.8 0.0 copy-start
  56.8 0.0 copy-start.11
  56.8 0.0 copy-start.12
  56.8 4.8 %all-to-all-start.1 = ((f32[4,512,128]{2,1,0:T(8,128)}), f32[4,512,128]{2,1,0:T(8,128)S(1)}, u32[]{:S(2)}, u32[]{:S(2)}) async-start(f32[4,512,128]{2,1,0:T(8,128)} %dressed_late.1), calls=%async_computation.1 | async-start | bytes 2097152 | tf_op jit(solution)/shard_map/all_to_all | solution.py:240
  61.6 0.0 copy-done.9
  61.6 0.1 copy.14
  61.7 0.1 reshape.16
  61.7 0.0 copy-done
  61.7 0.1 factor_ready.1.refs_1_
  61.9 0.0 copy-done.11
  61.9 0.1 dynamic_slice.3
  62.0 0.0 copy-done.12
  62.0 0.2 select_reduce_fusion
  62.2 0.1 pad_add_fusion.refs_0_
  62.2 0.0 copy-start.3
  62.2 0.0 copy-start.8
  62.2 0.0 copy-start.10
  62.2 12.0 %all-gather.2.cloned.1.call-done.refs_2_ = f32[32,512,128]{2,1,0:T(8,128)} async-done(((f32[2,512,128]{2,1,0:T(8,128)}), f32[32,512,128]{2,1,0:T(8,128)}) %all-gather.2.cloned.1.call-update) | async-done | bytes 8388624 | tf_op jit(solution)/shard_map/all_gather | solution.py:174
  74.3 2.6 %integral.1 = f32[512,128]{1,0:T(8,128)S(1)} custom-call(s32[24]{0:T(128)S(1)} %pad_add_fusion.refs_0_, bf16[8,128,512]{2,1,0:T(8,128)(2,1)S(1)} %factor_ready.1.refs_1_, f32[32,512,128]{2,1,0:T(8,128)} %all-gather.2.cloned.1.call-done.refs_2_), custom_call_target="tpu_custom_call" | custom-call | tf_op jit(solution)/shard_map/integral/pallas_call | solution.py:255
  76.9 0.0 all-to-all-done.1
  76.9 0.0 copy-done.3
  76.9 0.0 copy-done.8
  76.9 0.0 copy-done.10
  76.9 0.9 %divide_subtract_fusion = (f32[512,128]{1,0:T(8,128)}, f32[512,128]{1,0:T(8,128)}) fusion(f32[512,128]{1,0:T(8,128)S(1)} %copy-done.3, f32[128]{0:T(128)S(1)} %copy-done.10, f32[512]{0:T(512)S(1)} %copy-done.8, f32[512,128]{1,0:T(8,128)S(1)} %integral.1, f32[4,512,128]{2,1,0:T(8,128)S(1)} %all-to-all-done.1), kind=kLoop, calls=%fused_computation.5 | loop fusion | flops 458752 | bytes 2099712 | tf_op jit(solution)/shard_map/sub | solution.py:269
Async XLA Ops:
  7.2 67.1 %all-gather.2.cloned.1.call-start = ((), (), s32[]{:S(2)}) async-start(), calls=%async_computation.2 | async-start | bytes 8912896 | tf_op jit(solution)/shard_map/all_gather | solution.py:174
  7.9 17.6 %collective-permute-start.4 = (f32[512,128]{1,0:T(8,128)}, f32[512,128]{1,0:T(8,128)S(1)}, u32[]{:S(2)}, u32[]{:S(2)}) collective-permute-start(f32[512,128]{1,0:T(8,128)} %refs_0_.1), channel_id=1, source_target_pairs={{32,1},{33,2},{34,3},{35,4},{36,5},{37,6},{38,7},{39,0},{0,39},{1,... | collective-permute-start | bytes 786440 | tf_op jit(solution)/shard_map/ppermute | solution.py:162
  13.3 4.2 %copy-start.1 = (f32[512,128]{1,0:T(8,128)S(1)}, f32[512,128]{1,0:T(8,128)}, u32[]{:S(2)}) copy-start(f32[512,128]{1,0:T(8,128)} %refs_0_.1) | copy-start | bytes 786436
  13.3 32.7 %all-to-all-start = ((f32[4,1024,128]{2,1,0:T(8,128)}), f32[4,1024,128]{2,1,0:T(8,128)S(1)}, u32[]{:S(2)}, u32[]{:S(2)}) async-start(f32[4,1024,128]{2,1,0:T(8,128)} %bitcast.8), calls=%async_computation | async-start | bytes 4194304 | tf_op jit(solution)/shard_map/all_to_all | solution.py:181
  17.5 12.7 %collective-permute-start = (f32[512,128]{1,0:T(8,128)S(1)}, f32[512,128]{1,0:T(8,128)S(1)}, u32[]{:S(2)}, u32[]{:S(2)}) collective-permute-start(f32[512,128]{1,0:T(8,128)S(1)} %copy-done.1), channel_id=1, source_target_pairs={{0,1},{1,2},{2,3},{3,4},{4,5},{5,6},{6,7},{7,0},{32,39},{33,32},{3... | collective-permute-start | bytes 786440 | tf_op jit(solution)/shard_map/ppermute | solution.py:162
  25.5 9.3 %collective-permute-start.5 = (f32[512,128]{1,0:T(8,128)S(1)}, f32[512,128]{1,0:T(8,128)S(1)}, u32[]{:S(2)}, u32[]{:S(2)}) collective-permute-start(f32[512,128]{1,0:T(8,128)S(1)} %collective-permute-done.4.refs_0_), channel_id=1, source_target_pairs={{0,1},{1,2},{2,3},{3,4},{4,5},{5,6},{6,7},{7,0},{32,39},{33,32},{3... | collective-permute-start | bytes 786440 | tf_op jit(solution)/shard_map/ppermute | solution.py:162
  29.4 0.7 copy-start.6
  30.1 7.9 %collective-permute-start.1 = (f32[512,128]{1,0:T(8,128)S(1)}, f32[512,128]{1,0:T(8,128)}, u32[]{:S(2)}, u32[]{:S(2)}) collective-permute-start(f32[512,128]{1,0:T(8,128)S(1)} %collective-permute-done.refs_1_), channel_id=1, source_target_pairs={{0,1},{1,2},{2,3},{3,4},{4,5},{5,6},{6,7},{7,0},{32,39},{33,32},{3... | collective-permute-start | bytes 786440 | tf_op jit(solution)/shard_map/ppermute | solution.py:162
  34.1 0.7 copy-start.4
  34.8 9.9 %collective-permute-start.6 = (f32[512,128]{1,0:T(8,128)S(1)}, f32[512,128]{1,0:T(8,128)S(1)}, u32[]{:S(2)}, u32[]{:S(2)}) collective-permute-start(f32[512,128]{1,0:T(8,128)S(1)} %collective-permute-done.5.refs_1_), channel_id=1, source_target_pairs={{0,1},{1,2},{2,3},{3,4},{4,5},{5,6},{6,7},{7,0},{32,39},{33,32},{3... | collective-permute-start | bytes 786440 | tf_op jit(solution)/shard_map/ppermute | solution.py:162
  38.1 16.5 %collective-permute-start.2 = (f32[512,128]{1,0:T(8,128)}, f32[512,128]{1,0:T(8,128)S(1)}, u32[]{:S(2)}, u32[]{:S(2)}) collective-permute-start(f32[512,128]{1,0:T(8,128)} %collective-permute-done.1.refs_2_), channel_id=1, source_target_pairs={{0,1},{1,2},{2,3},{3,4},{4,5},{5,6},{6,7},{7,0},{32,39},{33,32},{3... | collective-permute-start | bytes 786440 | tf_op jit(solution)/shard_map/ppermute | solution.py:162
  42.8 11.7 %collective-permute-start.3 = (f32[512,128]{1,0:T(8,128)}, f32[512,128]{1,0:T(8,128)S(1)}, u32[]{:S(2)}, u32[]{:S(2)}) collective-permute-start(f32[512,128]{1,0:T(8,128)} %collective-permute-done.1.refs_2_), channel_id=1, source_target_pairs={{0,2},{1,3},{2,4},{3,5},{4,6},{5,7},{6,0},{7,1},{32,38},{33,39},{3... | collective-permute-start | bytes 786440 | tf_op jit(solution)/shard_map/ppermute | solution.py:162
  44.8 1.0 %copy-start.7 = (f32[512,128]{1,0:T(8,128)S(1)}, f32[512,128]{1,0:T(8,128)}, u32[]{:S(2)}) copy-start(f32[512,128]{1,0:T(8,128)} %copy-done.6) | copy-start | bytes 786436
  46.4 6.1 %copy-start.2 = (f32[512,128]{1,0:T(8,128)S(1)}, f32[512,128]{1,0:T(8,128)}, u32[]{:S(2)}) copy-start(f32[512,128]{1,0:T(8,128)} %refs_0_.1) | copy-start | bytes 786436
  46.4 6.1 %copy-start.5 = (f32[512,128]{1,0:T(8,128)S(1)}, f32[512,128]{1,0:T(8,128)}, u32[]{:S(2)}) copy-start(f32[512,128]{1,0:T(8,128)} %copy-done.4) | copy-start | bytes 786436
  48.2 6.6 %collective-permute-start.7 = (f32[4,512,128]{2,1,0:T(8,128)S(1)}, f32[4,512,128]{2,1,0:T(8,128)S(1)}, u32[]{:S(2)}, u32[]{:S(2)}) collective-permute-start(f32[4,512,128]{2,1,0:T(8,128)S(1)} %dressed_other.1), channel_id=1, source_target_pairs={{0,32},{32,0},{1,33},{33,1},{2,34},{34,2},{3,35},{35,3},{4,36},{36... | collective-permute-start | bytes 3145736 | tf_op jit(solution)/shard_map/ppermute | solution.py:165
  56.8 4.8 %copy-start.9 = (s32[8,2]{0,1:T(2,128)S(1)}, s32[8,2]{0,1:T(2,128)}, u32[]{:S(2)}) copy-start(s32[8,2]{0,1:T(2,128)} %param.15) | copy-start | bytes 196
  56.8 5.0 %copy-start = (f32[8,512,64]{1,2,0:T(8,128)S(1)}, f32[8,512,64]{1,2,0:T(8,128)}, u32[]{:S(2)}) copy-start(f32[8,512,64]{1,2,0:T(8,128)} %param.11) | copy-start | bytes 3145732
  56.8 5.1 %copy-start.11 = (s32[128]{0:T(128)S(1)}, s32[128]{0:T(128)}, u32[]{:S(2)}) copy-start(s32[128]{0:T(128)} %param.13) | copy-start | bytes 1540
  56.8 5.2 %copy-start.12 = (s32[32]{0:T(128)S(1)}, s32[32]{0:T(128)}, u32[]{:S(2)}) copy-start(s32[32]{0:T(128)} %param.14) | copy-start | bytes 388
  56.8 20.0 %all-to-all-start.1 = ((f32[4,512,128]{2,1,0:T(8,128)}), f32[4,512,128]{2,1,0:T(8,128)S(1)}, u32[]{:S(2)}, u32[]{:S(2)}) async-start(f32[4,512,128]{2,1,0:T(8,128)} %dressed_late.1), calls=%async_computation.1 | async-start | bytes 2097152 | tf_op jit(solution)/shard_map/all_to_all | solution.py:240
  62.2 14.6 %copy-start.3 = (f32[512,128]{1,0:T(8,128)S(1)}, f32[512,128]{1,0:T(8,128)}, u32[]{:S(2)}) copy-start(f32[512,128]{1,0:T(8,128)} %refs_0_.1) | copy-start | bytes 786436
  62.2 14.6 %copy-start.8 = (f32[512]{0:T(512)S(1)}, f32[512]{0:T(512)}, u32[]{:S(2)}) copy-start(f32[512]{0:T(512)} %param.16) | copy-start | bytes 6148
  62.2 14.7 %copy-start.10 = (f32[128]{0:T(128)S(1)}, f32[128]{0:T(128)}, u32[]{:S(2)}) copy-start(f32[128]{0:T(128)} %param.17) | copy-start | bytes 1540
Sparse Core Ops, SparseCore 0:
  10.1 64.1 all-gather.1

commit v9 on v7

--- a/solution.py
+++ b/solution.py
@@ -65,7 +65,7 @@
             out[s + k] = value if plus is None else value + plus(s + k)
 
 
-def product_kernel(first, count, added, *refs):
+def product_kernel(first, count, added, last_first, *refs):
     pieces, high, low, refs = refs[:count], refs[count], refs[count + 1], refs[count + 2 :]
     earlier, refs = refs[:added], refs[added:]
     out, held, right_high, right_low, left_high, left_low, sems = refs[:7]
@@ -77,7 +77,8 @@
     made = start_all(copies, sems)
     for k in range(count):
         made[k].wait()
-        at = slice(k * width, (k + 1) * width)
+        step = count - 1 - k if last_first else k
+        at = slice(step * width, (step + 1) * width)
         left_high[:, at], left_low[:, at] = split(held[k])
     for copy in made[count:]:
         copy.wait()
@@ -190,10 +191,10 @@
         name="dressing_ready",
     )(panels)
 
-    def product(pieces, first, name, flops, *earlier):
+    def product(pieces, first, name, flops, *earlier, last_first=False):
         count, added = len(pieces), len(earlier)
         return pl.pallas_call(
-            lambda *refs: product_kernel(first, count, added, *refs),
+            lambda *refs: product_kernel(first, count, added, last_first, *refs),
             out_shape=shape,
             in_specs=[HBM] * (count + 2 + added),
             out_specs=VMEM,
@@ -234,7 +235,7 @@
     )(*slices, high, low)
     other = swap(other)
     early = product([amplitudes, *amp_same[:2]], 0, "dressed_early", EARLY)
-    sums = product([amp_same[2], amp_far], 3, "dressed_late", LATE, early, other)
+    sums = product([amp_far, amp_same[2]], 3, "dressed_late", LATE, early, other, last_first=True)
     sums = lax.all_to_all(sums, "x", 0, 0)
 
     stacked = pl.pallas_call(

time: 85.2 us -> 85.2 us (level)
  no operation moved by 1% of the time
where the time goes in v9:
time: 85.2 us; the launch traced here: 84.6 us
  starting transfers between devices  44.4 us (52%)
  between operations  14.3 us (17%)
  waiting for transfers between devices  12.9 us (15%)
  Pallas kernels  9.17 us (11%)
  local copies, waits for them, and re-layouts  2.64 us (3%)
  other arithmetic  1.13 us (1%)
    ppermute x7, starting transfers between devices, ring(): return lax.ppermute(value, names, pairs_of)  31.2 us
    all_gather x1, waiting for transfers between devices, shards(): gathered = lax.all_gather(blocks, ('y', 'core'), axis=0, tiled=True)  12 us
    all_to_all x1, starting transfers between devices, shards(): sums = lax.all_to_all(sums, 'x', 0, 0)  4.76 us
    ppermute x1, starting transfers between devices, swap(): return lax.ppermute(value, 'core', [(0, 1), (1, 0)])  4.29 us
    all_to_all x1, starting transfers between devices, shards(): panels = lax.all_to_all(dressing.reshape(nx, depth, width), 'x', 0, 0)  4.16 us
    pallas_call x2, Pallas kernels, product(): pl.pallas_call(lambda *refs: product_kernel(first, count, added, last_fir...  4.07 us
    pallas_call x1, Pallas kernels, shards(): pl.pallas_call(lambda *refs: integral_kernel(pairs, *refs), out_shape=jax...  2.58 us
    unnamed x27, local copies, waits for them, and re-layouts  2.48 us
  transfers between devices with their start and end apart: 11, of which 2 were waited for; matrix products, arithmetic and copies ran while one was open for 1% of the time, Pallas kernels for 11%

profile of v9, /device:TPU:1, one launch (start us, length us, event | category | flops | bytes accessed | tf_op | source)
XLA Modules:
  0.0 84.6 jit_solution(15811739520229002489)
XLA Ops:
  7.2 0.0 all-gather.2.cloned.1.call-start
  7.2 0.7 all-gather.2.cloned.1.call-update
  7.9 5.4 %collective-permute-start.4 = (f32[512,128]{1,0:T(8,128)}, f32[512,128]{1,0:T(8,128)S(1)}, u32[]{:S(2)}, u32[]{:S(2)}) collective-permute-start(f32[512,128]{1,0:T(8,128)} %refs_0_.1), channel_id=1, source_target_pairs={{32,1},{33,2},{34,3},{35,4},{36,5},{37,6},{38,7},{39,0},{0,39},{1,... | collective-permute-start | bytes 786440 | tf_op jit(solution)/shard_map/ppermute | solution.py:161
  13.3 0.0 copy-start.1
  13.3 4.2 %all-to-all-start = ((f32[4,1024,128]{2,1,0:T(8,128)}), f32[4,1024,128]{2,1,0:T(8,128)S(1)}, u32[]{:S(2)}, u32[]{:S(2)}) async-start(f32[4,1024,128]{2,1,0:T(8,128)} %bitcast.8), calls=%async_computation | async-start | bytes 4194304 | tf_op jit(solution)/shard_map/all_to_all | solution.py:180
  17.5 0.0 copy-done.1
  17.5 8.0 %collective-permute-start = (f32[512,128]{1,0:T(8,128)S(1)}, f32[512,128]{1,0:T(8,128)S(1)}, u32[]{:S(2)}, u32[]{:S(2)}) collective-permute-start(f32[512,128]{1,0:T(8,128)S(1)} %copy-done.1), channel_id=1, source_target_pairs={{0,1},{1,2},{2,3},{3,4},{4,5},{5,6},{6,7},{7,0},{32,39},{33,32},{3... | collective-permute-start | bytes 786440 | tf_op jit(solution)/shard_map/ppermute | solution.py:161
  25.5 0.0 collective-permute-done.4.refs_0_
  25.5 3.9 %collective-permute-start.5 = (f32[512,128]{1,0:T(8,128)S(1)}, f32[512,128]{1,0:T(8,128)S(1)}, u32[]{:S(2)}, u32[]{:S(2)}) collective-permute-start(f32[512,128]{1,0:T(8,128)S(1)} %collective-permute-done.4.refs_0_), channel_id=1, source_target_pairs={{0,1},{1,2},{2,3},{3,4},{4,5},{5,6},{6,7},{7,0},{32,39},{33,32},{3... | collective-permute-start | bytes 786440 | tf_op jit(solution)/shard_map/ppermute | solution.py:161
  29.4 0.0 copy-start.6
  29.4 0.7 copy-done.6
  30.1 0.0 collective-permute-done.refs_1_
  30.1 4.0 %collective-permute-start.1 = (f32[512,128]{1,0:T(8,128)S(1)}, f32[512,128]{1,0:T(8,128)}, u32[]{:S(2)}, u32[]{:S(2)}) collective-permute-start(f32[512,128]{1,0:T(8,128)S(1)} %collective-permute-done.refs_1_), channel_id=1, source_target_pairs={{0,1},{1,2},{2,3},{3,4},{4,5},{5,6},{6,7},{7,0},{32,39},{33,32},{3... | collective-permute-start | bytes 786440 | tf_op jit(solution)/shard_map/ppermute | solution.py:161
  34.1 0.0 copy-start.4
  34.1 0.7 copy-done.4
  34.8 0.0 collective-permute-done.5.refs_1_
  34.8 3.2 %collective-permute-start.6 = (f32[512,128]{1,0:T(8,128)S(1)}, f32[512,128]{1,0:T(8,128)S(1)}, u32[]{:S(2)}, u32[]{:S(2)}) collective-permute-start(f32[512,128]{1,0:T(8,128)S(1)} %collective-permute-done.5.refs_1_), channel_id=1, source_target_pairs={{0,1},{1,2},{2,3},{3,4},{4,5},{5,6},{6,7},{7,0},{32,39},{33,32},{3... | collective-permute-start | bytes 786440 | tf_op jit(solution)/shard_map/ppermute | solution.py:161
  38.0 0.0 collective-permute-done.1.refs_2_
  38.1 4.1 %collective-permute-start.2 = (f32[512,128]{1,0:T(8,128)}, f32[512,128]{1,0:T(8,128)S(1)}, u32[]{:S(2)}, u32[]{:S(2)}) collective-permute-start(f32[512,128]{1,0:T(8,128)} %collective-permute-done.1.refs_2_), channel_id=1, source_target_pairs={{0,2},{1,3},{2,4},{3,5},{4,6},{5,7},{6,0},{7,1},{32,38},{33,39},{3... | collective-permute-start | bytes 786440 | tf_op jit(solution)/shard_map/ppermute | solution.py:161
  42.1 2.6 %collective-permute-start.3 = (f32[512,128]{1,0:T(8,128)}, f32[512,128]{1,0:T(8,128)S(1)}, u32[]{:S(2)}, u32[]{:S(2)}) collective-permute-start(f32[512,128]{1,0:T(8,128)} %collective-permute-done.1.refs_2_), channel_id=1, source_target_pairs={{0,1},{1,2},{2,3},{3,4},{4,5},{5,6},{6,7},{7,0},{32,39},{33,32},{3... | collective-permute-start | bytes 786440 | tf_op jit(solution)/shard_map/ppermute | solution.py:161
  44.7 0.0 collective-permute-done.6.refs_2_
  44.8 0.0 copy-start.7
  44.8 0.9 %copy-done.7 = f32[512,128]{1,0:T(8,128)S(1)} copy-done((f32[512,128]{1,0:T(8,128)S(1)}, f32[512,128]{1,0:T(8,128)}, u32[]{:S(2)}) %copy-start.7) | copy-done | bytes 262168
  45.7 0.2 slices_ready.1
  46.0 0.0 all-to-all-done.refs_0_
  46.0 0.4 dressing_ready.1
  46.4 0.0 copy-start.2
  46.4 0.0 copy-start.5
  46.4 1.8 %dressed_other.1 = f32[4,512,128]{2,1,0:T(8,128)S(1)} custom-call(bf16[512,384]{1,0:T(8,128)(2,1)S(1)} %get-tuple-element.8.refs_0_, bf16[512,384]{1,0:T(8,128)(2,1)S(1)} %get-tuple-element.9.refs_1_, bf16[640,512]{1,0:T(8,128)(2,1)S(1)} %get-tuple-element.6.refs_3_.refs_2_, bf16[640,512]{1,0:T(8,128)(2,1)S(1)} %get-tuple-element.7.refs_4_.refs_3_), custom_call_target="tpu_custom_call" | custom-call | flops 1000 | bytes 1000000 | tf_op jit(solution)/shard_map/dressed_other/pallas_call | solution.py:222
  48.2 4.3 %collective-permute-start.7 = (f32[4,512,128]{2,1,0:T(8,128)S(1)}, f32[4,512,128]{2,1,0:T(8,128)S(1)}, u32[]{:S(2)}, u32[]{:S(2)}) collective-permute-start(f32[4,512,128]{2,1,0:T(8,128)S(1)} %dressed_other.1), channel_id=1, source_target_pairs={{0,32},{32,0},{1,33},{33,1},{2,34},{34,2},{3,35},{35,3},{4,36},{36... | collective-permute-start | bytes 3145736 | tf_op jit(solution)/shard_map/ppermute | solution.py:164
  52.5 0.0 copy-done.2
  52.5 0.0 copy-done.5
  52.5 2.1 %dressed_early.1.refs_4_ = f32[4,512,128]{2,1,0:T(8,128)S(1)} custom-call(f32[512,128]{1,0:T(8,128)S(1)} %copy-done.2, f32[512,128]{1,0:T(8,128)S(1)} %copy-done.5, f32[512,128]{1,0:T(8,128)} %collective-permute-done.1.refs_2_, bf16[640,512]{1,0:T(8,128)(2,1)S(1)} %get-tuple-element.6.refs_3_.refs_2_, bf16[640,512]{1,0:T(8,128)(2,1)S(1)} %get-tuple-element.7.refs_4_.refs_3_), custom_call_target="tpu_custom_call" | custom-call | flops 30000001024 | bytes 1000000 | tf_op jit(solution)/shard_map/dressed_early/pallas_call | solution.py:196
  54.6 0.0 collective-permute-done.2.refs_0_
  54.6 0.0 collective-permute-done.3.refs_1_
  54.6 0.2 collective-permute-done.7.refs_5_
  54.8 2.0 %dressed_late.1 = f32[4,512,128]{2,1,0:T(8,128)} custom-call(f32[512,128]{1,0:T(8,128)S(1)} %collective-permute-done.2.refs_0_, f32[512,128]{1,0:T(8,128)S(1)} %collective-permute-done.3.refs_1_, bf16[640,512]{1,0:T(8,128)(2,1)S(1)} %get-tuple-element.6.refs_3_.refs_2_, bf16[640,512]{1,0:T(8,128)(2,1)S(1)} %get-tuple-element.7.refs_4_.refs_3_, ...), custom_call_target="tpu_custom_call" | custom-call | flops 1000 | bytes 1000000 | tf_op jit(solution)/shard_map/dressed_late/pallas_call | solution.py:196
  56.8 0.0 copy-start.9
  56.8 0.0 copy-start
  56.8 0.0 copy-start.11
  56.8 0.0 copy-start.12
  56.8 4.8 %all-to-all-start.1 = ((f32[4,512,128]{2,1,0:T(8,128)}), f32[4,512,128]{2,1,0:T(8,128)S(1)}, u32[]{:S(2)}, u32[]{:S(2)}) async-start(f32[4,512,128]{2,1,0:T(8,128)} %dressed_late.1), calls=%async_computation.1 | async-start | bytes 2097152 | tf_op jit(solution)/shard_map/all_to_all | solution.py:239
  61.6 0.0 copy-done.9
  61.6 0.1 copy.14
  61.7 0.1 reshape.16
  61.7 0.0 copy-done
  61.7 0.1 factor_ready.1.refs_1_
  61.9 0.0 copy-done.11
  61.9 0.1 dynamic_slice.3
  62.0 0.0 copy-done.12
  62.0 0.2 select_reduce_fusion
  62.2 0.1 pad_add_fusion.refs_0_
  62.2 0.0 copy-start.3
  62.2 0.0 copy-start.8
  62.2 0.0 copy-start.10
  62.2 12.0 %all-gather.2.cloned.1.call-done.refs_2_ = f32[32,512,128]{2,1,0:T(8,128)} async-done(((f32[2,512,128]{2,1,0:T(8,128)}), f32[32,512,128]{2,1,0:T(8,128)}) %all-gather.2.cloned.1.call-update) | async-done | bytes 8388624 | tf_op jit(solution)/shard_map/all_gather | solution.py:173
  74.3 2.6 %integral.1 = f32[512,128]{1,0:T(8,128)S(1)} custom-call(s32[24]{0:T(128)S(1)} %pad_add_fusion.refs_0_, bf16[8,128,512]{2,1,0:T(8,128)(2,1)S(1)} %factor_ready.1.refs_1_, f32[32,512,128]{2,1,0:T(8,128)} %all-gather.2.cloned.1.call-done.refs_2_), custom_call_target="tpu_custom_call" | custom-call | tf_op jit(solution)/shard_map/integral/pallas_call | solution.py:254
  76.9 0.0 all-to-all-done.1
  76.9 0.0 copy-done.3
  76.9 0.0 copy-done.8
  76.9 0.0 copy-done.10
  76.9 0.9 %divide_subtract_fusion = (f32[512,128]{1,0:T(8,128)}, f32[512,128]{1,0:T(8,128)}) fusion(f32[512,128]{1,0:T(8,128)S(1)} %copy-done.3, f32[128]{0:T(128)S(1)} %copy-done.10, f32[512]{0:T(512)S(1)} %copy-done.8, f32[512,128]{1,0:T(8,128)S(1)} %integral.1, f32[4,512,128]{2,1,0:T(8,128)S(1)} %all-to-all-done.1), kind=kLoop, calls=%fused_computation.5 | loop fusion | flops 458752 | bytes 2099712 | tf_op jit(solution)/shard_map/sub | solution.py:268
Async XLA Ops:
  7.2 67.1 %all-gather.2.cloned.1.call-start = ((), (), s32[]{:S(2)}) async-start(), calls=%async_computation.2 | async-start | bytes 8912896 | tf_op jit(solution)/shard_map/all_gather | solution.py:173
  7.9 17.6 %collective-permute-start.4 = (f32[512,128]{1,0:T(8,128)}, f32[512,128]{1,0:T(8,128)S(1)}, u32[]{:S(2)}, u32[]{:S(2)}) collective-permute-start(f32[512,128]{1,0:T(8,128)} %refs_0_.1), channel_id=1, source_target_pairs={{32,1},{33,2},{34,3},{35,4},{36,5},{37,6},{38,7},{39,0},{0,39},{1,... | collective-permute-start | bytes 786440 | tf_op jit(solution)/shard_map/ppermute | solution.py:161
  13.3 4.2 %copy-start.1 = (f32[512,128]{1,0:T(8,128)S(1)}, f32[512,128]{1,0:T(8,128)}, u32[]{:S(2)}) copy-start(f32[512,128]{1,0:T(8,128)} %refs_0_.1) | copy-start | bytes 786436
  13.3 32.7 %all-to-all-start = ((f32[4,1024,128]{2,1,0:T(8,128)}), f32[4,1024,128]{2,1,0:T(8,128)S(1)}, u32[]{:S(2)}, u32[]{:S(2)}) async-start(f32[4,1024,128]{2,1,0:T(8,128)} %bitcast.8), calls=%async_computation | async-start | bytes 4194304 | tf_op jit(solution)/shard_map/all_to_all | solution.py:180
  17.5 12.7 %collective-permute-start = (f32[512,128]{1,0:T(8,128)S(1)}, f32[512,128]{1,0:T(8,128)S(1)}, u32[]{:S(2)}, u32[]{:S(2)}) collective-permute-start(f32[512,128]{1,0:T(8,128)S(1)} %copy-done.1), channel_id=1, source_target_pairs={{0,1},{1,2},{2,3},{3,4},{4,5},{5,6},{6,7},{7,0},{32,39},{33,32},{3... | collective-permute-start | bytes 786440 | tf_op jit(solution)/shard_map/ppermute | solution.py:161
  25.5 9.3 %collective-permute-start.5 = (f32[512,128]{1,0:T(8,128)S(1)}, f32[512,128]{1,0:T(8,128)S(1)}, u32[]{:S(2)}, u32[]{:S(2)}) collective-permute-start(f32[512,128]{1,0:T(8,128)S(1)} %collective-permute-done.4.refs_0_), channel_id=1, source_target_pairs={{0,1},{1,2},{2,3},{3,4},{4,5},{5,6},{6,7},{7,0},{32,39},{33,32},{3... | collective-permute-start | bytes 786440 | tf_op jit(solution)/shard_map/ppermute | solution.py:161
  29.4 0.7 copy-start.6
  30.1 7.9 %collective-permute-start.1 = (f32[512,128]{1,0:T(8,128)S(1)}, f32[512,128]{1,0:T(8,128)}, u32[]{:S(2)}, u32[]{:S(2)}) collective-permute-start(f32[512,128]{1,0:T(8,128)S(1)} %collective-permute-done.refs_1_), channel_id=1, source_target_pairs={{0,1},{1,2},{2,3},{3,4},{4,5},{5,6},{6,7},{7,0},{32,39},{33,32},{3... | collective-permute-start | bytes 786440 | tf_op jit(solution)/shard_map/ppermute | solution.py:161
  34.1 0.7 copy-start.4
  34.8 9.9 %collective-permute-start.6 = (f32[512,128]{1,0:T(8,128)S(1)}, f32[512,128]{1,0:T(8,128)S(1)}, u32[]{:S(2)}, u32[]{:S(2)}) collective-permute-start(f32[512,128]{1,0:T(8,128)S(1)} %collective-permute-done.5.refs_1_), channel_id=1, source_target_pairs={{0,1},{1,2},{2,3},{3,4},{4,5},{5,6},{6,7},{7,0},{32,39},{33,32},{3... | collective-permute-start | bytes 786440 | tf_op jit(solution)/shard_map/ppermute | solution.py:161
  38.1 16.5 %collective-permute-start.2 = (f32[512,128]{1,0:T(8,128)}, f32[512,128]{1,0:T(8,128)S(1)}, u32[]{:S(2)}, u32[]{:S(2)}) collective-permute-start(f32[512,128]{1,0:T(8,128)} %collective-permute-done.1.refs_2_), channel_id=1, source_target_pairs={{0,2},{1,3},{2,4},{3,5},{4,6},{5,7},{6,0},{7,1},{32,38},{33,39},{3... | collective-permute-start | bytes 786440 | tf_op jit(solution)/shard_map/ppermute | solution.py:161
  42.1 12.4 %collective-permute-start.3 = (f32[512,128]{1,0:T(8,128)}, f32[512,128]{1,0:T(8,128)S(1)}, u32[]{:S(2)}, u32[]{:S(2)}) collective-permute-start(f32[512,128]{1,0:T(8,128)} %collective-permute-done.1.refs_2_), channel_id=1, source_target_pairs={{0,1},{1,2},{2,3},{3,4},{4,5},{5,6},{6,7},{7,0},{32,39},{33,32},{3... | collective-permute-start | bytes 786440 | tf_op jit(solution)/shard_map/ppermute | solution.py:161
  44.8 1.0 %copy-start.7 = (f32[512,128]{1,0:T(8,128)S(1)}, f32[512,128]{1,0:T(8,128)}, u32[]{:S(2)}) copy-start(f32[512,128]{1,0:T(8,128)} %copy-done.6) | copy-start | bytes 786436
  46.4 6.1 %copy-start.2 = (f32[512,128]{1,0:T(8,128)S(1)}, f32[512,128]{1,0:T(8,128)}, u32[]{:S(2)}) copy-start(f32[512,128]{1,0:T(8,128)} %refs_0_.1) | copy-start | bytes 786436
  46.4 6.1 %copy-start.5 = (f32[512,128]{1,0:T(8,128)S(1)}, f32[512,128]{1,0:T(8,128)}, u32[]{:S(2)}) copy-start(f32[512,128]{1,0:T(8,128)} %copy-done.4) | copy-start | bytes 786436
  48.2 6.6 %collective-permute-start.7 = (f32[4,512,128]{2,1,0:T(8,128)S(1)}, f32[4,512,128]{2,1,0:T(8,128)S(1)}, u32[]{:S(2)}, u32[]{:S(2)}) collective-permute-start(f32[4,512,128]{2,1,0:T(8,128)S(1)} %dressed_other.1), channel_id=1, source_target_pairs={{0,32},{32,0},{1,33},{33,1},{2,34},{34,2},{3,35},{35,3},{4,36},{36... | collective-permute-start | bytes 3145736 | tf_op jit(solution)/shard_map/ppermute | solution.py:164
  56.8 4.8 %copy-start.9 = (s32[8,2]{0,1:T(2,128)S(1)}, s32[8,2]{0,1:T(2,128)}, u32[]{:S(2)}) copy-start(s32[8,2]{0,1:T(2,128)} %param.15) | copy-start | bytes 196
  56.8 5.0 %copy-start = (f32[8,512,64]{1,2,0:T(8,128)S(1)}, f32[8,512,64]{1,2,0:T(8,128)}, u32[]{:S(2)}) copy-start(f32[8,512,64]{1,2,0:T(8,128)} %param.11) | copy-start | bytes 3145732
  56.8 5.1 %copy-start.11 = (s32[128]{0:T(128)S(1)}, s32[128]{0:T(128)}, u32[]{:S(2)}) copy-start(s32[128]{0:T(128)} %param.13) | copy-start | bytes 1540
  56.8 5.2 %copy-start.12 = (s32[32]{0:T(128)S(1)}, s32[32]{0:T(128)}, u32[]{:S(2)}) copy-start(s32[32]{0:T(128)} %param.14) | copy-start | bytes 388
  56.8 20.0 %all-to-all-start.1 = ((f32[4,512,128]{2,1,0:T(8,128)}), f32[4,512,128]{2,1,0:T(8,128)S(1)}, u32[]{:S(2)}, u32[]{:S(2)}) async-start(f32[4,512,128]{2,1,0:T(8,128)} %dressed_late.1), calls=%async_computation.1 | async-start | bytes 2097152 | tf_op jit(solution)/shard_map/all_to_all | solution.py:239
  62.2 14.6 %copy-start.3 = (f32[512,128]{1,0:T(8,128)S(1)}, f32[512,128]{1,0:T(8,128)}, u32[]{:S(2)}) copy-start(f32[512,128]{1,0:T(8,128)} %refs_0_.1) | copy-start | bytes 786436
  62.2 14.7 %copy-start.8 = (f32[512]{0:T(512)S(1)}, f32[512]{0:T(512)}, u32[]{:S(2)}) copy-start(f32[512]{0:T(512)} %param.16) | copy-start | bytes 6148
  62.2 14.7 %copy-start.10 = (f32[128]{0:T(128)S(1)}, f32[128]{0:T(128)}, u32[]{:S(2)}) copy-start(f32[128]{0:T(128)} %param.17) | copy-start | bytes 1540
Sparse Core Ops, SparseCore 0:
  10.1 64.1 all-gather.1

commit v10 on v8

--- a/solution.py
+++ b/solution.py
@@ -65,7 +65,7 @@
             out[s + k] = value if plus is None else value + plus(s + k)
 
 
-def product_kernel(first, count, added, *refs):
+def product_kernel(first, count, added, last_first, *refs):
     pieces, high, low, refs = refs[:count], refs[count], refs[count + 1], refs[count + 2 :]
     earlier, refs = refs[:added], refs[added:]
     out, held, right_high, right_low, left_high, left_low, sems = refs[:7]
@@ -77,7 +77,8 @@
     made = start_all(copies, sems)
     for k in range(count):
         made[k].wait()
-        at = slice(k * width, (k + 1) * width)
+        step = count - 1 - k if last_first else k
+        at = slice(step * width, (step + 1) * width)
         left_high[:, at], left_low[:, at] = split(held[k])
     for copy in made[count:]:
         copy.wait()
@@ -192,10 +193,10 @@
         name="dressing_ready",
     )(panels)
 
-    def product(pieces, first, name, flops, *earlier):
+    def product(pieces, first, name, flops, *earlier, last_first=False):
         count, added = len(pieces), len(earlier)
         return pl.pallas_call(
-            lambda *refs: product_kernel(first, count, added, *refs),
+            lambda *refs: product_kernel(first, count, added, last_first, *refs),
             out_shape=shape,
             in_specs=[HBM] * (count + 2 + added),
             out_specs=VMEM,
@@ -236,7 +237,7 @@
     )(*slices, high, low)
     other = swap(other)
     early = product([amplitudes, *amp_same[:2]], 0, "dressed_early", EARLY)
-    sums = product([amp_same[2], amp_far], 3, "dressed_late", LATE, early, other)
+    sums = product([amp_far, amp_same[2]], 3, "dressed_late", LATE, early, other, last_first=True)
     sums = lax.all_to_all(sums, "x", 0, 0)
 
     stacked = pl.pallas_call(

time: 85.2 us -> 85.2 us (level)
  no operation moved by 1% of the time
where the time goes in v10:
time: 85.2 us; the launch traced here: 84.6 us
  starting transfers between devices  44.4 us (52%)
  between operations  14.3 us (17%)
  waiting for transfers between devices  12.9 us (15%)
  Pallas kernels  9.16 us (11%)
  local copies, waits for them, and re-layouts  2.64 us (3%)
  other arithmetic  1.13 us (1%)
    ppermute x7, starting transfers between devices, ring(): return lax.ppermute(value, names, pairs_of)  31.2 us
    all_gather x1, waiting for transfers between devices, shards(): gathered = lax.all_gather(blocks, ('y', 'core'), axis=0, tiled=True)  12 us
    all_to_all x1, starting transfers between devices, shards(): sums = lax.all_to_all(sums, 'x', 0, 0)  4.76 us
    ppermute x1, starting transfers between devices, swap(): return lax.ppermute(value, 'core', [(0, 1), (1, 0)])  4.29 us
    all_to_all x1, starting transfers between devices, shards(): panels = lax.all_to_all(dressing.reshape(nx, depth, width), 'x', 0, 0)  4.16 us
    pallas_call x2, Pallas kernels, product(): pl.pallas_call(lambda *refs: product_kernel(first, count, added, last_fir...  4.07 us
    pallas_call x1, Pallas kernels, shards(): pl.pallas_call(lambda *refs: integral_kernel(pairs, *refs), out_shape=jax...  2.57 us
    unnamed x27, local copies, waits for them, and re-layouts  2.48 us
  transfers between devices with their start and end apart: 11, of which 2 were waited for; matrix products, arithmetic and copies ran while one was open for 1% of the time, Pallas kernels for 11%

profile of v10, /device:TPU:1, one launch (start us, length us, event | category | flops | bytes accessed | tf_op | source)
XLA Modules:
  0.0 84.6 jit_solution(8497105751333149167)
XLA Ops:
  7.2 0.0 all-gather.2.cloned.1.call-start
  7.2 0.7 all-gather.2.cloned.1.call-update
  7.9 5.4 %collective-permute-start.4 = (f32[512,128]{1,0:T(8,128)}, f32[512,128]{1,0:T(8,128)S(1)}, u32[]{:S(2)}, u32[]{:S(2)}) collective-permute-start(f32[512,128]{1,0:T(8,128)} %refs_0_.1), channel_id=1, source_target_pairs={{32,1},{33,2},{34,3},{35,4},{36,5},{37,6},{38,7},{39,0},{0,39},{1,... | collective-permute-start | bytes 786440 | tf_op jit(solution)/shard_map/ppermute | solution.py:163
  13.3 0.0 copy-start.1
  13.3 4.2 %all-to-all-start = ((f32[4,1024,128]{2,1,0:T(8,128)}), f32[4,1024,128]{2,1,0:T(8,128)S(1)}, u32[]{:S(2)}, u32[]{:S(2)}) async-start(f32[4,1024,128]{2,1,0:T(8,128)} %bitcast.8), calls=%async_computation | async-start | bytes 4194304 | tf_op jit(solution)/shard_map/all_to_all | solution.py:182
  17.5 0.0 copy-done.1
  17.5 8.0 %collective-permute-start = (f32[512,128]{1,0:T(8,128)S(1)}, f32[512,128]{1,0:T(8,128)S(1)}, u32[]{:S(2)}, u32[]{:S(2)}) collective-permute-start(f32[512,128]{1,0:T(8,128)S(1)} %copy-done.1), channel_id=1, source_target_pairs={{0,1},{1,2},{2,3},{3,4},{4,5},{5,6},{6,7},{7,0},{32,39},{33,32},{3... | collective-permute-start | bytes 786440 | tf_op jit(solution)/shard_map/ppermute | solution.py:163
  25.5 0.0 collective-permute-done.4.refs_0_
  25.5 3.9 %collective-permute-start.5 = (f32[512,128]{1,0:T(8,128)S(1)}, f32[512,128]{1,0:T(8,128)S(1)}, u32[]{:S(2)}, u32[]{:S(2)}) collective-permute-start(f32[512,128]{1,0:T(8,128)S(1)} %collective-permute-done.4.refs_0_), channel_id=1, source_target_pairs={{0,1},{1,2},{2,3},{3,4},{4,5},{5,6},{6,7},{7,0},{32,39},{33,32},{3... | collective-permute-start | bytes 786440 | tf_op jit(solution)/shard_map/ppermute | solution.py:163
  29.4 0.0 copy-start.6
  29.4 0.7 copy-done.6
  30.1 0.0 collective-permute-done.refs_1_
  30.1 4.0 %collective-permute-start.1 = (f32[512,128]{1,0:T(8,128)S(1)}, f32[512,128]{1,0:T(8,128)}, u32[]{:S(2)}, u32[]{:S(2)}) collective-permute-start(f32[512,128]{1,0:T(8,128)S(1)} %collective-permute-done.refs_1_), channel_id=1, source_target_pairs={{0,1},{1,2},{2,3},{3,4},{4,5},{5,6},{6,7},{7,0},{32,39},{33,32},{3... | collective-permute-start | bytes 786440 | tf_op jit(solution)/shard_map/ppermute | solution.py:163
  34.1 0.0 copy-start.4
  34.1 0.7 copy-done.4
  34.8 0.0 collective-permute-done.5.refs_1_
  34.8 3.2 %collective-permute-start.6 = (f32[512,128]{1,0:T(8,128)S(1)}, f32[512,128]{1,0:T(8,128)S(1)}, u32[]{:S(2)}, u32[]{:S(2)}) collective-permute-start(f32[512,128]{1,0:T(8,128)S(1)} %collective-permute-done.5.refs_1_), channel_id=1, source_target_pairs={{0,1},{1,2},{2,3},{3,4},{4,5},{5,6},{6,7},{7,0},{32,39},{33,32},{3... | collective-permute-start | bytes 786440 | tf_op jit(solution)/shard_map/ppermute | solution.py:163
  38.0 0.0 collective-permute-done.1.refs_2_
  38.1 4.1 %collective-permute-start.2 = (f32[512,128]{1,0:T(8,128)}, f32[512,128]{1,0:T(8,128)S(1)}, u32[]{:S(2)}, u32[]{:S(2)}) collective-permute-start(f32[512,128]{1,0:T(8,128)} %collective-permute-done.1.refs_2_), channel_id=1, source_target_pairs={{0,2},{1,3},{2,4},{3,5},{4,6},{5,7},{6,0},{7,1},{32,38},{33,39},{3... | collective-permute-start | bytes 786440 | tf_op jit(solution)/shard_map/ppermute | solution.py:163
  42.1 2.6 %collective-permute-start.3 = (f32[512,128]{1,0:T(8,128)}, f32[512,128]{1,0:T(8,128)S(1)}, u32[]{:S(2)}, u32[]{:S(2)}) collective-permute-start(f32[512,128]{1,0:T(8,128)} %collective-permute-done.1.refs_2_), channel_id=1, source_target_pairs={{0,1},{1,2},{2,3},{3,4},{4,5},{5,6},{6,7},{7,0},{32,39},{33,32},{3... | collective-permute-start | bytes 786440 | tf_op jit(solution)/shard_map/ppermute | solution.py:163
  44.7 0.0 collective-permute-done.6.refs_2_
  44.8 0.0 copy-start.7
  44.8 0.9 %copy-done.7 = f32[512,128]{1,0:T(8,128)S(1)} copy-done((f32[512,128]{1,0:T(8,128)S(1)}, f32[512,128]{1,0:T(8,128)}, u32[]{:S(2)}) %copy-start.7) | copy-done | bytes 262168
  45.7 0.2 slices_ready.1
  46.0 0.0 all-to-all-done.refs_0_
  46.0 0.4 dressing_ready.1
  46.4 0.0 copy-start.2
  46.4 0.0 copy-start.5
  46.4 1.8 %dressed_other.1 = f32[4,512,128]{2,1,0:T(8,128)S(1)} custom-call(bf16[512,384]{1,0:T(8,128)(2,1)S(1)} %get-tuple-element.8.refs_0_, bf16[512,384]{1,0:T(8,128)(2,1)S(1)} %get-tuple-element.9.refs_1_, bf16[640,512]{1,0:T(8,128)(2,1)S(1)} %get-tuple-element.6.refs_3_.refs_2_, bf16[640,512]{1,0:T(8,128)(2,1)S(1)} %get-tuple-element.7.refs_4_.refs_3_), custom_call_target="tpu_custom_call" | custom-call | flops 1000 | bytes 1000000 | tf_op jit(solution)/shard_map/dressed_other/pallas_call | solution.py:224
  48.2 4.3 %collective-permute-start.7 = (f32[4,512,128]{2,1,0:T(8,128)S(1)}, f32[4,512,128]{2,1,0:T(8,128)S(1)}, u32[]{:S(2)}, u32[]{:S(2)}) collective-permute-start(f32[4,512,128]{2,1,0:T(8,128)S(1)} %dressed_other.1), channel_id=1, source_target_pairs={{0,32},{32,0},{1,33},{33,1},{2,34},{34,2},{3,35},{35,3},{4,36},{36... | collective-permute-start | bytes 3145736 | tf_op jit(solution)/shard_map/ppermute | solution.py:166
  52.5 0.0 copy-done.2
  52.5 0.0 copy-done.5
  52.5 2.1 %dressed_early.1.refs_4_ = f32[4,512,128]{2,1,0:T(8,128)S(1)} custom-call(f32[512,128]{1,0:T(8,128)S(1)} %copy-done.2, f32[512,128]{1,0:T(8,128)S(1)} %copy-done.5, f32[512,128]{1,0:T(8,128)} %collective-permute-done.1.refs_2_, bf16[640,512]{1,0:T(8,128)(2,1)S(1)} %get-tuple-element.6.refs_3_.refs_2_, bf16[640,512]{1,0:T(8,128)(2,1)S(1)} %get-tuple-element.7.refs_4_.refs_3_), custom_call_target="tpu_custom_call" | custom-call | flops 30000001024 | bytes 1000000 | tf_op jit(solution)/shard_map/dressed_early/pallas_call | solution.py:198
  54.6 0.0 collective-permute-done.2.refs_0_
  54.6 0.0 collective-permute-done.3.refs_1_
  54.6 0.2 collective-permute-done.7.refs_5_
  54.8 2.0 %dressed_late.1 = f32[4,512,128]{2,1,0:T(8,128)} custom-call(f32[512,128]{1,0:T(8,128)S(1)} %collective-permute-done.2.refs_0_, f32[512,128]{1,0:T(8,128)S(1)} %collective-permute-done.3.refs_1_, bf16[640,512]{1,0:T(8,128)(2,1)S(1)} %get-tuple-element.6.refs_3_.refs_2_, bf16[640,512]{1,0:T(8,128)(2,1)S(1)} %get-tuple-element.7.refs_4_.refs_3_, ...), custom_call_target="tpu_custom_call" | custom-call | flops 1000 | bytes 1000000 | tf_op jit(solution)/shard_map/dressed_late/pallas_call | solution.py:198
  56.8 0.0 copy-start.9
  56.8 0.0 copy-start
  56.8 0.0 copy-start.11
  56.8 0.0 copy-start.12
  56.8 4.8 %all-to-all-start.1 = ((f32[4,512,128]{2,1,0:T(8,128)}), f32[4,512,128]{2,1,0:T(8,128)S(1)}, u32[]{:S(2)}, u32[]{:S(2)}) async-start(f32[4,512,128]{2,1,0:T(8,128)} %dressed_late.1), calls=%async_computation.1 | async-start | bytes 2097152 | tf_op jit(solution)/shard_map/all_to_all | solution.py:241
  61.6 0.0 copy-done.9
  61.6 0.1 copy.14
  61.7 0.1 reshape.16
  61.7 0.0 copy-done
  61.7 0.1 factor_ready.1.refs_1_
  61.9 0.0 copy-done.11
  61.9 0.1 dynamic_slice.3
  62.0 0.0 copy-done.12
  62.0 0.2 select_reduce_fusion
  62.2 0.1 pad_add_fusion.refs_0_
  62.2 0.0 copy-start.3
  62.2 0.0 copy-start.8
  62.2 0.0 copy-start.10
  62.2 12.0 %all-gather.2.cloned.1.call-done.refs_2_ = f32[32,512,128]{2,1,0:T(8,128)} async-done(((f32[2,512,128]{2,1,0:T(8,128)}), f32[32,512,128]{2,1,0:T(8,128)}) %all-gather.2.cloned.1.call-update) | async-done | bytes 8388624 | tf_op jit(solution)/shard_map/all_gather | solution.py:175
  74.3 2.6 %integral.1 = f32[512,128]{1,0:T(8,128)S(1)} custom-call(s32[24]{0:T(128)S(1)} %pad_add_fusion.refs_0_, bf16[8,128,512]{2,1,0:T(8,128)(2,1)S(1)} %factor_ready.1.refs_1_, f32[32,512,128]{2,1,0:T(8,128)} %all-gather.2.cloned.1.call-done.refs_2_), custom_call_target="tpu_custom_call" | custom-call | tf_op jit(solution)/shard_map/integral/pallas_call | solution.py:256
  76.9 0.0 all-to-all-done.1
  76.9 0.0 copy-done.3
  76.9 0.0 copy-done.8
  76.9 0.0 copy-done.10
  76.9 0.9 %divide_subtract_fusion = (f32[512,128]{1,0:T(8,128)}, f32[512,128]{1,0:T(8,128)}) fusion(f32[512,128]{1,0:T(8,128)S(1)} %copy-done.3, f32[128]{0:T(128)S(1)} %copy-done.10, f32[512]{0:T(512)S(1)} %copy-done.8, f32[512,128]{1,0:T(8,128)S(1)} %integral.1, f32[4,512,128]{2,1,0:T(8,128)S(1)} %all-to-all-done.1), kind=kLoop, calls=%fused_computation.5 | loop fusion | flops 458752 | bytes 2099712 | tf_op jit(solution)/shard_map/sub | solution.py:270
Async XLA Ops:
  7.2 67.1 %all-gather.2.cloned.1.call-start = ((), (), s32[]{:S(2)}) async-start(), calls=%async_computation.2 | async-start | bytes 8912896 | tf_op jit(solution)/shard_map/all_gather | solution.py:175
  7.9 17.6 %collective-permute-start.4 = (f32[512,128]{1,0:T(8,128)}, f32[512,128]{1,0:T(8,128)S(1)}, u32[]{:S(2)}, u32[]{:S(2)}) collective-permute-start(f32[512,128]{1,0:T(8,128)} %refs_0_.1), channel_id=1, source_target_pairs={{32,1},{33,2},{34,3},{35,4},{36,5},{37,6},{38,7},{39,0},{0,39},{1,... | collective-permute-start | bytes 786440 | tf_op jit(solution)/shard_map/ppermute | solution.py:163
  13.3 4.2 %copy-start.1 = (f32[512,128]{1,0:T(8,128)S(1)}, f32[512,128]{1,0:T(8,128)}, u32[]{:S(2)}) copy-start(f32[512,128]{1,0:T(8,128)} %refs_0_.1) | copy-start | bytes 786436
  13.3 32.7 %all-to-all-start = ((f32[4,1024,128]{2,1,0:T(8,128)}), f32[4,1024,128]{2,1,0:T(8,128)S(1)}, u32[]{:S(2)}, u32[]{:S(2)}) async-start(f32[4,1024,128]{2,1,0:T(8,128)} %bitcast.8), calls=%async_computation | async-start | bytes 4194304 | tf_op jit(solution)/shard_map/all_to_all | solution.py:182
  17.5 12.7 %collective-permute-start = (f32[512,128]{1,0:T(8,128)S(1)}, f32[512,128]{1,0:T(8,128)S(1)}, u32[]{:S(2)}, u32[]{:S(2)}) collective-permute-start(f32[512,128]{1,0:T(8,128)S(1)} %copy-done.1), channel_id=1, source_target_pairs={{0,1},{1,2},{2,3},{3,4},{4,5},{5,6},{6,7},{7,0},{32,39},{33,32},{3... | collective-permute-start | bytes 786440 | tf_op jit(solution)/shard_map/ppermute | solution.py:163
  25.5 9.3 %collective-permute-start.5 = (f32[512,128]{1,0:T(8,128)S(1)}, f32[512,128]{1,0:T(8,128)S(1)}, u32[]{:S(2)}, u32[]{:S(2)}) collective-permute-start(f32[512,128]{1,0:T(8,128)S(1)} %collective-permute-done.4.refs_0_), channel_id=1, source_target_pairs={{0,1},{1,2},{2,3},{3,4},{4,5},{5,6},{6,7},{7,0},{32,39},{33,32},{3... | collective-permute-start | bytes 786440 | tf_op jit(solution)/shard_map/ppermute | solution.py:163
  29.4 0.7 copy-start.6
  30.1 7.9 %collective-permute-start.1 = (f32[512,128]{1,0:T(8,128)S(1)}, f32[512,128]{1,0:T(8,128)}, u32[]{:S(2)}, u32[]{:S(2)}) collective-permute-start(f32[512,128]{1,0:T(8,128)S(1)} %collective-permute-done.refs_1_), channel_id=1, source_target_pairs={{0,1},{1,2},{2,3},{3,4},{4,5},{5,6},{6,7},{7,0},{32,39},{33,32},{3... | collective-permute-start | bytes 786440 | tf_op jit(solution)/shard_map/ppermute | solution.py:163
  34.1 0.7 copy-start.4
  34.8 9.9 %collective-permute-start.6 = (f32[512,128]{1,0:T(8,128)S(1)}, f32[512,128]{1,0:T(8,128)S(1)}, u32[]{:S(2)}, u32[]{:S(2)}) collective-permute-start(f32[512,128]{1,0:T(8,128)S(1)} %collective-permute-done.5.refs_1_), channel_id=1, source_target_pairs={{0,1},{1,2},{2,3},{3,4},{4,5},{5,6},{6,7},{7,0},{32,39},{33,32},{3... | collective-permute-start | bytes 786440 | tf_op jit(solution)/shard_map/ppermute | solution.py:163
  38.1 16.5 %collective-permute-start.2 = (f32[512,128]{1,0:T(8,128)}, f32[512,128]{1,0:T(8,128)S(1)}, u32[]{:S(2)}, u32[]{:S(2)}) collective-permute-start(f32[512,128]{1,0:T(8,128)} %collective-permute-done.1.refs_2_), channel_id=1, source_target_pairs={{0,2},{1,3},{2,4},{3,5},{4,6},{5,7},{6,0},{7,1},{32,38},{33,39},{3... | collective-permute-start | bytes 786440 | tf_op jit(solution)/shard_map/ppermute | solution.py:163
  42.1 12.4 %collective-permute-start.3 = (f32[512,128]{1,0:T(8,128)}, f32[512,128]{1,0:T(8,128)S(1)}, u32[]{:S(2)}, u32[]{:S(2)}) collective-permute-start(f32[512,128]{1,0:T(8,128)} %collective-permute-done.1.refs_2_), channel_id=1, source_target_pairs={{0,1},{1,2},{2,3},{3,4},{4,5},{5,6},{6,7},{7,0},{32,39},{33,32},{3... | collective-permute-start | bytes 786440 | tf_op jit(solution)/shard_map/ppermute | solution.py:163
  44.8 1.0 %copy-start.7 = (f32[512,128]{1,0:T(8,128)S(1)}, f32[512,128]{1,0:T(8,128)}, u32[]{:S(2)}) copy-start(f32[512,128]{1,0:T(8,128)} %copy-done.6) | copy-start | bytes 786436
  46.4 6.1 %copy-start.2 = (f32[512,128]{1,0:T(8,128)S(1)}, f32[512,128]{1,0:T(8,128)}, u32[]{:S(2)}) copy-start(f32[512,128]{1,0:T(8,128)} %refs_0_.1) | copy-start | bytes 786436
  46.4 6.1 %copy-start.5 = (f32[512,128]{1,0:T(8,128)S(1)}, f32[512,128]{1,0:T(8,128)}, u32[]{:S(2)}) copy-start(f32[512,128]{1,0:T(8,128)} %copy-done.4) | copy-start | bytes 786436
  48.2 6.6 %collective-permute-start.7 = (f32[4,512,128]{2,1,0:T(8,128)S(1)}, f32[4,512,128]{2,1,0:T(8,128)S(1)}, u32[]{:S(2)}, u32[]{:S(2)}) collective-permute-start(f32[4,512,128]{2,1,0:T(8,128)S(1)} %dressed_other.1), channel_id=1, source_target_pairs={{0,32},{32,0},{1,33},{33,1},{2,34},{34,2},{3,35},{35,3},{4,36},{36... | collective-permute-start | bytes 3145736 | tf_op jit(solution)/shard_map/ppermute | solution.py:166
  56.8 4.8 %copy-start.9 = (s32[8,2]{0,1:T(2,128)S(1)}, s32[8,2]{0,1:T(2,128)}, u32[]{:S(2)}) copy-start(s32[8,2]{0,1:T(2,128)} %param.15) | copy-start | bytes 196
  56.8 5.0 %copy-start = (f32[8,512,64]{1,2,0:T(8,128)S(1)}, f32[8,512,64]{1,2,0:T(8,128)}, u32[]{:S(2)}) copy-start(f32[8,512,64]{1,2,0:T(8,128)} %param.11) | copy-start | bytes 3145732
  56.8 5.1 %copy-start.11 = (s32[128]{0:T(128)S(1)}, s32[128]{0:T(128)}, u32[]{:S(2)}) copy-start(s32[128]{0:T(128)} %param.13) | copy-start | bytes 1540
  56.8 5.2 %copy-start.12 = (s32[32]{0:T(128)S(1)}, s32[32]{0:T(128)}, u32[]{:S(2)}) copy-start(s32[32]{0:T(128)} %param.14) | copy-start | bytes 388
  56.8 20.0 %all-to-all-start.1 = ((f32[4,512,128]{2,1,0:T(8,128)}), f32[4,512,128]{2,1,0:T(8,128)S(1)}, u32[]{:S(2)}, u32[]{:S(2)}) async-start(f32[4,512,128]{2,1,0:T(8,128)} %dressed_late.1), calls=%async_computation.1 | async-start | bytes 2097152 | tf_op jit(solution)/shard_map/all_to_all | solution.py:241
  62.2 14.6 %copy-start.3 = (f32[512,128]{1,0:T(8,128)S(1)}, f32[512,128]{1,0:T(8,128)}, u32[]{:S(2)}) copy-start(f32[512,128]{1,0:T(8,128)} %refs_0_.1) | copy-start | bytes 786436
  62.2 14.6 %copy-start.8 = (f32[512]{0:T(512)S(1)}, f32[512]{0:T(512)}, u32[]{:S(2)}) copy-start(f32[512]{0:T(512)} %param.16) | copy-start | bytes 6148
  62.2 14.7 %copy-start.10 = (f32[128]{0:T(128)S(1)}, f32[128]{0:T(128)}, u32[]{:S(2)}) copy-start(f32[128]{0:T(128)} %param.17) | copy-start | bytes 1540
Sparse Core Ops, SparseCore 0:
  10.1 64.1 all-gather.1
